TPU v7x, 32 devices: a whole 2x2x4 slice. The times are simulated.
32 devices in a mesh: blk: 8 (over z, x), head: 4 (over y, core).
Axes of the slice: x: 2, y: 2, z: 4, core: 2. Of those that a mesh axis runs over, the one named last changes fastest.
Arguments:
- hidden_in: bfloat16 [4096, 768], P(('blk', 'head')), may hold values from -6 to 6
- out_grad: bfloat16 [4096, 768], P(('blk', 'head')), may hold values from -6 to 6
- segment_ids: int32 [4096], replicated, may hold values from 0 to 4, as said below
- alibi_slopes: float32 [12], replicated, may hold values from 0.00012207031 to 0.015625
- qkv_weight: bfloat16 [2, 768, 2304], P(None, ('blk', 'head')), may hold values from -0.21875 to 0.21875
- out_weight: bfloat16 [2, 768, 768], P(None, ('blk', 'head')), may hold values from -0.875 to 0.875
- gate_up_weight: bfloat16 [2, 768, 6144], P(None, ('blk', 'head')), may hold values from -0.21875 to 0.21875
- down_weight: bfloat16 [2, 3072, 768], P(None, ('blk', 'head')), may hold values from -0.109375 to 0.109375
- gains: bfloat16 [2, 2, 768], P(None, None, ('blk', 'head')), may hold values from 0.25 to 1.75
- biases: bfloat16 [2, 6, 768], P(None, None, ('blk', 'head')), may hold values from -3 to 3
Outputs:
- output: bfloat16 [4096, 768], P(('blk', 'head'))
- input_grad: float32 [4096, 768], P(('blk', 'head'))
- qkv_weight_grad: float32 [2, 768, 2304], P(None, ('blk', 'head'))
- out_weight_grad: float32 [2, 768, 768], P(None, ('blk', 'head'))
- gate_up_weight_grad: float32 [2, 768, 6144], P(None, ('blk', 'head'))
- down_weight_grad: float32 [2, 3072, 768], P(None, ('blk', 'head'))
- gains_grad: float32 [2, 2, 768], P(None, None, ('blk', 'head'))
- biases_grad: float32 [2, 6, 768], P(None, None, ('blk', 'head'))
Inputs may be any that keep to these rules, and one draw needn't show every extreme that they name: `segment_ids`: segment numbers never fall along the tokens and all five documents occur. Document 1 starts within the first 512 tokens and document 2 starts within the last 512.
All inputs are finite; a program needn't handle non-finite values.
Results may differ from a plain program's by a relative error of at most 0.039.
Values may be sent and summed in bfloat16 or wider, within the bound.
A program may use at most 256 MiB of HBM per device.

v0:
```python
import jax
import jax.numpy as jnp
from jax import lax
from jax.sharding import PartitionSpec as P

H = 12


epsilon = 1e-06
masked_out = -1e30


def layer_norm(hidden_state, ln_gain, ln_shift):
    row_mean = jnp.mean(hidden_state, axis=-1, keepdims=True)
    centred = hidden_state - row_mean
    row_var = jnp.mean(centred * centred, axis=-1, keepdims=True)
    return centred * lax.rsqrt(row_var + epsilon) * ln_gain + ln_shift


def geglu(gate_part, up_part):
    return jax.nn.gelu(gate_part, approximate=False) * up_part


def weight_grad(left_rows, right_rows):
    return lax.dot_general(
        left_rows, right_rows, (((0,), (0,)), ((), ())), preferred_element_type=jnp.float32
    )


def input_grad_of(grad_rows, weight_now):
    return lax.dot_general(
        grad_rows, weight_now, (((1,), (1,)), ((), ())), preferred_element_type=jnp.float32
    )


def score_block(queries, key_rows, query_first, key_first, segment_ids, slopes, score_scale):
    query_count = queries.shape[0]
    key_count = key_rows.shape[0]
    raw_scores = (
        jnp.einsum("qhd,khd->hqk", queries, key_rows, preferred_element_type=jnp.float32)
        * score_scale
    )
    query_pos = query_first + lax.iota(jnp.int32, query_count)
    key_pos = key_first + lax.iota(jnp.int32, key_count)
    distance = jnp.abs(query_pos[:, None] - key_pos[None, :]).astype(jnp.float32)
    query_seg = lax.dynamic_slice_in_dim(segment_ids, query_first, query_count, 0)
    key_seg = lax.dynamic_slice_in_dim(segment_ids, key_first, key_count, 0)
    key_mask = (query_seg[:, None] == key_seg[None, :])[None]
    return (raw_scores - slopes[:, None, None] * distance[None], key_mask)


def over_blocks(running, arrays, block_len, step_fn):
    block_count = arrays[0].shape[0] // block_len
    shaped = tuple(
        (member.reshape((block_count, block_len) + member.shape[1:]) for member in arrays)
    )

    def one_step(state_now, packed):
        number, block_parts = packed
        return (step_fn(state_now, block_parts, number * block_len), None)

    result, unused = lax.scan(one_step, running, (jnp.arange(block_count, dtype=jnp.int32), shaped))
    return result


def shards(
    hidden_in,
    out_grad,
    segment_ids,
    alibi_slopes,
    qkv_weight,
    out_weight,
    gate_up_weight,
    down_weight,
    gains,
    biases,
):
    head_count = lax.axis_size("head")
    token_rows = hidden_in.shape[0]
    model_width = hidden_in.shape[1]
    block_rows = token_rows * head_count
    group_width = model_width // head_count
    local_heads = H // head_count
    head_dim = model_width // H
    score_scale = head_dim ** (-0.5)
    block_first = lax.axis_index("blk") * block_rows
    slopes = lax.dynamic_slice_in_dim(
        alibi_slopes, lax.axis_index("head") * local_heads, local_heads, 0
    )
    layers = qkv_weight.shape[0]

    def scores_at(queries, key_rows, query_first, key_first):
        return score_block(
            queries, key_rows, query_first, key_first, segment_ids, slopes, score_scale
        )

    def fetch(layer_number):
        return (
            lax.all_gather(qkv_weight[layer_number], ("blk", "head"), axis=0, tiled=True),
            lax.all_gather(out_weight[layer_number], ("blk", "head"), axis=0, tiled=True),
            lax.all_gather(gate_up_weight[layer_number], ("blk", "head"), axis=0, tiled=True),
            lax.all_gather(down_weight[layer_number], ("blk", "head"), axis=0, tiled=True),
            lax.all_gather(gains[layer_number], ("blk", "head"), axis=1, tiled=True),
            lax.all_gather(biases[layer_number], ("blk", "head"), axis=1, tiled=True),
        )

    hidden_state = hidden_in.astype(jnp.float32)
    kept_layers = []
    for layer_number in range(layers):
        weights_now = fetch(layer_number)
        (
            forward_qkv_w,
            forward_out_w,
            forward_gate_up_w,
            forward_down_w,
            forward_gain_rows,
            forward_bias_rows,
        ) = weights_now
        forward_gain_float = forward_gain_rows.astype(jnp.float32)
        forward_bias_float = forward_bias_rows.astype(jnp.float32)
        forward_inputs = hidden_state.astype(jnp.bfloat16)
        zero_bias = jnp.zeros((model_width,), jnp.float32)
        projected = jnp.dot(
            forward_inputs, forward_qkv_w, preferred_element_type=jnp.float32
        ) + jnp.concatenate([forward_bias_float[0], zero_bias, forward_bias_float[1]])
        grouped = lax.all_to_all(
            projected.astype(jnp.bfloat16).reshape(token_rows, 3, model_width),
            "head",
            split_axis=2,
            concat_axis=0,
            tiled=True,
        )
        forward_query_flat = grouped[:, 0]
        forward_key_flat = grouped[:, 1]
        forward_value_flat = grouped[:, 2]
        forward_query_heads = forward_query_flat.reshape(block_rows, local_heads, head_dim)
        start_state = (
            jnp.full((local_heads, block_rows), masked_out, jnp.float32),
            jnp.zeros((local_heads, block_rows), jnp.float32),
            jnp.zeros((block_rows, local_heads, head_dim), jnp.float32),
        )
        query_heads = forward_query_heads

        def forward_step_fn(state_now, block_parts, key_first):
            row_top, row_total, weighted = state_now
            key_rows = block_parts[0].reshape(-1, local_heads, head_dim)
            value_rows = block_parts[1].reshape(-1, local_heads, head_dim)
            scores, key_mask = scores_at(query_heads, key_rows, block_first, key_first)
            masked = jnp.where(key_mask, scores, masked_out)
            new_top = jnp.maximum(row_top, jnp.max(masked, axis=-1))
            exponent = jnp.where(key_mask, jnp.exp(masked - new_top[:, :, None]), 0.0)
            rescale = jnp.exp(row_top - new_top)
            row_total = row_total * rescale + jnp.sum(exponent, axis=-1)
            weighted = weighted * rescale.T[:, :, None] + jnp.einsum(
                "hqk,khd->qhd",
                exponent.astype(jnp.bfloat16),
                value_rows,
                preferred_element_type=jnp.float32,
            )
            return (new_top, row_total, weighted)

        forward_row_top, forward_row_total, forward_weighted = over_blocks(
            start_state,
            (
                lax.all_gather(forward_key_flat, "blk", axis=0, tiled=True),
                lax.all_gather(forward_value_flat, "blk", axis=0, tiled=True),
            ),
            block_rows,
            forward_step_fn,
        )
        forward_context_f = forward_weighted / forward_row_total.T[:, :, None]
        forward_log_sum = forward_row_top + jnp.log(forward_row_total)
        context_heads = forward_context_f.reshape(block_rows, group_width).astype(jnp.bfloat16)
        forward_context = lax.all_to_all(
            context_heads, "head", split_axis=0, concat_axis=1, tiled=True
        )
        branch = (
            jnp.dot(forward_context, forward_out_w, preferred_element_type=jnp.float32)
            + forward_bias_float[2]
        )
        forward_first_sum = hidden_state + branch
        normed = layer_norm(forward_first_sum, forward_gain_float[0], forward_bias_float[3])
        forward_normed_low = normed.astype(jnp.bfloat16)
        mixed_proj = jnp.dot(
            forward_normed_low, forward_gate_up_w, preferred_element_type=jnp.float32
        )
        ff_width = mixed_proj.shape[1] // 2
        forward_gate_part = mixed_proj[:, :ff_width]
        forward_up_part = mixed_proj[:, ff_width:]
        forward_hidden_units = geglu(forward_gate_part, forward_up_part).astype(jnp.bfloat16)
        feed_out = (
            jnp.dot(forward_hidden_units, forward_down_w, preferred_element_type=jnp.float32)
            + forward_bias_float[4]
        )
        forward_second_sum = normed + feed_out
        result = layer_norm(forward_second_sum, forward_gain_float[1], forward_bias_float[5])
        forward_saved = (
            forward_inputs,
            forward_query_flat,
            forward_key_flat,
            forward_value_flat,
            forward_context_f,
            forward_log_sum,
            forward_context,
            forward_first_sum,
            forward_normed_low,
            forward_gate_part,
            forward_up_part,
            forward_hidden_units,
            forward_second_sum,
        )
        hidden_state = result
        saved = forward_saved
        kept_layers.append((weights_now, saved))
    output = hidden_state.astype(jnp.bfloat16)
    grad_state = out_grad.astype(jnp.float32)
    collected = [None] * layers
    for layer_number in reversed(range(layers)):
        weights_now, saved = kept_layers[layer_number]
        weights_now = fetch(layer_number)
        qkv_w, out_w, gate_up_w, down_w, gain_rows, bias_rows = weights_now
        gain_float = gain_rows.astype(jnp.float32)
        bias_float = bias_rows.astype(jnp.float32)
        (
            inputs,
            query_flat,
            key_flat,
            value_flat,
            context_f,
            backward_log_sum,
            context,
            first_sum,
            normed_low,
            gate_part,
            up_part,
            hidden_units,
            second_sum,
        ) = saved
        unused, pull_second = jax.vjp(layer_norm, second_sum, gain_float[1], bias_float[5])
        grad_second, grad_gain_two, grad_shift_two = pull_second(grad_state)
        feed_grad = grad_second.astype(jnp.bfloat16)
        grad_down = weight_grad(hidden_units, feed_grad)
        grad_bias_down = jnp.sum(feed_grad.astype(jnp.float32), axis=0)
        grad_units = input_grad_of(feed_grad, down_w)
        unused, pull_glu = jax.vjp(geglu, gate_part, up_part)
        grad_gate, grad_up = pull_glu(grad_units)
        mixed_grad = jnp.concatenate([grad_gate, grad_up], axis=1).astype(jnp.bfloat16)
        grad_gate_up = weight_grad(normed_low, mixed_grad)
        grad_normed = grad_second + input_grad_of(mixed_grad, gate_up_w)
        unused, pull_first = jax.vjp(layer_norm, first_sum, gain_float[0], bias_float[3])
        grad_first, grad_gain_one, grad_shift_one = pull_first(grad_normed)
        branch_grad = grad_first.astype(jnp.bfloat16)
        grad_bias_out = jnp.sum(branch_grad.astype(jnp.float32), axis=0)
        grad_out = weight_grad(context, branch_grad)
        context_grad = input_grad_of(branch_grad, out_w).astype(jnp.bfloat16)
        grad_heads = lax.all_to_all(context_grad, "head", split_axis=1, concat_axis=0, tiled=True)
        backward_grad_rows = grad_heads.reshape(block_rows, local_heads, head_dim)
        delta_rows = jnp.sum(backward_grad_rows.astype(jnp.float32) * context_f, axis=-1)
        backward_delta_heads = delta_rows.T
        backward_query_heads = query_flat.reshape(block_rows, local_heads, head_dim)
        backward_key_heads = key_flat.reshape(block_rows, local_heads, head_dim)
        backward_value_heads = value_flat.reshape(block_rows, local_heads, head_dim)
        empty_grad = jnp.zeros((block_rows, local_heads, head_dim), jnp.float32)
        query_query_heads = backward_query_heads
        grad_rows = backward_grad_rows
        log_sum = backward_log_sum
        delta_heads = backward_delta_heads

        def query_step_fn(state_now, block_parts, key_first):
            key_rows = block_parts[0].reshape(-1, local_heads, head_dim)
            value_rows = block_parts[1].reshape(-1, local_heads, head_dim)
            scores, key_mask = scores_at(query_query_heads, key_rows, block_first, key_first)
            probability = jnp.exp(jnp.where(key_mask, scores - log_sum[:, :, None], masked_out))
            prob_grad = jnp.einsum(
                "qhd,khd->hqk", grad_rows, value_rows, preferred_element_type=jnp.float32
            )
            score_grad = (probability * (prob_grad - delta_heads[:, :, None])).astype(jnp.bfloat16)
            return state_now + score_scale * jnp.einsum(
                "hqk,khd->qhd", score_grad, key_rows, preferred_element_type=jnp.float32
            )

        query_grad = over_blocks(
            empty_grad,
            (
                lax.all_gather(key_flat, "blk", axis=0, tiled=True),
                lax.all_gather(value_flat, "blk", axis=0, tiled=True),
            ),
            block_rows,
            query_step_fn,
        )
        key_heads = backward_key_heads
        value_heads = backward_value_heads

        def step_fn(state_now, block_parts, query_first):
            key_grad_now, value_grad_now = state_now
            remote_queries = block_parts[0].astype(jnp.bfloat16).reshape(-1, local_heads, head_dim)
            remote_grads = block_parts[1].astype(jnp.bfloat16).reshape(-1, local_heads, head_dim)
            remote_lse = block_parts[2].T
            remote_delta = block_parts[3].T
            scores, key_mask = scores_at(remote_queries, key_heads, query_first, block_first)
            probability = jnp.exp(jnp.where(key_mask, scores - remote_lse[:, :, None], masked_out))
            prob_grad = jnp.einsum(
                "qhd,khd->hqk", remote_grads, value_heads, preferred_element_type=jnp.float32
            )
            score_grad = (probability * (prob_grad - remote_delta[:, :, None])).astype(jnp.bfloat16)
            value_grad_now = value_grad_now + jnp.einsum(
                "hqk,qhd->khd",
                probability.astype(jnp.bfloat16),
                remote_grads,
                preferred_element_type=jnp.float32,
            )
            key_grad_now = key_grad_now + score_scale * jnp.einsum(
                "hqk,qhd->khd", score_grad, remote_queries, preferred_element_type=jnp.float32
            )
            return (key_grad_now, value_grad_now)

        key_grad, value_grad = over_blocks(
            (empty_grad, empty_grad),
            (
                lax.all_gather(query_flat.astype(jnp.float32), "blk", axis=0, tiled=True),
                lax.all_gather(grad_heads.astype(jnp.float32), "blk", axis=0, tiled=True),
                lax.all_gather(backward_log_sum.T, "blk", axis=0, tiled=True),
                lax.all_gather(delta_rows, "blk", axis=0, tiled=True),
            ),
            block_rows,
            step_fn,
        )
        stacked = (
            jnp.stack([query_grad, key_grad, value_grad], axis=1)
            .reshape(block_rows, 3, group_width)
            .astype(jnp.bfloat16)
        )
        proj_grad = lax.all_to_all(
            stacked, "head", split_axis=0, concat_axis=2, tiled=True
        ).reshape(token_rows, 3 * model_width)
        grad_qkv = weight_grad(inputs, proj_grad)
        grad_bias_query = jnp.sum(proj_grad[:, :model_width].astype(jnp.float32), axis=0)
        grad_bias_value = jnp.sum(proj_grad[:, 2 * model_width :].astype(jnp.float32), axis=0)
        grad_input = grad_first + input_grad_of(proj_grad, qkv_w)
        small_grads = jnp.stack(
            [
                grad_gain_one,
                grad_gain_two,
                grad_bias_query,
                grad_bias_value,
                grad_bias_out,
                grad_shift_one,
                grad_bias_down,
                grad_shift_two,
            ],
            axis=1,
        )
        grad_state = grad_input
        layer_grads = (grad_qkv, grad_out, grad_gate_up, grad_down, small_grads)
        collected[layer_number] = (
            lax.psum_scatter(layer_grads[0], ("blk", "head"), scatter_dimension=0, tiled=True),
            lax.psum_scatter(layer_grads[1], ("blk", "head"), scatter_dimension=0, tiled=True),
            lax.psum_scatter(layer_grads[2], ("blk", "head"), scatter_dimension=0, tiled=True),
            lax.psum_scatter(layer_grads[3], ("blk", "head"), scatter_dimension=0, tiled=True),
            lax.psum_scatter(layer_grads[4], ("blk", "head"), scatter_dimension=0, tiled=True),
        )
    stacked_grads = [
        jnp.stack([collected[layer_number][member] for layer_number in range(layers)])
        for member in range(5)
    ]
    small_all = stacked_grads[4]
    gain_grads = jnp.transpose(small_all[:, :, 0:2], (0, 2, 1))
    bias_grads = jnp.transpose(small_all[:, :, 2:8], (0, 2, 1))
    return (
        output,
        grad_state,
        stacked_grads[0],
        stacked_grads[1],
        stacked_grads[2],
        stacked_grads[3],
        gain_grads,
        bias_grads,
    )


def solution(mesh):
    return jax.shard_map(
        shards,
        mesh=mesh,
        in_specs=(
            P(("blk", "head"), None),
            P(("blk", "head"), None),
            P(),
            P(),
            P(None, ("blk", "head"), None),
            P(None, ("blk", "head"), None),
            P(None, ("blk", "head"), None),
            P(None, ("blk", "head"), None),
            P(None, None, ("blk", "head")),
            P(None, None, ("blk", "head")),
        ),
        out_specs=(
            P(("blk", "head"), None),
            P(("blk", "head"), None),
            P(None, ("blk", "head"), None),
            P(None, ("blk", "head"), None),
            P(None, ("blk", "head"), None),
            P(None, ("blk", "head"), None),
            P(None, None, ("blk", "head")),
            P(None, None, ("blk", "head")),
        ),
        check_vma=False,
    )
```

profile of v0, /device:TPU:21, one launch (start us, length us, event | category | flops | bytes accessed | tf_op | source)
XLA Modules:
  0.0 2466.1 jit_solution(11680002086594312081)
XLA Ops:
  9.8 31.2 %all-gather.9 = bf16[1,6,768]{1,0,2:T(2,128)(2,1)S(1)} all-gather(bf16[1,6,24]{1,0,2:T(2,128)(2,1)S(1)} %copy.222), channel_id=11, replica_groups=mesh['blk'=8,'head'=4] {'blk','head'}, dimensions={2}, use_global_device_ids=true | all-gather | bytes 9504 | tf_op jit(solution)/shard_map/all_gather | solution.py:104
  41.6 38.9 %all-gather.1 = bf16[1,6,768]{1,0,2:T(2,128)(2,1)S(1)} all-gather(bf16[1,6,24]{1,0,2:T(2,128)(2,1)S(1)} %copy.220), channel_id=3, replica_groups=mesh['blk'=8,'head'=4] {'blk','head'}, dimensions={2}, use_global_device_ids=true | all-gather | bytes 9504 | tf_op jit(solution)/shard_map/all_gather | solution.py:104
  128.0 41.1 %all-gather.5 = bf16[1,2,768]{1,0,2:T(2,128)(2,1)S(1)} all-gather(bf16[1,2,24]{1,0,2:T(2,128)(2,1)S(1)} %copy.221), channel_id=7, replica_groups=mesh['blk'=8,'head'=4] {'blk','head'}, dimensions={2}, use_global_device_ids=true | all-gather | bytes 3168 | tf_op jit(solution)/shard_map/all_gather | solution.py:103
  181.4 42.3 %all-gather.43.cloned.1.call-done = bf16[4096,1,192]{0,2,1:T(8,128)(2,1)} async-done(((bf16[512,1,192]{0,2,1:T(8,128)(2,1)}), bf16[4096,1,192]{0,2,1:T(8,128)(2,1)}) %all-gather.43.cloned.1.call-update) | async-done | bytes 1572880 | tf_op jit(solution)/shard_map/all_gather | solution.py:166
  227.4 68.5 %while.90 = (s32[]{:T(128)}, f32[3,512]{1,0:T(4,128)S(1)}, f32[3,512]{1,0:T(4,128)S(1)}, f32[512,3,64]{0,2,1:T(8,128)}, s32[512]{0:T(512)S(1)}, /*index=5*/s32[8...) while((s32[]{:T(128)}, f32[3,512]{1,0:T(4,128)S(1)}, ...), condition=%wide.region_3.4_spmd.clone, body=%wide.region_0.3_spmd.clone.sunk | while | flops 211331072 | bytes 15646995 | solution.py:62
  309.5 54.8 %all-gather.47.cloned.1.call-done = bf16[1,768,6144]{2,1,0:T(8,128)(2,1)} async-done(((bf16[1,24,6144]{2,1,0:T(8,128)(2,1)}), bf16[1,768,6144]{2,1,0:T(8,128)(2,1)}) %all-gather.47.cloned.1.call-update) | async-done | bytes 9437200 | tf_op jit(solution)/shard_map/all_gather | solution.py:101
  375.4 54.7 %all-gather.49.cloned.1.call-done = bf16[1,3072,768]{2,1,0:T(8,128)(2,1)} async-done(((bf16[1,96,768]{2,1,0:T(8,128)(2,1)}), bf16[1,3072,768]{2,1,0:T(8,128)(2,1)}) %all-gather.49.cloned.1.call-update) | async-done | bytes 4718608 | tf_op jit(solution)/shard_map/all_gather | solution.py:102
  433.6 57.4 %all-gather.51.cloned.1.call-done = bf16[1,768,2304]{2,1,0:T(8,128)(2,1)} async-done(((bf16[1,24,2304]{2,1,0:T(8,128)(2,1)}), bf16[1,768,2304]{2,1,0:T(8,128)(2,1)}) %all-gather.51.cloned.1.call-update) | async-done | bytes 3538960 | tf_op jit(solution)/shard_map/all_gather | solution.py:99
  511.9 33.9 %all-gather.13 = bf16[1,2,768]{1,0,2:T(2,128)(2,1)S(1)} all-gather(bf16[1,2,24]{1,0,2:T(2,128)(2,1)S(1)} %copy.223), channel_id=15, replica_groups=mesh['blk'=8,'head'=4] {'blk','head'}, dimensions={2}, use_global_device_ids=true | all-gather | bytes 3168 | tf_op jit(solution)/shard_map/all_gather | solution.py:103
  558.1 42.1 %all-gather.55.cloned.1.call-done = bf16[4096,1,192]{0,2,1:T(8,128)(2,1)} async-done(((bf16[512,1,192]{0,2,1:T(8,128)(2,1)}), bf16[4096,1,192]{0,2,1:T(8,128)(2,1)}) %all-gather.55.cloned.1.call-update) | async-done | bytes 1572880 | tf_op jit(solution)/shard_map/all_gather | solution.py:166
  604.0 68.6 %while.91 = (s32[]{:T(128)}, f32[3,512]{1,0:T(4,128)S(1)}, f32[3,512]{1,0:T(4,128)S(1)}, f32[512,3,64]{0,2,1:T(8,128)}, s32[512]{0:T(512)S(1)}, /*index=5*/s32[8...) while((s32[]{:T(128)}, f32[3,512]{1,0:T(4,128)S(1)}, ...), condition=%wide.region_11.12_spmd.clone, body=%wide.region_8.11_spmd.clone.sunk | while | flops 211331072 | bytes 15646995 | solution.py:62
  703.4 82.6 %all-gather.59.cloned.1.call-done = bf16[1,768,6144]{2,1,0:T(8,128)(2,1)} async-done(((bf16[1,24,6144]{2,1,0:T(8,128)(2,1)}), bf16[1,768,6144]{2,1,0:T(8,128)(2,1)}) %all-gather.59.cloned.1.call-update) | async-done | bytes 9437200 | tf_op jit(solution)/shard_map/all_gather | solution.py:101
  797.5 54.4 %all-gather.61.cloned.1.call-done = bf16[1,3072,768]{2,1,0:T(8,128)(2,1)} async-done(((bf16[1,96,768]{2,1,0:T(8,128)(2,1)}), bf16[1,3072,768]{2,1,0:T(8,128)(2,1)}) %all-gather.61.cloned.1.call-update) | async-done | bytes 4718608 | tf_op jit(solution)/shard_map/all_gather | solution.py:102
  898.2 90.0 %while.92 = (s32[]{:T(128)}, f32[512,3,64]{0,2,1:T(8,128)}, bf16[8,512,192]{1,2,0:T(8,128)(2,1)}, s32[512]{0:T(512)S(1)}, s32[8]{0:T(128)}, /*index=5*/s32[4096]...) while((s32[]{:T(128)}, f32[512,3,64]{0,2,1:T(8,128)}, ...), condition=%wide.region_22.23_spmd.clone, body=%wide.region_21.22_spmd.clone.sunk | while | flops 309625856 | bytes 11497725 | solution.py:62
  1020.6 153.9 %while.93 = (s32[]{:T(128)}, f32[512,3,64]{0,2,1:T(8,128)}, f32[512,3,64]{0,2,1:T(8,128)}, bf16[8,512,192]{1,0,2:T(8,128)(2,1)}, s32[8]{0:T(128)}, /*index=5*/s3...) while((s32[]{:T(128)}, f32[512,3,64]{0,2,1:T(8,128)}, ...), condition=%wide.region_24.25_spmd.clone, body=%wide.region_23.24_spmd.clone.sunk | while | flops 415204352 | bytes 17754388 | solution.py:62
  1318.2 89.8 %while.94 = (s32[]{:T(128)}, f32[512,3,64]{0,2,1:T(8,128)}, bf16[8,512,192]{1,2,0:T(8,128)(2,1)}, s32[512]{0:T(512)S(1)}, s32[8]{0:T(128)}, /*index=5*/s32[4096]...) while((s32[]{:T(128)}, f32[512,3,64]{0,2,1:T(8,128)}, ...), condition=%wide.region_31.32_spmd.clone, body=%wide.region_30.31_spmd.clone.sunk | while | flops 309625856 | bytes 11546933 | solution.py:62
  1413.6 141.7 %while.95 = (s32[]{:T(128)}, f32[512,3,64]{0,2,1:T(8,128)}, f32[512,3,64]{0,2,1:T(8,128)}, bf16[8,512,192]{1,0,2:T(8,128)(2,1)}, s32[8]{0:T(128)}, /*index=5*/s3...) while((s32[]{:T(128)}, f32[512,3,64]{0,2,1:T(8,128)}, ...), condition=%wide.region_33.34_spmd.clone, body=%wide.region_32.33_spmd.clone.sunk | while | flops 415204352 | bytes 17754388 | solution.py:62
  1559.2 31.2 %all_to_all.133 = bf16[512,3,192]{2,1,0:T(4,128)(2,1)S(1)} all-to-all(bf16[512,3,192]{2,1,0:T(4,128)(2,1)S(1)} %copy.192), channel_id=1, replica_groups=mesh['blk'=8,'head'=4] {'head'}, dimensions={0} | all-to-all | bytes 1179648 | tf_op jit(solution)/shard_map/all_to_all | solution.py:333
  1642.5 47.6 %all-reduce.2 = (f32[768,8]{0,1:T(8,128)}, f32[768,8]{0,1:T(8,128)}) all-reduce(f32[768,8]{0,1:T(8,128)} %stack.161, f32[768,8]{0,1:T(8,128)} %stack.151), channel_id=29, replica_groups=mesh['blk'=8,'head'=4] {'blk','head'}, use_global_device_ids=true, to_apply=%region_59.60.clone | all-reduce | flops 12288 | bytes 98304
  1696.9 69.0 %reduce-scatter.25.cloned.1.call-done = f32[96,768]{1,0:T(8,128)} async-done(((f32[3072,768]{1,0:T(8,128)}), f32[96,768]{1,0:T(8,128)}) %reduce-scatter.25.cloned.1.call-update) | async-done | bytes 294928 | tf_op jit(solution)/shard_map/reduce_scatter | solution.py:359
  1765.9 140.5 %reduce-scatter.23.cloned.1.call-done = f32[96,768]{1,0:T(8,128)} async-done(((f32[3072,768]{1,0:T(8,128)}), f32[96,768]{1,0:T(8,128)}) %reduce-scatter.23.cloned.1.call-update) | async-done | bytes 294928 | tf_op jit(solution)/shard_map/reduce_scatter | solution.py:359
  1908.4 123.0 %reduce-scatter.27.cloned.1.call-done = f32[24,2304]{1,0:T(8,128)} async-done(((f32[768,2304]{1,0:T(8,128)}), f32[24,2304]{1,0:T(8,128)}) %reduce-scatter.27.cloned.1.call-update) | async-done | bytes 221200
  2033.8 210.7 %reduce-scatter.21.cloned.1.call-done = f32[24,6144]{1,0:T(8,128)} async-done(((f32[768,6144]{1,0:T(8,128)}), f32[24,6144]{1,0:T(8,128)}) %reduce-scatter.21.cloned.1.call-update) | async-done | bytes 589840 | tf_op jit(solution)/shard_map/reduce_scatter | solution.py:358
  2244.5 212.0 %reduce-scatter.19.cloned.1.call-done = f32[24,6144]{1,0:T(8,128)} async-done(((f32[768,6144]{1,0:T(8,128)}), f32[24,6144]{1,0:T(8,128)}) %reduce-scatter.19.cloned.1.call-update) | async-done | bytes 589840 | tf_op jit(solution)/shard_map/reduce_scatter | solution.py:358
  (1048 shorter events, 1037.0 us)
Async XLA Ops:
  7.2 99.4 %all-gather.39.cloned.1.call-start = ((), (), s32[]{:S(2)}) async-start(), calls=%async_computation.24 | async-start | bytes 3649536 | tf_op jit(solution)/shard_map/all_gather | solution.py:99
  8.9 168.8 %all-gather.41.cloned.1.call-start = ((), (), s32[]{:S(2)}) async-start(), calls=%async_computation.25 | async-start | bytes 1769472 | tf_op jit(solution)/shard_map/all_gather | solution.py:165
  123.8 99.8 %all-gather.43.cloned.1.call-start = ((), (), s32[]{:S(2)}) async-start(), calls=%async_computation.26 | async-start | bytes 1769472 | tf_op jit(solution)/shard_map/all_gather | solution.py:166
  124.6 182.9 %all-gather.45.cloned.1.call-start = ((), (), s32[]{:S(2)}) async-start(), calls=%async_computation.27 | async-start | bytes 1216512 | tf_op jit(solution)/shard_map/all_gather | solution.py:100
  125.3 239.1 %all-gather.47.cloned.1.call-start = ((), (), s32[]{:S(2)}) async-start(), calls=%async_computation.28 | async-start | bytes 9732096 | tf_op jit(solution)/shard_map/all_gather | solution.py:101
  126.2 303.9 %all-gather.49.cloned.1.call-start = ((), (), s32[]{:S(2)}) async-start(), calls=%async_computation.29 | async-start | bytes 4866048 | tf_op jit(solution)/shard_map/all_gather | solution.py:102
  127.0 364.0 %all-gather.51.cloned.1.call-start = ((), (), s32[]{:S(2)}) async-start(), calls=%async_computation.30 | async-start | bytes 3649536 | tf_op jit(solution)/shard_map/all_gather | solution.py:99
  302.4 252.0 %all-gather.53.cloned.1.call-start = ((), (), s32[]{:S(2)}) async-start(), calls=%async_computation.31 | async-start | bytes 1769472 | tf_op jit(solution)/shard_map/all_gather | solution.py:165
  508.4 91.9 %all-gather.55.cloned.1.call-start = ((), (), s32[]{:S(2)}) async-start(), calls=%async_computation.32 | async-start | bytes 1769472 | tf_op jit(solution)/shard_map/all_gather | solution.py:166
  509.1 174.8 %all-gather.63.cloned.1.call-start = ((), (), s32[]{:S(2)}) async-start(), calls=%async_computation.36 | async-start | bytes 1769472 | tf_op jit(solution)/shard_map/all_gather | solution.py:320
  509.7 191.6 %all-gather.57.cloned.1.call-start = ((), (), s32[]{:S(2)}) async-start(), calls=%async_computation.33 | async-start | bytes 1216512 | tf_op jit(solution)/shard_map/all_gather | solution.py:100
  510.4 275.6 %all-gather.59.cloned.1.call-start = ((), (), s32[]{:S(2)}) async-start(), calls=%async_computation.34 | async-start | bytes 9732096 | tf_op jit(solution)/shard_map/all_gather | solution.py:101
  511.0 340.9 %all-gather.61.cloned.1.call-start = ((), (), s32[]{:S(2)}) async-start(), calls=%async_computation.35 | async-start | bytes 4866048 | tf_op jit(solution)/shard_map/all_gather | solution.py:102
  873.0 143.8 %all-gather.35.cloned.1.call-start = ((), (), s32[]{:S(2)}) async-start(), calls=%async_computation.16 | async-start | bytes 1769472 | tf_op jit(solution)/shard_map/all_gather | solution.py:321
  1194.9 59.2 %all-gather.65.cloned.1.call-start = ((), (), s32[]{:S(2)}) async-start(), calls=%async_computation.37 | async-start | bytes 1769472 | tf_op jit(solution)/shard_map/all_gather | solution.py:320
  1195.5 214.3 %all-gather.37.cloned.1.call-start = ((), (), s32[]{:S(2)}) async-start(), calls=%async_computation.17 | async-start | bytes 1769472 | tf_op jit(solution)/shard_map/all_gather | solution.py:321
  1238.1 398.9 %reduce-scatter.17.cloned.1.call-start = ((), (), s32[]{:S(2)}) async-start(), calls=%async_computation.19 | async-start | bytes 2433024 | tf_op jit(solution)/shard_map/reduce_scatter | solution.py:357
  1240.1 397.0 %reduce-scatter.15.cloned.1.call-start = ((), (), s32[]{:S(2)}) async-start(), calls=%async_computation.18 | async-start | bytes 2433024 | tf_op jit(solution)/shard_map/reduce_scatter | solution.py:357
  1243.0 452.3 %reduce-scatter.29.cloned.1.call-start = ((), (), s32[]{:S(2)}) async-start(), calls=%async_computation.39 | async-start | bytes 7299072
  1247.8 518.1 %reduce-scatter.25.cloned.1.call-start = ((), (), s32[]{:S(2)}) async-start(), calls=%async_computation.23 | async-start | bytes 9732096 | tf_op jit(solution)/shard_map/reduce_scatter | solution.py:359
  1254.0 652.4 %reduce-scatter.23.cloned.1.call-start = ((), (), s32[]{:S(2)}) async-start(), calls=%async_computation.22 | async-start | bytes 9732096 | tf_op jit(solution)/shard_map/reduce_scatter | solution.py:359
  1289.9 741.4 %reduce-scatter.27.cloned.1.call-start = ((), (), s32[]{:S(2)}) async-start(), calls=%async_computation.38 | async-start | bytes 7299072
  1603.2 641.3 %reduce-scatter.21.cloned.1.call-start = ((), (), s32[]{:S(2)}) async-start(), calls=%async_computation.21 | async-start | bytes 19464192 | tf_op jit(solution)/shard_map/reduce_scatter | solution.py:358
  1612.8 843.6 %reduce-scatter.19.cloned.1.call-start = ((), (), s32[]{:S(2)}) async-start(), calls=%async_computation.20 | async-start | bytes 19464192 | tf_op jit(solution)/shard_map/reduce_scatter | solution.py:358
  (144 other events, 5160.1 us)
Sparse Core Ops, SparseCore 0:
  11.5 60.7 all-gather.38
  123.9 53.6 all-gather.40
  179.7 43.8 all-gather.42
  226.4 52.5 all-gather.44
  282.4 81.9 all-gather.46
  367.7 62.3 all-gather.48
  433.0 57.9 all-gather.50
  508.5 45.8 all-gather.52
  556.4 43.7 all-gather.54
  602.1 43.6 all-gather.62
  648.8 52.4 all-gather.56
  704.1 81.9 all-gather.58
  789.5 62.3 all-gather.60
  897.8 54.3 all-gather.34
  1197.5 47.7 all-gather.64
  1247.2 43.9 all-gather.36
  1296.3 96.0 reduce-scatter.16
  1398.4 98.0 reduce-scatter.14
  1502.2 122.3 reduce-scatter.28
  1631.3 134.5 reduce-scatter.24
  1771.8 134.5 reduce-scatter.22
  1913.1 118.1 reduce-scatter.26
  2037.7 206.6 reduce-scatter.20
  2250.7 205.6 reduce-scatter.18
where the time goes:
time: 2490 us; the launch traced here: 2470 us
  waiting for transfers between devices  1190 us (48%)
  blocking collectives  358 us (14%)
  matrix products  356 us (14%)
  local copies, waits for them, and re-layouts  342 us (14%)
  other arithmetic  128 us (5%)
  loops' own time  45.2 us (2%)
  starting transfers between devices  30.6 us (1%)
    reduce_scatter x2, waiting for transfers between devices, shards(): lax.psum_scatter(layer_grads[2], ('blk', 'head'), scatter_dimension=0, ti...  423 us
    reduce_scatter x2, waiting for transfers between devices, shards(): lax.psum_scatter(layer_grads[3], ('blk', 'head'), scatter_dimension=0, ti...  210 us
    dynamic_slice x128, local copies, waits for them, and re-layouts, over_blocks(): lax.scan(one_step, running, (jnp.arange(block_count, dtype=jnp.int32), sh...  159 us
    all_gather x2, waiting for transfers between devices, fetch(): lax.all_gather(gate_up_weight[layer_number], ('blk', 'head'), axis=0, til...  137 us
    unnamed x26, waiting for transfers between devices  128 us
    all_gather x2, waiting for transfers between devices, fetch(): lax.all_gather(down_weight[layer_number], ('blk', 'head'), axis=0, tiled=...  109 us
    all_gather x2, waiting for transfers between devices, shards(): lax.all_gather(forward_value_flat, 'blk', axis=0, tiled=True)  84.4 us
    all_gather x2, blocking collectives, fetch(): lax.all_gather(gains[layer_number], ('blk', 'head'), axis=1, tiled=True)  75 us
  transfers between devices with their start and end apart: 28, of which 16 were waited for; matrix products, arithmetic and copies ran while one was open for 26% of the time, Pallas kernels for 0%

commit v1 on v0

v1 whole, which is shorter than its diff:
```python
import functools
import jax
import jax.numpy as jnp
from jax import lax
from jax.experimental import pallas as pl
from jax.experimental.pallas import tpu as pltpu
from jax.sharding import PartitionSpec as P

MESH = pl.DeviceIdType.MESH
BF = jnp.bfloat16
F32 = jnp.float32
NT = (((1,), (1,)), ((), ()))
NN = (((1,), (0,)), ((), ()))
TN = (((0,), (0,)), ((), ()))


def dot(a, b, dims):
    return lax.dot_general(a, b, dims, preferred_element_type=F32)


def in_half(half, rows):
    lane = lax.broadcasted_iota(jnp.int32, (rows, 128), 1)
    return (lane >= 64) if half else (lane < 64)


def ones_half(half, rows, count):
    lane = lax.broadcasted_iota(jnp.int32, (rows, 128), 1)
    first = 0 if half else 64
    return jnp.where((lane >= first) & (lane < first + count), 1.0, 0.0).astype(BF)


def k_operand(kv_ref, kaug_ref, b, h):
    col = 128 * (h // 2)
    return jnp.where(in_half(h % 2, kv_ref.shape[1]), kv_ref[b, :, col : col + 128], kaug_ref[h, b])


def v_operand(kv_ref, b, h):
    col, half = 128 * ((3 + h) // 2), (3 + h) % 2
    rows = kv_ref.shape[1]
    return jnp.where(in_half(half, rows), kv_ref[b, :, col : col + 128], ones_half(half, rows, 3))


def fwd_block(side, diag, b, q_ref, kv_ref, kaug_ref, m_ref, acc_ref):
    for h in range(3):
        k = k_operand(kv_ref, kaug_ref, b, h)
        if diag:
            s = jnp.minimum(dot(q_ref[0, h], k, NT), dot(q_ref[1, h], k, NT))
        else:
            s = dot(q_ref[side, h], k, NT)
        m_old = m_ref[h]
        m_new = jnp.maximum(m_old, jnp.max(s, axis=1, keepdims=True))
        p = jnp.exp(s - m_new[:, :1]).astype(BF)
        acc_ref[h] = acc_ref[h] * jnp.exp(m_old - m_new) + dot(p, v_operand(kv_ref, b, h), NN)
        m_ref[h] = m_new


def fwd_finish(m_ref, acc_ref, ctx_ref, ctxf_ref, lse_ref):
    for h in range(3):
        half = (3 + h) % 2
        first = 0 if half else 64
        acc = acc_ref[h]
        total = acc[:, first : first + 1]
        ctx = acc[:, 64 * half : 64 * half + 64] / total
        ctxf_ref[:, 64 * h : 64 * h + 64] = ctx
        ctx_ref[:, 64 * h : 64 * h + 64] = ctx.astype(BF)
        lse_ref[h] = m_ref[h] + jnp.log(total)


def attn_fwd_kernel(nz, comm, q_ref, own_ref, kaug_ref, ctx_ref, ctxf_ref, lse_ref, kv_ref,
                    m_ref, acc_ref, zsend, xsend, recv):
    blk, head = lax.axis_index("blk"), lax.axis_index("head")
    z, x = blk // 2, blk % 2
    other = 1 - x

    def device(zz, xx):
        return (zz * 2 + xx, head)

    if comm:
        barrier = pltpu.get_barrier_semaphore()
        pl.semaphore_signal(barrier, inc=1, device_id=device(z, other), device_id_type=MESH)

        @pl.when(z > 0)
        def _():
            pl.semaphore_signal(barrier, inc=1, device_id=device(z - 1, x), device_id_type=MESH)

        @pl.when(z < nz - 1)
        def _():
            pl.semaphore_signal(barrier, inc=1, device_id=device(z + 1, x), device_id_type=MESH)

        kv_ref[blk] = own_ref[...]
        ends = (z == 0).astype(jnp.int32) + (z == nz - 1).astype(jnp.int32)
        pl.semaphore_wait(barrier, 3 - ends)

    def to_right(b):
        return pltpu.make_async_remote_copy(
            src_ref=kv_ref.at[b], dst_ref=kv_ref.at[b], send_sem=zsend.at[b], recv_sem=recv.at[b],
            device_id=device(z + 1, x), device_id_type=MESH)

    def to_left(b):
        return pltpu.make_async_remote_copy(
            src_ref=kv_ref.at[b], dst_ref=kv_ref.at[b], send_sem=zsend.at[nz * 2 + b], recv_sem=recv.at[b],
            device_id=device(z - 1, x), device_id_type=MESH)

    def to_other(b):
        return pltpu.make_async_remote_copy(
            src_ref=kv_ref.at[b], dst_ref=kv_ref.at[b], send_sem=xsend.at[b], recv_sem=recv.at[b],
            device_id=device(z, other), device_id_type=MESH)

    def arrived(b):
        if comm:
            to_other(b).wait_recv()

    if comm:
        @pl.when(z < nz - 1)
        def _():
            to_right(blk).start()

        @pl.when(z > 0)
        def _():
            to_left(blk).start()

        to_other(blk).start()

    def compute(b, diag=False):
        side = (b > blk).astype(jnp.int32)
        fwd_block(side, diag, b, q_ref, kv_ref, kaug_ref, m_ref, acc_ref)

    m_ref[...] = jnp.full(m_ref.shape, -1e30, F32)
    acc_ref[...] = jnp.zeros(acc_ref.shape, F32)
    compute(blk, True)

    def step(d, carry):
        zl, zr = z - d, z + d

        @pl.when(zl >= 0)
        def _():
            b = zl * 2 + x
            if comm:
                arrived(b)
                to_other(b).start()

                @pl.when(z < nz - 1)
                def _():
                    to_right(b).start()

        @pl.when(zr < nz)
        def _():
            b = zr * 2 + x
            if comm:
                arrived(b)
                to_other(b).start()

                @pl.when(z > 0)
                def _():
                    to_left(b).start()

        def visit(i, c):
            zz = jnp.where(i % 2 == 0, z - d + i // 2, z + d - i // 2)
            xx = jnp.where(i < 2, x, other)
            seen = (zz >= 0) & (zz < nz) & ((i != 3) | (d > 1))

            @pl.when(seen)
            def _():
                b = zz * 2 + xx

                @pl.when(i >= 2)
                def _():
                    arrived(b)
                compute(b)
            return c
        lax.fori_loop(0, 4, visit, 0)
        return carry

    lax.fori_loop(1, nz, step, 0)

    def last(i, c):
        zz = jnp.where(i == 0, z - (nz - 1), z + (nz - 1))

        @pl.when((zz >= 0) & (zz < nz))
        def _():
            b = zz * 2 + other
            arrived(b)
            compute(b)
        return c
    lax.fori_loop(0, 2, last, 0)
    fwd_finish(m_ref, acc_ref, ctx_ref, ctxf_ref, lse_ref)

    if comm:
        def drain(zz, c):
            b = zz * 2 + x
            to_other(b).wait_send()

            @pl.when((zz <= z) & (z < nz - 1))
            def _():
                to_right(b).wait_send()

            @pl.when((zz >= z) & (z > 0))
            def _():
                to_left(b).wait_send()
            return c
        lax.fori_loop(0, nz, drain, 0)


def attn_fwd(qa, own, kaug, comm=True, cid=0):
    n, rows = kaug.shape[1], kaug.shape[2]
    V = pl.BlockSpec(memory_space=pltpu.VMEM)
    return pl.pallas_call(
        functools.partial(attn_fwd_kernel, n // 2, comm),
        out_shape=(
            jax.ShapeDtypeStruct((rows, 192), BF),
            jax.ShapeDtypeStruct((rows, 192), F32),
            jax.ShapeDtypeStruct((3, rows, 128), F32),
            jax.ShapeDtypeStruct((n, rows, 384), BF),
        ),
        in_specs=[V] * 3,
        out_specs=(V,) * 4,
        scratch_shapes=[
            pltpu.VMEM((3, rows, 128), F32),
            pltpu.VMEM((3, rows, 128), F32),
            pltpu.SemaphoreType.DMA((2 * n,)),
            pltpu.SemaphoreType.DMA((n,)),
            pltpu.SemaphoreType.DMA((n,)),
        ],
        compiler_params=pltpu.CompilerParams(
            collective_id=cid if comm else None, has_side_effects=comm, vmem_limit_bytes=56 * 2**20),
        cost_estimate=pl.CostEstimate(flops=20 * 10**9, bytes_accessed=10**8, transcendentals=10**7),
        name="attn_fwd",
    )(qa, own, kaug)


def attn_bwd_kernel(nz, comm, q_ref, do_ref, kv_ref, kaug_ref, dq_ref, dkv_ref,
                    dqacc, part, stage, xin, zin, xsend, xrecv, zsend, zrecv):
    blk, head = lax.axis_index("blk"), lax.axis_index("head")
    z, x = blk // 2, blk % 2
    other = 1 - x
    rows = dq_ref.shape[0]

    def device(zz, xx):
        return (zz * 2 + xx, head)

    if comm:
        barrier = pltpu.get_barrier_semaphore()
        pl.semaphore_signal(barrier, inc=1, device_id=device(z, other), device_id_type=MESH)

        def greet(d, c):
            pl.semaphore_signal(barrier, inc=1, device_id=device((z + d) % nz, x), device_id_type=MESH)
            return c
        lax.fori_loop(1, nz, greet, 0)
        pl.semaphore_wait(barrier, nz)

    dqacc[...] = jnp.zeros(dqacc.shape, F32)

    def compute(b, diag):
        side = (b > blk).astype(jnp.int32)
        dks, dvs = [], []
        for h in range(3):
            k = k_operand(kv_ref, kaug_ref, b, h)
            v = v_operand(kv_ref, b, h)
            if diag:
                s = jnp.minimum(dot(k, q_ref[0, h], NT), dot(k, q_ref[1, h], NT))
            else:
                s = dot(k, q_ref[side, h], NT)
            p = jnp.exp(s)
            ds = (p * dot(v, do_ref[h], NT)).astype(BF)
            dvs.append(dot(p.astype(BF), do_ref[h], NN))
            dks.append(dot(ds, q_ref[side, h], NN))
            dqacc[h] += dot(ds, k, TN)
        low = in_half(0, rows)
        part[:, 0:128] = jnp.where(low, dks[0], dks[1])
        part[:, 128:256] = jnp.where(low, dks[2], dvs[0])
        part[:, 256:384] = jnp.where(low, dvs[1], dvs[2])

    def to_other(zz):
        return pltpu.make_async_remote_copy(
            src_ref=stage.at[zz, 0], dst_ref=xin.at[zz], send_sem=xsend.at[zz], recv_sem=xrecv.at[zz],
            device_id=device(z, other), device_id_type=MESH)

    def to_owner(zz):
        return pltpu.make_async_remote_copy(
            src_ref=stage.at[zz, 1], dst_ref=zin.at[z], send_sem=zsend.at[zz], recv_sem=zrecv.at[z],
            device_id=device(zz, x), device_id_type=MESH)

    def from_sender(zz):
        return pltpu.make_async_remote_copy(
            src_ref=stage.at[zz, 1], dst_ref=zin.at[zz], send_sem=zsend.at[zz], recv_sem=zrecv.at[zz],
            device_id=device(zz, x), device_id_type=MESH)

    def far(zz):
        compute(zz * 2 + other, False)
        stage[zz, 0] = part[...].astype(BF)
        if comm:
            to_other(zz).start()

    def step(i, c):
        zz = (z + 1 + i) % nz
        far(zz)
        compute(zz * 2 + x, False)
        if comm:
            to_other(zz).wait_recv()
        stage[zz, 1] = (part[...] + xin[zz].astype(F32)).astype(BF)
        if comm:
            to_owner(zz).start()
        return c

    lax.fori_loop(0, nz - 1, step, 0)
    far(z)
    compute(blk, True)
    for h in range(3):
        half = h % 2
        dq_ref[:, 64 * h : 64 * h + 64] = (dqacc[h][:, 64 * half : 64 * half + 64] * 0.125).astype(BF)
    if comm:
        to_other(z).wait_recv()
    part[...] += xin[z].astype(F32)

    def gather(i, c):
        zz = (z + nz - 1 - i) % nz
        if comm:
            from_sender(zz).wait_recv()
        part[...] += zin[zz].astype(F32)
        return c
    lax.fori_loop(0, nz - 1, gather, 0)
    dkv_ref[...] = part[...].astype(BF)

    if comm:
        def drain(i, c):
            zz = (z + 1 + i) % nz
            to_other(zz).wait_send()
            to_owner(zz).wait_send()
            return c
        lax.fori_loop(0, nz - 1, drain, 0)
        to_other(z).wait_send()


def attn_bwd(qb, do, kv, kaug, comm=True, cid=1):
    n, rows = kaug.shape[1], kaug.shape[2]
    nz = n // 2
    V = pl.BlockSpec(memory_space=pltpu.VMEM)
    return pl.pallas_call(
        functools.partial(attn_bwd_kernel, nz, comm),
        out_shape=(
            jax.ShapeDtypeStruct((rows, 192), BF),
            jax.ShapeDtypeStruct((rows, 384), BF),
        ),
        in_specs=[V] * 4,
        out_specs=(V,) * 2,
        scratch_shapes=[
            pltpu.VMEM((3, rows, 128), F32),
            pltpu.VMEM((rows, 384), F32),
            pltpu.VMEM((nz, 2, rows, 384), BF),
            pltpu.VMEM((nz, rows, 384), BF),
            pltpu.VMEM((nz, rows, 384), BF),
            pltpu.SemaphoreType.DMA((nz,)),
            pltpu.SemaphoreType.DMA((nz,)),
            pltpu.SemaphoreType.DMA((nz,)),
            pltpu.SemaphoreType.DMA((nz,)),
        ],
        compiler_params=pltpu.CompilerParams(
            collective_id=cid if comm else None, has_side_effects=comm, vmem_limit_bytes=60 * 2**20),
        cost_estimate=pl.CostEstimate(flops=40 * 10**9, bytes_accessed=2 * 10**8, transcendentals=10**7),
        name="attn_bwd",
    )(qb, do, kv, kaug)


EPS = 1e-06


def layer_norm(hidden_state, ln_gain, ln_shift):
    row_mean = jnp.mean(hidden_state, axis=-1, keepdims=True)
    centred = hidden_state - row_mean
    row_var = jnp.mean(centred * centred, axis=-1, keepdims=True)
    return centred * lax.rsqrt(row_var + EPS) * ln_gain + ln_shift


def norm_back(grad, total, gain):
    row_mean = jnp.mean(total, axis=-1, keepdims=True)
    centred = total - row_mean
    scale = lax.rsqrt(jnp.mean(centred * centred, axis=-1, keepdims=True) + EPS)
    n = centred * scale
    dn = grad * gain
    e = scale * (dn - jnp.mean(dn, axis=-1, keepdims=True) - n * jnp.mean(dn * n, axis=-1, keepdims=True))
    return e, jnp.sum(grad * n, axis=0), jnp.sum(grad, axis=0)


def gelu_parts(u):
    cdf = 0.5 * (1.0 + lax.erf(u * (0.5 ** 0.5)))
    pdf = jnp.exp(-0.5 * u * u) * ((2.0 * jnp.pi) ** -0.5)
    return cdf, pdf


def three(value):
    high = lax.reduce_precision(value, 8, 7)
    rest = value - high
    mid = lax.reduce_precision(rest, 8, 7)
    return [part.astype(BF) for part in (high, mid, rest - mid)]


def aug(columns, rows):
    out = jnp.stack(columns, axis=-1)
    return jnp.pad(out, ((0, 0), (0, 64 - out.shape[1])))


def shards(hidden_in, out_grad, segment_ids, alibi_slopes, qkv_weight, out_weight, gate_up_weight, down_weight, gains, biases):
    nh, nb = lax.axis_size("head"), lax.axis_size("blk")
    head, blk = lax.axis_index("head"), lax.axis_index("blk")
    token_rows, width = hidden_in.shape
    rows = token_rows * nh
    layers, wrows = qkv_weight.shape[:2]
    ff = gate_up_weight.shape[2] // 2
    ffd = down_weight.shape[1]
    group = width // nh
    quarter = ff // nh
    tokens = segment_ids.shape[0]

    small = jnp.concatenate([gains.reshape(layers, -1), biases.reshape(layers, -1)], axis=1)
    small = jnp.broadcast_to(small.reshape(layers, wrows, 1, 8), (layers, wrows, nh, 8))
    qkv_cols = qkv_weight.reshape(layers, wrows, 3, nh, group).transpose(0, 1, 3, 2, 4).reshape(layers, wrows, nh, 3 * group)
    gu_cols = gate_up_weight.reshape(layers, wrows, 2, nb, nh, ffd).transpose(0, 1, 4, 2, 3, 5).reshape(layers, wrows, nh, 2 * quarter)
    spread = lax.all_to_all(jnp.concatenate([qkv_cols, small, gu_cols], axis=3), "head", split_axis=2, concat_axis=1, tiled=True)
    spread = spread.reshape(layers, nh * wrows, -1)
    qk, gu0 = 3 * group, 3 * group + 8

    first = jnp.concatenate([spread[0, :, :gu0]] + [spread[l, :, qk:gu0] for l in range(1, layers)], axis=1)
    first = lax.all_gather(first, "blk", axis=0, tiled=True)
    qkv_w = [first[:, :qk]]
    smalls = []
    for l in range(layers):
        s = first[:, qk + 8 * l : qk + 8 * l + 8].astype(F32).reshape(nb * nh, 8, wrows)
        smalls.append(s.transpose(1, 0, 2).reshape(8, width))
    outs_all = lax.all_gather(out_weight, ("blk", "head"), axis=1, tiled=True)
    gu_w, down_w = [], []
    for l in range(layers):
        if l:
            qkv_w.append(lax.all_gather(spread[l, :, :qk], "blk", axis=0, tiled=True))
        gu_w.append(lax.all_gather(spread[l, :, gu0:], "blk", axis=0, tiled=True))
        down_w.append(lax.all_gather(down_weight[l], "blk", axis=0, tiled=True))
    out_w = [outs_all[l] for l in range(layers)]
    out_rows = [lax.dynamic_slice_in_dim(outs_all[l], head * group, group, 0) for l in range(layers)]

    slopes = lax.dynamic_slice_in_dim(alibi_slopes, head * 3, 3, 0)
    position = jnp.arange(tokens, dtype=jnp.int32).astype(F32)
    same = (segment_ids[:, None] == jnp.arange(5, dtype=jnp.int32)[None, :])
    apart = [jnp.where(same[:, s], 0.0, -1e30).astype(BF) for s in range(5)]
    inside = [same[:, s].astype(BF) for s in range(5)]
    one = jnp.ones((tokens,), BF)
    nothing = jnp.zeros((tokens, 64), BF)
    kaug = []
    for h in range(3):
        a = aug(three(slopes[h] * position) + [one] * 3 + apart, tokens)
        kaug.append(jnp.concatenate([nothing, a] if h % 2 == 0 else [a, nothing], axis=1))
    kaug = jnp.stack(kaug).reshape(3, nb, rows, 128)
    own_pos = (blk * rows).astype(F32) + jnp.arange(rows, dtype=jnp.int32).astype(F32)
    own_in = [lax.dynamic_slice_in_dim(v, blk * rows, rows, 0) for v in inside]
    own_one = jnp.ones((rows,), BF)

    def q_operand(q, lse):
        sides = []
        for sign in (1.0, -1.0):
            for h in range(3):
                row = -sign * slopes[h] * own_pos
                if lse is not None:
                    row = row - lse[h]
                a = aug([own_one * sign] * 3 + three(row) + own_in, rows)
                qh = q[:, 64 * h : 64 * h + 64] * jnp.asarray(0.125, BF)
                sides.append(jnp.concatenate([qh, a] if h % 2 == 0 else [a, qh], axis=1))
        return jnp.stack(sides).reshape(2, 3, rows, 128)

    def spread_rows(v):
        return lax.all_gather(v, "head", axis=0, tiled=True)

    def sum_rows(v):
        parts = lax.all_to_all(v.astype(BF).reshape(nh, token_rows, v.shape[1]), "head", split_axis=0, concat_axis=0, tiled=True)
        return jnp.sum(parts.astype(F32), axis=0)

    def mm(a, b, dims=NN):
        return lax.dot_general(a, b, dims, preferred_element_type=F32)

    state = hidden_in.astype(F32)
    saved = []
    for l in range(layers):
        gain, bias = smalls[l][:2], smalls[l][2:]
        xr = spread_rows(state.astype(BF))
        qb = lax.dynamic_slice_in_dim(bias[0], head * group, group, 0)
        vb = lax.dynamic_slice_in_dim(bias[1], head * group, group, 0)
        proj = (mm(xr, qkv_w[l]) + jnp.concatenate([qb, jnp.zeros((group,), F32), vb])).astype(BF)
        q = proj[:, :group]
        ctx, ctxf, lse, kv = attn_fwd(q_operand(q, None), proj[:, group:], kaug)
        lse = lse[:, :, 0]
        ctx_tok = lax.all_to_all(ctx, "head", split_axis=0, concat_axis=1, tiled=True)
        sum1 = state + (mm(ctx_tok, out_w[l]) + bias[2])
        y = layer_norm(sum1, gain[0], bias[3])
        yr = spread_rows(y.astype(BF))
        mixed = mm(yr, gu_w[l])
        gate, up = mixed[:, :quarter], mixed[:, quarter:]
        cdf, _ = gelu_parts(gate)
        hid = (gate * cdf * up).astype(BF)
        sum2 = y + (sum_rows(mm(hid, down_w[l])) + bias[4])
        state = layer_norm(sum2, gain[1], bias[5])
        saved.append((xr, q, ctx, ctxf, lse, kv, sum1, yr, gate, up, hid, sum2))
    output = state.astype(BF)

    grad = out_grad.astype(F32)
    done = [None] * layers
    for l in reversed(range(layers)):
        gain, bias = smalls[l][:2], smalls[l][2:]
        xr, q, ctx, ctxf, lse, kv, sum1, yr, gate, up, hid, sum2 = saved[l]
        e2, d_gain2, d_shift2 = norm_back(grad, sum2, gain[1])
        df_tok = e2.astype(BF)
        d_down_bias = jnp.sum(df_tok.astype(F32), axis=0)
        df = spread_rows(df_tok)
        dhid = mm(df, down_w[l], NT)
        cdf, pdf = gelu_parts(gate)
        dgu = jnp.concatenate([dhid * up * (cdf + gate * pdf), dhid * (gate * cdf)], axis=1).astype(BF)
        d_down = mm(hid, df, TN).astype(BF)
        d_gu = mm(yr, dgu, TN).astype(BF)
        ff_sum = lax.psum_scatter(jnp.concatenate([d_gu, d_down], axis=1), "blk", scatter_dimension=0, tiled=True)
        dy = e2 + sum_rows(mm(dgu, gu_w[l], NT))
        e1, d_gain1, d_shift1 = norm_back(dy, sum1, gain[0])
        da_tok = e1.astype(BF)
        d_out_bias = jnp.sum(da_tok.astype(F32), axis=0)
        da = spread_rows(da_tok)
        dctx = mm(da, out_rows[l], NT).astype(BF)
        d_out = mm(ctx, da, TN).astype(BF)
        delta = jnp.sum((dctx.astype(F32) * ctxf).reshape(rows, 3, 64), axis=2)
        do = []
        for h in range(3):
            a = aug(three(-delta[:, h]), rows)
            dh = dctx[:, 64 * h : 64 * h + 64]
            do.append(jnp.concatenate([a, dh] if h % 2 == 0 else [dh, a], axis=1))
        dq, dkv = attn_bwd(q_operand(q, lse), jnp.stack(do), kv, kaug)
        dproj = jnp.concatenate([dq, dkv], axis=1)
        d_qkv = mm(xr, dproj, TN).astype(BF)
        d_out = d_out.reshape(width, group)
        at_sum = lax.psum_scatter(jnp.concatenate([d_qkv, d_out], axis=1), "blk", scatter_dimension=0, tiled=True)
        d_bias = jnp.sum(dproj.astype(F32), axis=0)
        grad = e1 + sum_rows(mm(dproj, qkv_w[l], NT))
        tok_small = jnp.stack([d_gain1, d_gain2, d_out_bias, d_shift1, d_down_bias, d_shift2])
        zero = jnp.zeros((2, width), F32)
        head_small = jnp.stack([
            lax.dynamic_update_slice_in_dim(zero[0], d_bias[:group], head * group, 0),
            lax.dynamic_update_slice_in_dim(zero[1], d_bias[2 * group :], head * group, 0)])
        done[l] = (ff_sum, at_sum, tok_small, head_small)

    small_g = jnp.stack([jnp.concatenate([done[l][2], done[l][3]]) for l in range(layers)])
    small_g = small_g.reshape(layers * 8, nb * nh, wrows).transpose(1, 0, 2).reshape(nb * nh, layers * 8 * wrows)
    small_sum = lax.psum_scatter(small_g, ("blk", "head"), scatter_dimension=0, tiled=True).reshape(layers, 8, wrows)
    gains_grad = small_sum[:, 0:2]
    biases_grad = jnp.concatenate([small_sum[:, 6:8], small_sum[:, 2:6]], axis=1)

    def piece(index, lo, hi):
        return jnp.stack([done[l][index][:, lo:hi] for l in range(layers)])

    gu_piece = piece(0, 0, 2 * quarter)
    qkv_piece = piece(1, 0, qk)
    back = jnp.concatenate([qkv_piece, gu_piece], axis=2).reshape(layers, nh, wrows, -1)
    back = lax.all_to_all(back, "head", split_axis=1, concat_axis=1, tiled=True).astype(F32)
    qkv_grad = back[..., :qk].reshape(layers, nh, wrows, 3, group).transpose(0, 2, 3, 1, 4).reshape(layers, wrows, 3 * width)
    gu_grad = back[..., qk:].reshape(layers, nh, wrows, 2, nb, ffd).transpose(0, 2, 3, 4, 1, 5).reshape(layers, wrows, 2 * ff)
    down_grad = piece(0, 2 * quarter, 2 * quarter + width).astype(F32)
    out_piece = piece(1, qk, qk + group).reshape(layers, wrows, width)
    moves = [(b * nh + h, h * nb + b) for b in range(nb) for h in range(nh)]
    out_grad_w = lax.ppermute(out_piece, ("blk", "head"), moves).astype(F32)
    return output, grad, qkv_grad, out_grad_w, gu_grad, down_grad, gains_grad, biases_grad


def solution(mesh):
    both = ("blk", "head")
    tok, mid, last = P(both, None), P(None, both, None), P(None, None, both)
    return jax.shard_map(
        shards, mesh=mesh,
        in_specs=(tok, tok, P(), P(), mid, mid, mid, mid, last, last),
        out_specs=(tok, tok, mid, mid, mid, mid, last, last),
        check_vma=False,
    )
```

time: 2490 us -> 865 us (0.35)
  waiting for transfers between devices: 1190 us -> 180 us
  matrix products: 356 us -> 43 us
  local copies, waits for them, and re-layouts: 342 us -> 80 us
  Pallas kernels: 0 us -> 225 us
  blocking collectives: 358 us -> 202 us
  other arithmetic: 128 us -> 51.1 us
  loops' own time: 45.2 us -> 0 us
    reduce_scatter x6 -> x4, waiting for transfers between devices: 632 us -> 155 us  [the longest x2 155 us: shards(): lax.psum_scatter(jnp.concatenate([d_gu, d_down], axis=1), 'blk', scatter_...]
    all_gather x16 -> x5, waiting for transfers between devices: 417 us -> 0.05 us  [the longest x2 0.04 us: shards(): down_w.append(lax.all_gather(down_weight[l], 'blk', axis=0, tiled=True))]
    dot_general x135 -> x24, matrix products: 352 us -> 43 us  [mm(): return lax.dot_general(a, b, dims, preferred_element_type=F32)]
    pallas_call x0 -> x4, Pallas kernels: none -> 225 us  [the longest x2 124 us: attn_bwd(): pl.pallas_call(functools.partial(attn_bwd_kernel, nz, comm), out_shape=(j...]
    dynamic_slice x178 -> x5, local copies, waits for them, and re-layouts: 197 us -> 0.39 us  [the longest x2 0.16 us: shards(): vb = lax.dynamic_slice_in_dim(bias[1], head * group, group, 0)]
    unnamed x26 -> x9, waiting for transfers between devices: 128 us -> 1.84 us
    all_gather x8 -> x10, blocking collectives: 246 us -> 145 us  [the longest x8 78 us: spread_rows(): return lax.all_gather(v, 'head', axis=0, tiled=True)]
    all_to_all x4 -> x1, blocking collectives: 64.4 us -> 14.2 us  [shards(): lax.all_to_all(jnp.concatenate([qkv_cols, small, gu_cols], axis=3), 'head...]
  transfers between devices with their start and end apart: 28 -> 19, of which waited for: 16 -> 8; matrix products, arithmetic and copies ran while one was open for 26% -> 16% of each run, Pallas kernels for 0% -> 19%
where the time goes in v1:
time: 865 us; the launch traced here: 853 us
  Pallas kernels  225 us (26%)
  blocking collectives  202 us (23%)
  waiting for transfers between devices  180 us (21%)
  local copies, waits for them, and re-layouts  80 us (9%)
  starting transfers between devices  52.8 us (6%)
  other arithmetic  51.1 us (6%)
  matrix products  43 us (5%)
  between operations  19 us (2%)
    reduce_scatter x2, waiting for transfers between devices, shards(): lax.psum_scatter(jnp.concatenate([d_gu, d_down], axis=1), 'blk', scatter_...  155 us
    pallas_call x2, Pallas kernels, attn_bwd(): pl.pallas_call(functools.partial(attn_bwd_kernel, nz, comm), out_shape=(j...  124 us
    pallas_call x2, Pallas kernels, attn_fwd(): pl.pallas_call(functools.partial(attn_fwd_kernel, n // 2, comm), out_shap...  101 us
    all_gather x8, blocking collectives, spread_rows(): return lax.all_gather(v, 'head', axis=0, tiled=True)  78 us
    unnamed x1, blocking collectives  43.1 us
    dot_general x24, matrix products, mm(): return lax.dot_general(a, b, dims, preferred_element_type=F32)  43 us
    all_gather x1, blocking collectives, shards(): qkv_w.append(lax.all_gather(spread[l, :, :qk], 'blk', axis=0, tiled=True))  38.3 us
    all_gather x1, blocking collectives, shards(): first = lax.all_gather(first, 'blk', axis=0, tiled=True)  28.2 us
  transfers between devices with their start and end apart: 19, of which 8 were waited for; matrix products, arithmetic and copies ran while one was open for 16% of the time, Pallas kernels for 19%

profile of v1, /device:TPU:21, one launch (start us, length us, event | category | flops | bytes accessed | tf_op | source)
XLA Modules:
  0.0 852.7 jit_solution(1628751159365426211)
XLA Ops:
  14.0 14.2 %all_to_all.88 = bf16[2,24,4,2120]{3,1,0,2:T(8,128)(2,1)S(1)} all-to-all(bf16[2,24,4,2120]{3,1,0,2:T(8,128)(2,1)S(1)} %copy.182), channel_id=1, replica_groups=mesh['blk'=8,'head'=4] {'head'}, dimensions={2} | all-to-all | bytes 1628160 | tf_op jit(solution)/shard_map/all_to_all | solution.py:418
  48.1 11.2 %all_gather.46 = bf16[512,768]{1,0:T(8,128)(2,1)} all-gather(bf16[128,768]{1,0:T(8,128)(2,1)S(1)} %copy-done.40), channel_id=1, replica_groups=mesh['blk'=8,'head'=4] {'head'}, dimensions={0}, use_global_device_ids=true | all-gather | bytes 983040 | tf_op jit(solution)/shard_map/all_gather | solution.py:468
  73.6 28.2 %all_gather.45 = bf16[768,592]{1,0:T(8,128)(2,1)S(1)} all-gather(bf16[96,592]{1,0:T(8,128)(2,1)S(1)} %pad_maximum_fusion.19), channel_id=1, replica_groups=mesh['blk'=8,'head'=4] {'blk'}, dimensions={0}, use_global_device_ids=true | all-gather | bytes 1022976 | tf_op jit(solution)/shard_map/all_gather | solution.py:423
  112.1 46.4 %attn_fwd.2 = (bf16[512,192]{1,0:T(8,128)(2,1)}, f32[512,192]{1,0:T(8,128)}, f32[3,512,128]{2,1,0:T(8,128)}, bf16[8,512,384]{2,1,0:T(8,128)(2,1)}) custom-call(bf16[2,3,512,128]{3,2,1,0:T(8,128)(2,1)} %bitcast.301, bf16[512,384]{1,0:T(8,128)(2,1)} %slice.469.own_ref, bf16[3,8,512,128]{3,2,1,0:T(8,128)(2,1)} %pad_maximum_fusion.2.kaug_ref), custom_call_target="tpu_custom_call" | custom-call | flops 20000000000 | bytes 100000000 | tf_op jit(solution)/shard_map/attn_fwd/pallas_call | solution.py:207
  163.8 10.1 %all-to-all-start.1 = ((bf16[4,128,192]{1,2,0:T(8,128)(2,1)}), bf16[4,128,192]{1,2,0:T(8,128)(2,1)S(1)}, u32[]{:S(2)}, u32[]{:S(2)}) async-start(bf16[4,128,192]{1,2,0:T(8,128)(2,1)} %copy.195), calls=%async_computation.1 | async-start | bytes 393216 | tf_op jit(solution)/shard_map/all_to_all | solution.py:488
  179.5 9.4 %all_gather.48 = bf16[512,768]{1,0:T(8,128)(2,1)S(1)} all-gather(bf16[128,768]{1,0:T(8,128)(2,1)S(1)} %fusion.51), channel_id=1, replica_groups=mesh['blk'=8,'head'=4] {'head'}, dimensions={0}, use_global_device_ids=true | all-gather | bytes 983040 | tf_op jit(solution)/shard_map/all_gather | solution.py:468
  202.9 38.3 %all-gather.2 = bf16[1,768,576]{2,1,0:T(8,128)(2,1)S(1)} all-gather(bf16[1,96,576]{2,1,0:T(8,128)(2,1)S(1)} %copy-done.53), channel_id=4, replica_groups=mesh['blk'=8,'head'=4] {'blk'}, dimensions={1}, use_global_device_ids=true | all-gather | bytes 995328 | tf_op jit(solution)/shard_map/all_gather | solution.py:433
  242.0 11.4 %all_gather.51 = bf16[512,768]{1,0:T(8,128)(2,1)S(1)} all-gather(bf16[128,768]{1,0:T(8,128)(2,1)S(1)} %fusion.52), channel_id=1, replica_groups=mesh['blk'=8,'head'=4] {'head'}, dimensions={0}, use_global_device_ids=true | all-gather | bytes 983040 | tf_op jit(solution)/shard_map/all_gather | solution.py:468
  257.1 54.4 %attn_fwd.3 = (bf16[512,192]{1,0:T(8,128)(2,1)}, f32[512,192]{1,0:T(8,128)}, f32[3,512,128]{2,1,0:T(8,128)}, bf16[8,512,384]{2,1,0:T(8,128)(2,1)}) custom-call(bf16[2,3,512,128]{3,2,1,0:T(8,128)(2,1)} %bitcast.300, bf16[512,384]{1,0:T(8,128)(2,1)} %slice.487.own_ref, bf16[3,8,512,128]{3,2,1,0:T(8,128)(2,1)} %pad_maximum_fusion.2.kaug_ref), custom_call_target="tpu_custom_call" | custom-call | flops 20000000000 | bytes 100000000 | tf_op jit(solution)/shard_map/attn_fwd/pallas_call | solution.py:207
  313.2 5.8 all-to-all-start.3
  325.0 9.2 %all_gather.53 = bf16[512,768]{1,0:T(8,128)(2,1)S(1)} all-gather(bf16[128,768]{1,0:T(8,128)(2,1)S(1)} %fusion.53), channel_id=1, replica_groups=mesh['blk'=8,'head'=4] {'head'}, dimensions={0}, use_global_device_ids=true | all-gather | bytes 983040 | tf_op jit(solution)/shard_map/all_gather | solution.py:468
  349.4 7.4 all-to-all-done.4
  359.0 9.2 %all_gather.56 = bf16[512,768]{1,0:T(8,128)(2,1)S(1)} all-gather(bf16[128,768]{1,0:T(8,128)(2,1)S(1)} %get-tuple-element.125), channel_id=1, replica_groups=mesh['blk'=8,'head'=4] {'head'}, dimensions={0}, use_global_device_ids=true | all-gather | bytes 983040 | tf_op jit(solution)/shard_map/all_gather | solution.py:468
  389.1 9.6 %all_gather.57 = bf16[512,768]{1,0:T(8,128)(2,1)S(1)} all-gather(bf16[128,768]{1,0:T(8,128)(2,1)S(1)} %get-tuple-element.127), channel_id=1, replica_groups=mesh['blk'=8,'head'=4] {'head'}, dimensions={0}, use_global_device_ids=true | all-gather | bytes 983040 | tf_op jit(solution)/shard_map/all_gather | solution.py:468
  402.2 60.2 %attn_bwd.2 = (bf16[512,192]{1,0:T(8,128)(2,1)}, bf16[512,384]{1,0:T(8,128)(2,1)}) custom-call(bf16[2,3,512,128]{3,2,1,0:T(8,128)(2,1)} %bitcast.299, bf16[3,512,128]{2,1,0:T(8,128)(2,1)} %pad_maximum_fusion.13.do_ref, bf16[8,512,384]{2,1,0:T(8,128)(2,1)} %get-tuple-element.24.kv_ref, bf16[3,8,512,128]{3,2,1,0:T(8,128)(2,1)} %pad_maximum_fusion.2.kaug_ref), custom_call_target="tpu_custom_call" | custom-call | flops 40000000000 | bytes 200000000 | tf_op jit(solution)/shard_map/attn_bwd/pallas_call | solution.py:338
  465.7 5.8 all-to-all-start.6
  482.9 8.9 %all_gather.58 = bf16[512,768]{1,0:T(8,128)(2,1)S(1)} all-gather(bf16[128,768]{1,0:T(8,128)(2,1)S(1)} %get-tuple-element.119), channel_id=1, replica_groups=mesh['blk'=8,'head'=4] {'head'}, dimensions={0}, use_global_device_ids=true | all-gather | bytes 983040 | tf_op jit(solution)/shard_map/all_gather | solution.py:468
  510.4 9.2 %all_gather.59 = bf16[512,768]{1,0:T(8,128)(2,1)S(1)} all-gather(bf16[128,768]{1,0:T(8,128)(2,1)S(1)} %get-tuple-element.122), channel_id=1, replica_groups=mesh['blk'=8,'head'=4] {'head'}, dimensions={0}, use_global_device_ids=true | all-gather | bytes 983040 | tf_op jit(solution)/shard_map/all_gather | solution.py:468
  524.0 63.8 %attn_bwd.3 = (bf16[512,192]{1,0:T(8,128)(2,1)}, bf16[512,384]{1,0:T(8,128)(2,1)}) custom-call(bf16[2,3,512,128]{3,2,1,0:T(8,128)(2,1)} %bitcast.298, bf16[3,512,128]{2,1,0:T(8,128)(2,1)} %pad_maximum_fusion.14.do_ref, bf16[8,512,384]{2,1,0:T(8,128)(2,1)} %get-tuple-element.29.kv_ref, bf16[3,8,512,128]{3,2,1,0:T(8,128)(2,1)} %pad_maximum_fusion.2.kaug_ref), custom_call_target="tpu_custom_call" | custom-call | flops 40000000000 | bytes 200000000 | tf_op jit(solution)/shard_map/attn_bwd/pallas_call | solution.py:338
  612.6 43.1 %all-reduce.30 = f32[32,384]{1,0:T(8,128)S(1)} all-reduce(f32[32,384]{1,0:T(8,128)S(1)} %reshape.1081), channel_id=11, replica_groups=mesh['blk'=8,'head'=4] {'blk','head'}, use_global_device_ids=true, to_apply=%region_42.43.clone | all-reduce | flops 12288 | bytes 98304
  660.0 5.5 collective-permute-start
  666.4 73.4 %reduce-scatter.11.cloned.1.call-done = bf16[96,2304]{1,0:T(8,128)(2,1)} async-done(((bf16[768,2304]{1,0:T(8,128)(2,1)}), bf16[96,2304]{1,0:T(8,128)(2,1)}) %reduce-scatter.11.cloned.1.call-update) | async-done | bytes 442384 | tf_op jit(solution)/shard_map/reduce_scatter | solution.py:515
  740.8 81.4 %reduce-scatter.9.cloned.1.call-done = bf16[96,2304]{1,0:T(8,128)(2,1)} async-done(((bf16[768,2304]{1,0:T(8,128)(2,1)}), bf16[96,2304]{1,0:T(8,128)(2,1)}) %reduce-scatter.9.cloned.1.call-update) | async-done | bytes 442384 | tf_op jit(solution)/shard_map/reduce_scatter | solution.py:515
  833.3 6.0 all-to-all-done.9
  (651 shorter events, 211.7 us)
Async XLA Ops:
  7.2 170.2 %all-gather.11.cloned.1.call-start = ((), (), s32[]{:S(2)}) async-start(), calls=%async_computation.14 | async-start | bytes 2433024 | tf_op jit(solution)/shard_map/all_gather | solution.py:429
  7.9 180.9 %all-gather.13.cloned.1.call-start = ((), (), s32[]{:S(2)}) async-start(), calls=%async_computation.17 | async-start | bytes 2654208 | tf_op jit(solution)/shard_map/all_gather | solution.py:434
  30.3 164.1 %all-gather.15.cloned.1.call-start = ((), (), s32[]{:S(2)}) async-start(), calls=%async_computation.18 | async-start | bytes 1327104 | tf_op jit(solution)/shard_map/all_gather | solution.py:435
  31.1 303.2 %all-gather.17.cloned.1.call-start = ((), (), s32[]{:S(2)}) async-start(), calls=%async_computation.19 | async-start | bytes 2654208 | tf_op jit(solution)/shard_map/all_gather | solution.py:434
  31.6 308.0 %all-gather.19.cloned.1.call-start = ((), (), s32[]{:S(2)}) async-start(), calls=%async_computation.20 | async-start | bytes 1327104 | tf_op jit(solution)/shard_map/all_gather | solution.py:435
  107.2 134.1 %copy-start.83 = (f32[768]{0:T(1024)}, f32[768]{0:T(1024)S(1)}, u32[]{:S(2)}) copy-start(f32[768]{0:T(1024)S(1)} %mul.762) | copy-start | bytes 9220
  107.3 134.5 %copy-start.85 = (f32[768]{0:T(1024)}, f32[768]{0:T(1024)S(1)}, u32[]{:S(2)}) copy-start(f32[768]{0:T(1024)S(1)} %mul.772) | copy-start | bytes 9220
  108.1 133.7 %copy-start.93 = (f32[768]{0:T(1024)}, f32[768]{0:T(1024)S(1)}, u32[]{:S(2)}) copy-start(f32[768]{0:T(1024)S(1)} %add.509) | copy-start | bytes 9220
  163.8 13.5 %all-to-all-start.1 = ((bf16[4,128,192]{1,2,0:T(8,128)(2,1)}), bf16[4,128,192]{1,2,0:T(8,128)(2,1)S(1)}, u32[]{:S(2)}, u32[]{:S(2)}) async-start(bf16[4,128,192]{1,2,0:T(8,128)(2,1)} %copy.195), calls=%async_computation.1 | async-start | bytes 393216 | tf_op jit(solution)/shard_map/all_to_all | solution.py:488
  179.1 62.2 %copy-start.105 = (f32[128]{0:T(128)}, f32[128]{0:T(128)S(1)}, u32[]{:S(2)}) copy-start(f32[128]{0:T(128)S(1)} %broadcast_multiply_fusion.11) | copy-start | bytes 1540
  197.6 43.6 %all-to-all-start.2 = ((bf16[4,128,768]{2,1,0:T(8,128)(2,1)}), bf16[4,128,768]{2,1,0:T(8,128)(2,1)S(1)}, u32[]{:S(2)}, u32[]{:S(2)}) async-start(bf16[4,128,768]{2,1,0:T(8,128)(2,1)} %bitcast.30), calls=%async_computation.2 | async-start | bytes 1572864 | tf_op jit(solution)/shard_map/all_to_all | solution.py:471
  313.2 9.2 %all-to-all-start.3 = ((bf16[4,128,192]{1,2,0:T(8,128)(2,1)}), bf16[4,128,192]{1,2,0:T(8,128)(2,1)}, u32[]{:S(2)}, u32[]{:S(2)}) async-start(bf16[4,128,192]{1,2,0:T(8,128)(2,1)} %copy.197), calls=%async_computation.3 | async-start | bytes 393216 | tf_op jit(solution)/shard_map/all_to_all | solution.py:488
  342.9 13.9 %all-to-all-start.4 = ((bf16[4,128,768]{2,1,0:T(8,128)(2,1)}), bf16[4,128,768]{2,1,0:T(8,128)(2,1)S(1)}, u32[]{:S(2)}, u32[]{:S(2)}) async-start(bf16[4,128,768]{2,1,0:T(8,128)(2,1)} %bitcast.46), calls=%async_computation.4 | async-start | bytes 1572864 | tf_op jit(solution)/shard_map/all_to_all | solution.py:471
  372.5 14.0 %all-to-all-start.5 = ((bf16[4,128,768]{2,1,0:T(8,128)(2,1)}), bf16[4,128,768]{2,1,0:T(8,128)(2,1)S(1)}, u32[]{:S(2)}, u32[]{:S(2)}) async-start(bf16[4,128,768]{2,1,0:T(8,128)(2,1)} %bitcast.293), calls=%async_computation.5 | async-start | bytes 1572864 | tf_op jit(solution)/shard_map/all_to_all | solution.py:471
  465.7 16.5 %all-to-all-start.6 = ((bf16[4,128,768]{2,1,0:T(8,128)(2,1)}), bf16[4,128,768]{2,1,0:T(8,128)(2,1)S(1)}, u32[]{:S(2)}, u32[]{:S(2)}) async-start(bf16[4,128,768]{2,1,0:T(8,128)(2,1)} %bitcast.292), calls=%async_computation.6 | async-start | bytes 1572864 | tf_op jit(solution)/shard_map/all_to_all | solution.py:471
  496.0 13.7 %all-to-all-start.7 = ((bf16[4,128,768]{2,1,0:T(8,128)(2,1)}), bf16[4,128,768]{2,1,0:T(8,128)(2,1)S(1)}, u32[]{:S(2)}, u32[]{:S(2)}) async-start(bf16[4,128,768]{2,1,0:T(8,128)(2,1)} %bitcast.61), calls=%async_computation.7 | async-start | bytes 1572864 | tf_op jit(solution)/shard_map/all_to_all | solution.py:471
  500.0 157.0 %reduce-scatter.15.cloned.1.call-start = ((), (), s32[]{:S(2)}) async-start(), calls=%async_computation.22 | async-start | bytes 1327104 | tf_op jit(solution)/shard_map/reduce_scatter | solution.py:533
  504.7 154.2 %reduce-scatter.13.cloned.1.call-start = ((), (), s32[]{:S(2)}) async-start(), calls=%async_computation.21 | async-start | bytes 1327104 | tf_op jit(solution)/shard_map/reduce_scatter | solution.py:533
  524.0 63.8 %copy-start.30 = (bf16[512,768]{1,0:T(8,128)(2,1)S(1)}, bf16[512,768]{1,0:T(8,128)(2,1)}, u32[]{:S(2)}) copy-start(bf16[512,768]{1,0:T(8,128)(2,1)} %all_gather.46) | copy-start | bytes 2359300
  591.3 148.5 %reduce-scatter.11.cloned.1.call-start = ((), (), s32[]{:S(2)}) async-start(), calls=%async_computation.16 | async-start | bytes 3981312 | tf_op jit(solution)/shard_map/reduce_scatter | solution.py:515
  597.2 225.0 %reduce-scatter.9.cloned.1.call-start = ((), (), s32[]{:S(2)}) async-start(), calls=%async_computation.15 | async-start | bytes 3981312 | tf_op jit(solution)/shard_map/reduce_scatter | solution.py:515
  607.1 217.3 %all-to-all-start.8 = ((bf16[4,128,768]{2,1,0:T(8,128)(2,1)}), bf16[4,128,768]{2,1,0:T(8,128)(2,1)S(1)}, u32[]{:S(2)}, u32[]{:S(2)}) async-start(bf16[4,128,768]{2,1,0:T(8,128)(2,1)} %bitcast.74), calls=%async_computation.8 | async-start | bytes 1572864 | tf_op jit(solution)/shard_map/all_to_all | solution.py:471
  660.0 170.0 %collective-permute-start = (bf16[2,24,768]{2,1,0:T(8,128)(2,1)S(1)}, bf16[2,24,768]{2,1,0:T(8,128)(2,1)S(1)}, u32[]{:S(2)}, u32[]{:S(2)}) collective-permute-start(bf16[2,24,768]{2,1,0:T(8,128)(2,1)S(1)} %pad_maximum_fusion.20), channel_id=1, source_target_pairs={{0,0},{1,8},{2,16},{3,24},{4,1},{5,9},{6,17},{7,25},{8,2},{9,10},{... | collective-permute-start | bytes 221192 | tf_op jit(solution)/shard_map/ppermute | solution.py:561
  824.5 14.8 %all-to-all-start.9 = ((bf16[2,4,24,2112]{3,2,0,1:T(8,128)(2,1)}), bf16[2,4,24,2112]{3,2,0,1:T(8,128)(2,1)S(1)}, u32[]{:S(2)}, u32[]{:S(2)}) async-start(bf16[2,4,24,2112]{3,2,0,1:T(8,128)(2,1)} %copy.226), calls=%async_computation.11 | async-start | bytes 1671168 | tf_op jit(solution)/shard_map/all_to_all | solution.py:555
  (139 other events, 1168.4 us)
Sparse Core Ops, SparseCore 0:
  10.9 56.7 all-gather.10
  70.4 63.2 all-gather.12
  135.8 40.7 all-gather.14
  179.2 65.3 all-gather.16
  247.2 46.4 all-gather.18
  504.9 74.1 reduce-scatter.14
  591.5 63.6 reduce-scatter.12
  658.8 80.9 reduce-scatter.10
  743.5 78.6 reduce-scatter.8

commit v2 on v1

v2 whole, which is shorter than its diff:
```python
import functools
import types

import jax
import jax.numpy as jnp
from jax import lax
from jax.experimental import pallas as pl
from jax.experimental.pallas import tpu as pltpu
from jax.sharding import PartitionSpec as P

MESH = pl.DeviceIdType.MESH
BF = jnp.bfloat16
F32 = jnp.float32
NT = (((1,), (1,)), ((), ()))
NN = (((1,), (0,)), ((), ()))
TN = (((0,), (0,)), ((), ()))
EPS = 1e-06
K_AT = ((0, 0), (0, 1), (2, 0))
V_AT = ((1, 0), (1, 1), (2, 1))
VMEM = pl.BlockSpec(memory_space=pltpu.VMEM)
ANY = pl.BlockSpec(memory_space=pl.ANY)


def dot(a, b, dims=NN):
    return lax.dot_general(a, b, dims, preferred_element_type=F32)


def lanes(rows):
    return lax.broadcasted_iota(jnp.int32, (rows, 128), 1)


def in_half(half, rows):
    return lanes(rows) >= 64 if half else lanes(rows) < 64


def ones_half(half, rows):
    first = 0 if half else 64
    lane = lanes(rows)
    return jnp.where((lane >= first) & (lane < first + 3), 1.0, 0.0).astype(BF)


def k_operand(kv, aug, h):
    col, half = K_AT[h]
    return jnp.where(in_half(half, kv.shape[0]), kv[:, 128 * col : 128 * col + 128], aug)


def v_operand(kv, h):
    col, half = V_AT[h]
    rows = kv.shape[0]
    return jnp.where(in_half(half, rows), kv[:, 128 * col : 128 * col + 128], ones_half(half, rows))


def split3(value):
    high = value.astype(BF).astype(F32)
    mid = (value - high).astype(BF).astype(F32)
    return high, mid, value - high - mid


def with_lanes(base, first, values):
    lane = lanes(base.shape[0])
    for i, v in enumerate(values):
        base = jnp.where(lane == first + i, v, base)
    return base


def layer_norm(total, gain, shift):
    centred = total - jnp.mean(total, axis=-1, keepdims=True)
    scale = lax.rsqrt(jnp.mean(centred * centred, axis=-1, keepdims=True) + EPS)
    return centred * scale * gain + shift


def norm_back(grad, total, gain):
    centred = total - jnp.mean(total, axis=-1, keepdims=True)
    scale = lax.rsqrt(jnp.mean(centred * centred, axis=-1, keepdims=True) + EPS)
    n = centred * scale
    dn = grad * gain
    e = scale * (dn - jnp.mean(dn, axis=-1, keepdims=True) - n * jnp.mean(dn * n, axis=-1, keepdims=True))
    return e, jnp.sum(grad * n, axis=0, keepdims=True), jnp.sum(grad, axis=0, keepdims=True)


def normal_cdf(u):
    return 0.5 * (1.0 + lax.erf(u * (0.5**0.5)))


def normal_pdf(u):
    return jnp.exp(-0.5 * u * u) * ((2.0 * jnp.pi) ** -0.5)


def remote(src, dst, send, recv, device):
    return pltpu.make_async_remote_copy(
        src_ref=src, dst_ref=dst, send_sem=send, recv_sem=recv, device_id=device, device_id_type=MESH)


class Place:
    def __init__(self, nb):
        self.nz = nb // 2
        self.blk, self.head = lax.axis_index("blk"), lax.axis_index("head")
        self.z, self.x = self.blk // 2, self.blk % 2
        self.y, self.c = self.head // 2, self.head % 2
        self.other = 1 - self.x
        self.near_head = 2 * self.y + 1 - self.c
        self.far_head = 2 * (1 - self.y) + self.c
        self.cross_head = 2 * (1 - self.y) + 1 - self.c
        self.core = (self.blk, self.near_head)
        self.across = (self.blk, self.far_head)
        self.beside = (self.z * 2 + self.other, self.head)

    def column(self, zz):
        return (zz * 2 + self.x, self.head)

    def turn(self, i):
        return (self.z + 1 + i) % self.nz

    def enter(self):
        barrier = pltpu.get_barrier_semaphore()
        for device in (self.core, self.across, self.beside):
            pl.semaphore_signal(barrier, inc=1, device_id=device, device_id_type=MESH)

        def greet(i, carry):
            pl.semaphore_signal(barrier, inc=1, device_id=self.column(self.turn(i)), device_id_type=MESH)
            return carry
        lax.fori_loop(0, self.nz - 1, greet, 0)
        pl.semaphore_wait(barrier, 3 + self.nz - 1)


class HeadGather:
    def __init__(self, at, buf, send, recv):
        self.near = remote(buf.at[at.head], buf.at[at.head], send.at[0], recv.at[0], at.core)
        self.far = remote(buf.at[at.head], buf.at[at.head], send.at[1], recv.at[1], at.across)
        self.pass_on = remote(buf.at[at.far_head], buf.at[at.far_head], send.at[2], recv.at[2], at.core)

    def start(self):
        self.far.start()
        self.near.start()

    def wait_near(self):
        self.near.wait_recv()

    def wait_far(self):
        self.far.wait_recv()
        self.pass_on.start()
        self.pass_on.wait_recv()

    def finish(self):
        self.near.wait_send()
        self.far.wait_send()
        self.pass_on.wait_send()


class HeadSum:
    def __init__(self, at, part, stage, inbox, send, recv):
        self.at, self.part, self.stage, self.inbox = at, part, stage, inbox
        to = (at.core, at.core, at.across)
        self.copies = [remote(stage.at[i], inbox.at[i], send.at[i], recv.at[i], to[i]) for i in range(3)]

    def send_cross(self):
        self.stage[0] = self.part[self.at.cross_head].astype(BF)
        self.copies[0].start()

    def send_near(self):
        self.stage[1] = self.part[self.at.near_head].astype(BF)
        self.copies[1].start()

    def relay(self):
        self.copies[0].wait_recv()
        self.stage[2] = (self.part[self.at.far_head] + self.inbox[0].astype(F32)).astype(BF)
        self.copies[2].start()

    def total(self):
        self.copies[1].wait_recv()
        near = self.part[self.at.head] + self.inbox[1].astype(F32)
        self.copies[2].wait_recv()
        return near + self.inbox[2].astype(F32)

    def finish(self):
        for copy in self.copies:
            copy.wait_send()


class BlockSum:
    def __init__(self, at, item):
        self.at, self.stage, self.xin, self.zin = at, item.stage, item.xin, item.zin
        self.xsend, self.xrecv, self.zsend, self.zrecv = item.xsend, item.xrecv, item.zsend, item.zrecv

    def to_beside(self, zz):
        return remote(self.stage.at[zz * 2 + self.at.other], self.xin.at[zz], self.xsend.at[zz], self.xrecv.at[zz], self.at.beside)

    def to_owner(self, zz):
        at = self.at
        return remote(self.stage.at[zz * 2 + at.x], self.zin.at[at.z], self.zsend.at[zz], self.zrecv.at[at.z], at.column(zz))

    def from_sender(self, zz):
        at = self.at
        return remote(self.stage.at[zz * 2 + at.x], self.zin.at[zz], self.zsend.at[zz], self.zrecv.at[zz], at.column(zz))

    def each(self, first, last, do):
        def step(i, carry):
            do(self.at.turn(i))
            return carry
        lax.fori_loop(first, last, step, 0)

    def start(self):
        self.each(0, self.at.nz, lambda zz: self.to_beside(zz).start())

    def relay_one(self, zz):
        self.to_beside(zz).wait_recv()
        own = zz * 2 + self.at.x
        self.stage[own] = (self.stage[own].astype(F32) + self.xin[zz].astype(F32)).astype(BF)
        self.to_owner(zz).start()

    def relay(self):
        self.each(0, self.at.nz - 1, self.relay_one)

    def total(self, emit):
        at = self.at
        self.to_beside(at.z).wait_recv()
        self.each(0, at.nz - 1, lambda zz: self.from_sender(zz).wait_recv())
        value = self.stage[at.blk].astype(F32) + self.xin[at.z].astype(F32)
        emit(lax.fori_loop(0, at.nz - 1, lambda i, v: v + self.zin[at.turn(i)].astype(F32), value))

    def finish(self):
        self.each(0, self.at.nz, lambda zz: self.to_beside(zz).wait_send())
        self.each(0, self.at.nz - 1, lambda zz: self.to_owner(zz).wait_send())


def box(tree):
    if isinstance(tree, dict):
        return types.SimpleNamespace(**{k: box(v) for k, v in tree.items()})
    return [box(v) for v in tree] if isinstance(tree, list) else tree


def call(body, name, collective_id, near=None, far=None, table=None, out=None, far_out=None, scratch=None):
    groups = [near or {}, far or {}, table or {}, out or {}, far_out or {}, scratch or {}]
    flat, trees = zip(*[jax.tree.flatten(g) for g in groups])
    counts = [len(f) for f in flat]

    def kernel(*refs):
        named, first = {}, 0
        for tree, count in zip(trees, counts):
            named.update(jax.tree.unflatten(tree, refs[first : first + count]))
            first += count
        body(box(named))

    smem = pl.BlockSpec(memory_space=pltpu.SMEM)
    results = pl.pallas_call(
        kernel,
        out_shape=tuple(flat[3]) + tuple(flat[4]),
        in_specs=[VMEM] * counts[0] + [ANY] * counts[1] + [smem] * counts[2],
        out_specs=(VMEM,) * counts[3] + (ANY,) * counts[4],
        scratch_shapes=list(flat[5]),
        compiler_params=pltpu.CompilerParams(
            collective_id=collective_id, has_side_effects=True, vmem_limit_bytes=63 * 2**20),
        cost_estimate=pl.CostEstimate(flops=10**11, bytes_accessed=2 * 10**8, transcendentals=10**7),
        name=name,
    )(*flat[0], *flat[1], *flat[2])
    done = jax.tree.unflatten(trees[3], results[: counts[3]])
    done.update(jax.tree.unflatten(trees[4], results[counts[3] :]))
    return box(done)


def shape(*dims, dtype=BF):
    return jax.ShapeDtypeStruct(dims, dtype)


def keep(*dims, dtype=BF):
    return pltpu.VMEM(dims, dtype)


def copies(*dims):
    return pltpu.SemaphoreType.DMA(dims)


Q_HALF = (0, 1, 0)
ROW_LANE = 9


def row_term(blk, slopes_ref, h, rows):
    position = (blk * rows + lax.broadcasted_iota(jnp.int32, (rows, 128), 0)).astype(F32)
    return position * slopes_ref[h]


def query_base(q_ref, qaug_ref, side, h, rows):
    if h < 2:
        data = q_ref[:, 0:128]
    else:
        data = jnp.concatenate([q_ref[:, 128:192], jnp.zeros((rows, 64), q_ref.dtype)], axis=1)
    half = Q_HALF[h]
    return jnp.where(in_half(half, rows), data.astype(F32) * 0.125, qaug_ref[side, h].astype(F32)), 0 if half else 64


def query_operand(at, q_ref, qaug_ref, slopes_ref, side, h, rows, lse=None):
    base, first = query_base(q_ref, qaug_ref, side, h, rows)
    term = row_term(at.blk, slopes_ref, h, rows)
    term = -term if side == 0 else term
    if lse is not None:
        term = term - lse
    return with_lanes(base, first + ROW_LANE, split3(term)).astype(BF)


def fwd_block(side, diag, kv, aug, q_ref, m_ref, acc_ref):
    for h in range(3):
        k = k_operand(kv, aug, h)
        if diag:
            s = jnp.minimum(dot(q_ref[0, h], k, NT), dot(q_ref[1, h], k, NT))
        else:
            s = dot(q_ref[side, h], k, NT)
        m_old = m_ref[h]
        m_new = jnp.maximum(m_old, jnp.max(s, axis=1, keepdims=True))
        p = jnp.exp(s - m_new[:, :1]).astype(BF)
        acc_ref[h] = acc_ref[h] * jnp.exp(m_old - m_new) + dot(p, v_operand(kv, h))
        m_ref[h] = m_new


class BlockGather:
    def __init__(self, at, item):
        self.at, self.buf, self.zsend, self.xsend, self.recv = at, item.buf, item.zsend, item.xsend, item.recv

    def copy(self, b, send, device):
        return remote(self.buf.at[b], self.buf.at[b], send, self.recv.at[b], device)

    def to_right(self, b):
        return self.copy(b, self.zsend.at[0, b], self.at.column(self.at.z + 1))

    def to_left(self, b):
        return self.copy(b, self.zsend.at[1, b], self.at.column(self.at.z - 1))

    def to_beside(self, b):
        return self.copy(b, self.xsend.at[b], self.at.beside)

    def start(self):
        at = self.at

        @pl.when(at.z < at.nz - 1)
        def _():
            self.to_right(at.blk).start()

        @pl.when(at.z > 0)
        def _():
            self.to_left(at.blk).start()
        self.to_beside(at.blk).start()

    def wait(self, b):
        self.to_beside(b).wait_recv()

    def serve(self, d):
        at = self.at

        @pl.when(at.z - d >= 0)
        def _():
            b = (at.z - d) * 2 + at.x
            self.wait(b)
            self.to_beside(b).start()

            @pl.when(at.z < at.nz - 1)
            def _():
                self.to_right(b).start()

        @pl.when(at.z + d < at.nz)
        def _():
            b = (at.z + d) * 2 + at.x
            self.wait(b)
            self.to_beside(b).start()

            @pl.when(at.z > 0)
            def _():
                self.to_left(b).start()

    def serve_all(self):
        def step(d, carry):
            self.serve(d)
            return carry
        lax.fori_loop(1, self.at.nz, step, 0)

    def collect(self):
        def step(zz, carry):
            self.wait(zz * 2 + self.at.other)
            return carry
        lax.fori_loop(0, self.at.nz, step, 0)

    def finish(self):
        at = self.at

        def drain(zz, carry):
            b = zz * 2 + at.x
            self.to_beside(b).wait_send()

            @pl.when((zz <= at.z) & (at.z < at.nz - 1))
            def _():
                self.to_right(b).wait_send()

            @pl.when((zz >= at.z) & (at.z > 0))
            def _():
                self.to_left(b).wait_send()
            return carry
        lax.fori_loop(0, at.nz, drain, 0)


def attention(at, gather, q_op, kaug, m_ref, acc_ref, behind):
    m_ref[...] = jnp.full(m_ref.shape, -1e30, F32)
    acc_ref[...] = jnp.zeros(acc_ref.shape, F32)
    kv = gather.buf
    nz = at.nz

    def compute(b, diag=False):
        fwd_block((b > at.blk).astype(jnp.int32), diag, kv.at[b], kaug[b], q_op, m_ref, acc_ref)

    compute(at.blk, True)

    def visit_step(d, first, last):
        def visit(i, carry):
            zz = jnp.where(i % 2 == 0, at.z - d + i // 2, at.z + d - i // 2)
            xx = jnp.where(i < 2, at.x, at.other)

            @pl.when((zz >= 0) & (zz < nz) & ((i != 3) | (d > 1)))
            def _():
                b = zz * 2 + xx

                @pl.when(i >= 2)
                def _():
                    gather.wait(b)
                compute(b)
            return carry
        lax.fori_loop(first, last, visit, 0)

    def step(d, carry):
        @pl.when(d < nz)
        def _():
            gather.serve(d)
            behind(d)
        visit_step(d, jnp.where(d < nz, 0, 2), 4)
        return carry
    lax.fori_loop(1, nz + 1, step, 0)


def attention_end(at, q_ref, qaug, slopes, m_ref, acc_ref, ctx_ref, ctxf_ref, qb_ref):
    rows = ctx_ref.shape[0]
    for h in range(3):
        half = V_AT[h][1]
        first = 0 if half else 64
        acc = acc_ref[h]
        total = acc[:, first : first + 1]
        ctx = acc[:, 64 * half : 64 * half + 64] / total
        ctxf_ref[:, 64 * h : 64 * h + 64] = ctx
        ctx_ref[:, 64 * h : 64 * h + 64] = ctx.astype(BF)
        lse = m_ref[h] + jnp.log(total)
        for side in range(2):
            qb_ref[side, h] = query_operand(at, q_ref, qaug, slopes, side, h, rows, lse)


def fwd_kernel(nb, layers, host, R):
    at = Place(nb)
    rows = R.kaug.shape[1]
    half_rows = rows // 2
    quarter = R.hid.shape[1]
    group = R.ctx_now[0].shape[1]
    at.enter()
    part = R.part
    head_sum = HeadSum(at, part, R.hs_stage, R.hs_in, R.hs_send, R.hs_recv)
    gather_x = [HeadGather(at, R.xr_now[l], R.x_send.at[l], R.x_recv.at[l]) for l in range(layers)]
    gather_y = [HeadGather(at, R.yr_now[l], R.y_send.at[l], R.y_recv.at[l]) for l in range(layers)]
    kv = BlockGather(at, R.kv_now)
    saves = []

    def save(source, target):
        saves.append(pltpu.make_async_copy(source, target, R.saved.at[len(saves)]))
        saves[-1].start()
        return len(saves) - 1

    waited = []

    def wait_saved(number):
        saves[number].wait()
        waited.append(number)

    if host:
        qkv, gu, down = [[BlockGather(at, item) for item in items] for items in (R.qkv_now, R.gu_now, R.down_now)]
        ow = BlockGather(at, R.ow_now)
        order = ((qkv, R.qkv_own), (gu, R.gu_own), (down, R.down_own))
        qkv[0].buf[at.blk] = R.qkv_own[0][...]
        qkv[0].start()

    R.xr_now[0][at.head] = R.x0[...]
    gather_x[0].start()
    if host:
        for gathers, owns in order:
            for l in range(layers):
                if gathers is not qkv or l:
                    gathers[l].buf[at.blk] = owns[l][...]
        ow.buf[at.blk] = R.ow_own[...]
    for side in range(2):
        for h in range(3):
            R.qaug_now[side, h] = R.qaug[side, h]

    def weight(gathers, given, l, lo=0, hi=None):
        if not host:
            return given[l][:, lo:hi]
        v = gathers[l].buf[:, :, lo:hi]
        return v.reshape(v.shape[0] * v.shape[1], v.shape[2])

    def small(l, t):
        return R.small[8 * l + t : 8 * l + t + 1, :]

    def of(buf, half):
        v = buf[pl.ds(2 * half, 2)]
        return v.reshape(half_rows, v.shape[2])

    def half_at(half):
        return pl.ds(pl.multiple_of(half * half_rows, half_rows), half_rows)

    def of_group(row):
        value = jnp.zeros((1, group), F32)
        for h in range(4):
            value = jnp.where(at.head == h, row[:, group * h : group * h + group], value)
        return value

    if host:
        qkv[0].serve_all()
        ow.start()
        gu[0].start()
        down[0].start()
        qkv[0].collect()
        tail = weight(qkv, None, 0, 512, 640).astype(F32).T
        R.small[...] = tail[64 : 64 + 8 * layers, :]
    else:
        R.small[...] = R.small_given[...]
    R.state[...] = R.x0[...].astype(F32)
    gather_x[0].wait_near()
    gather_x[0].wait_far()

    for l in range(layers):
        last = l == layers - 1
        x_all = R.xr_now[l][...].reshape(rows, -1)
        save(R.xr_now[l], R.xr[l])
        qb, vb = of_group(small(l, 2)), of_group(small(l, 3))
        none = jnp.zeros((1, 128), F32)
        kv_bias = jnp.concatenate([none, vb[:, :128], none[:, :64], vb[:, 128:192]], axis=1)
        if l:
            pl.semaphore_wait(R.kv_free, 3 - (at.z == 0).astype(jnp.int32) - (at.z == at.nz - 1).astype(jnp.int32))
        kv.buf[at.blk] = (dot(x_all, weight(qkv if host else None, R.qkv_given, l, 0, 384)) + kv_bias).astype(BF)
        kv.start()
        R.q[...] = (dot(x_all, weight(qkv if host else None, R.qkv_given, l, 384, 576)) + qb).astype(BF)
        for side in range(2):
            for h in range(3):
                R.q_op[side, h] = query_operand(at, R.q, R.qaug_now, R.slopes, side, h, rows)

        def behind(d, l=l):
            if host:
                if l == 0:
                    ow.serve(d)
                gu[l].serve(d)
                down[l].serve(d)
        attention(at, kv, R.q_op, R.kaug, R.m, R.acc, behind)
        attention_end(at, R.q, R.qaug_now, R.slopes, R.m, R.acc, R.ctx_now[l], R.ctxf_now[l], R.qb_now[l])
        kv_saved = save(kv.buf, R.kv[l])
        save(R.ctx_now[l], R.ctx[l])
        save(R.ctxf_now[l], R.ctxf[l])
        save(R.qb_now[l], R.qb[l])
        kv.finish()
        if l == 0 and host:
            ow.collect()
            for i in range(layers):
                step = group // nb
                for b in range(nb):
                    R.ow_wide[...] = ow.buf[b].astype(F32)
                    R.ow_flat[step * b : step * b + step, :] = R.ow_wide[step * i : step * i + step, :]
                R.out_now[i][...] = R.ow_flat[...].astype(BF)
                save(R.out_now[i], R.out_w[i])
        if not last and host:
            qkv[l + 1].start()
        out_w = R.out_now[l][...] if host else R.out_given[l][...]
        if l:
            head_sum.finish()
        for number, half in enumerate((1 - at.y, at.y)):
            a = dot(R.ctx_now[l][half_at(half), :], out_w)
            part[pl.ds(2 * half, 2)] = a.reshape(2, half_rows // 2, a.shape[1])
            if number == 0:
                head_sum.send_cross()
            else:
                head_sum.send_near()
        head_sum.relay()
        wait_saved(kv_saved)
        if not last:
            pl.semaphore_signal(R.kv_free, inc=1, device_id=at.beside, device_id_type=MESH)

            @pl.when(at.z > 0)
            def _():
                pl.semaphore_signal(R.kv_free, inc=1, device_id=at.column(at.z - 1), device_id_type=MESH)

            @pl.when(at.z < at.nz - 1)
            def _():
                pl.semaphore_signal(R.kv_free, inc=1, device_id=at.column(at.z + 1), device_id_type=MESH)
        R.sum1_now[l][...] = R.state[...] + (head_sum.total() + small(l, 4))
        save(R.sum1_now[l], R.sum1[l])
        y = layer_norm(R.sum1_now[l][...], small(l, 0), small(l, 5))
        R.yr_now[l][at.head] = y.astype(BF)
        gather_y[l].start()
        R.state[...] = y
        if host:
            gu[l].collect()
            down[l].collect()
        gather_y[l].wait_near()
        if l:
            wait_saved(mixed_saved)
        head_sum.finish()
        for number, half in enumerate((at.y, 1 - at.y)):
            if number == 1:
                if not last and host:
                    qkv[l + 1].serve_all()
                    gu[l + 1].start()
                    down[l + 1].start()
                gather_y[l].wait_far()
            here = half_at(half)
            y_half = of(R.yr_now[l], half)
            gu_w = lambda lo: weight(gu if host else None, R.gu_given, l, lo, lo + 256)
            for col in range(0, quarter, 256):
                gate = dot(y_half, gu_w(col))
                up = dot(y_half, gu_w(quarter + col))
                R.mixed_now[here, col : col + 256] = gate
                R.mixed_now[here, quarter + col : quarter + col + 256] = up
                R.hid[:, col : col + 256] = (gate * normal_cdf(gate) * up).astype(BF)
            f = dot(R.hid[...], weight(down if host else None, R.down_given, l))
            part[pl.ds(2 * half, 2)] = f.reshape(2, half_rows // 2, f.shape[1])
            if number == 0:
                head_sum.send_near()
            else:
                head_sum.send_cross()
        mixed_saved = save(R.mixed_now, R.mixed[l])
        save(R.yr_now[l], R.yr[l])
        if host:
            save(qkv[l].buf, R.qkv_w[l])
            save(gu[l].buf, R.gu_w[l])
            save(down[l].buf, R.down_w[l])
        head_sum.relay()
        if not last and host:
            qkv[l + 1].collect()
        R.sum2_now[l][...] = R.state[...] + (head_sum.total() + small(l, 6))
        save(R.sum2_now[l], R.sum2[l])
        state = layer_norm(R.sum2_now[l][...], small(l, 1), small(l, 7))
        R.state[...] = state
        if last:
            R.output[...] = state.astype(BF)
        else:
            R.xr_now[l + 1][at.head] = state.astype(BF)
            gather_x[l + 1].start()
            gather_x[l + 1].wait_near()
            gather_x[l + 1].wait_far()
    for l in range(layers):
        gather_x[l].finish()
        gather_y[l].finish()
    head_sum.finish()
    if host:
        for items in (qkv, gu, down):
            for item in items:
                item.finish()
        ow.finish()
    for number, copy in enumerate(saves):
        if number not in waited:
            copy.wait()


def block_gather_item(nb, *dims):
    return dict(buf=keep(nb, *dims), zsend=copies(2, nb), xsend=copies(nb), recv=copies(nb))


def fwd(x0, slopes, qaug, kaug, weights, layers, host):
    nb, rows = kaug.shape[:2]
    tokens, width = x0.shape
    group = width // 4
    each = range(layers)
    r = width // nb
    ff2 = (weights.gu_own if host else weights.gu_given)[0].shape[1]
    quarter = ff2 // 2
    keep_rows = lambda: [keep(4, tokens, width) for _ in each]
    scratch = dict(
        xr_now=keep_rows(), x_send=copies(layers, 3), x_recv=copies(layers, 3),
        yr_now=keep_rows(), y_send=copies(layers, 3), y_recv=copies(layers, 3),
        part=keep(4, tokens, width, dtype=F32), hs_stage=keep(3, tokens, width), hs_in=keep(3, tokens, width),
        hs_send=copies(3), hs_recv=copies(3), state=keep(tokens, width, dtype=F32),
        kv_now=block_gather_item(nb, rows, 384), kv_free=pltpu.SemaphoreType.REGULAR, saved=copies(16 * layers),
        q=keep(rows, group), q_op=keep(2, 3, rows, 128), qaug_now=keep(2, 3, rows, 128),
        m=keep(3, rows, 128, dtype=F32), acc=keep(3, rows, 128, dtype=F32),
        ctx_now=[keep(rows, group) for _ in each], ctxf_now=[keep(rows, group, dtype=F32) for _ in each],
        qb_now=[keep(2, 3, rows, 128) for _ in each],
        sum1_now=[keep(tokens, width, dtype=F32) for _ in each], sum2_now=[keep(tokens, width, dtype=F32) for _ in each],
        mixed_now=keep(rows, ff2, dtype=F32), hid=keep(rows // 2, quarter))
    far_out = dict(
        xr=[shape(4, tokens, width) for _ in each], yr=[shape(4, tokens, width) for _ in each],
        kv=[shape(nb, rows, 384) for _ in each], ctx=[shape(rows, group) for _ in each],
        ctxf=[shape(rows, group, dtype=F32) for _ in each], qb=[shape(2, 3, rows, 128) for _ in each],
        sum1=[shape(tokens, width, dtype=F32) for _ in each], sum2=[shape(tokens, width, dtype=F32) for _ in each],
        mixed=[shape(rows, ff2, dtype=F32) for _ in each])
    near = dict(x0=x0, qaug=qaug, kaug=kaug, **vars(weights))
    if host:
        far_out.update(qkv_w=[shape(nb, *w.shape) for w in weights.qkv_own], gu_w=[shape(nb, *w.shape) for w in weights.gu_own],
                       down_w=[shape(nb, *w.shape) for w in weights.down_own], out_w=[shape(group, width) for _ in each])
        scratch.update(
            qkv_now=[block_gather_item(nb, *w.shape) for w in weights.qkv_own],
            gu_now=[block_gather_item(nb, *w.shape) for w in weights.gu_own],
            down_now=[block_gather_item(nb, *w.shape) for w in weights.down_own],
            ow_now=block_gather_item(nb, *weights.ow_own.shape), out_now=[keep(group, width) for _ in each],
            ow_wide=keep(*weights.ow_own.shape, dtype=F32), ow_flat=keep(group, width, dtype=F32))
        near.update(qkv_given=[], gu_given=[], down_given=[], out_given=[])
    out = dict(output=shape(tokens, width), small=shape(8 * layers, width, dtype=F32))
    done = call(functools.partial(fwd_kernel, nb, layers, host), "forward", 0, near=near, table=dict(slopes=slopes),
                out=out, far_out=far_out, scratch=scratch)
    if host:
        done.qkv_w = [w.reshape(width, -1)[:, :576] for w in done.qkv_w]
        done.gu_w = [w.reshape(width, -1) for w in done.gu_w]
        done.down_w = [w.reshape(quarter, -1) for w in done.down_w]
    else:
        done.qkv_w, done.gu_w, done.down_w, done.out_w = weights.qkv_given, weights.gu_given, weights.down_given, weights.out_given
    done.xr = [v.reshape(rows, width) for v in done.xr]
    done.yr = [v.reshape(rows, width) for v in done.yr]
    return done


OW_ROWS = 32


def attn_back(at, R, l, dkv, top, ff_start, after_first):
    nz, rows = at.nz, R.kvbuf.shape[1]
    q_ref, kaug, do_ref, acc, dqacc = R.qb[l], R.kaug, R.do, R.dkv_acc, R.dqacc
    slots = R.dkv.stage.shape[0]

    def load(zz, slot):
        b = zz * 2 + (at.other if slot == 0 else at.x)
        return pltpu.make_async_copy(R.kv[l].at[b], R.kvbuf.at[slot], R.kvsem.at[slot])

    dqacc[...] = jnp.zeros(dqacc.shape, F32)

    def compute(b, slot, diag):
        side = (b > at.blk).astype(jnp.int32)
        kv, aug = R.kvbuf.at[slot], kaug[b]
        dks, dvs = [], []
        for h in range(3):
            k, v = k_operand(kv, aug, h), v_operand(kv, h)
            if diag:
                s = jnp.minimum(dot(k, q_ref[0, h], NT), dot(k, q_ref[1, h], NT))
            else:
                s = dot(k, q_ref[side, h], NT)
            p = jnp.exp(s)
            ds = (p * dot(v, do_ref[h], NT)).astype(BF)
            dvs.append(dot(p.astype(BF), do_ref[h]))
            dks.append(dot(ds, q_ref[side, h]))
            dqacc[h] += dot(ds, k, TN)
        low = in_half(0, rows)
        acc[:, 0:128] = jnp.where(low, dks[0], dks[1])
        acc[:, 128:256] = jnp.where(low, dvs[0], dvs[1])
        acc[:, 256:384] = jnp.where(low, dks[2], dvs[2])

    def to_beside(i):
        zz = at.turn(i)
        return remote(R.dkv.stage.at[i % slots, 0], R.dkv.xin.at[zz], R.dkv.xsend.at[zz], R.dkv.xrecv.at[zz], at.beside)

    def to_owner(i):
        zz = at.turn(i)
        return remote(R.dkv.stage.at[i % slots, 1], R.dkv.zin.at[at.z], R.dkv.zsend.at[zz], R.dkv.zrecv.at[at.z], at.column(zz))

    def from_sender(zz):
        return remote(R.dkv.stage.at[0, 1], R.dkv.zin.at[zz], R.dkv.zsend.at[zz], R.dkv.zrecv.at[zz], at.column(zz))

    def far(i):
        zz = at.turn(i)
        load(zz, 1).start()
        load(zz, 0).wait()
        compute(zz * 2 + at.other, 0, False)

        @pl.when(i >= slots)
        def _():
            to_beside(i - slots).wait_send()
        R.dkv.stage[i % slots, 0] = acc[...].astype(BF)
        to_beside(i).start()

    load(at.turn(0), 0).start()
    if not top:
        pl.semaphore_wait(R.dkv.free, nz)

    def step(i, carry):
        zz = at.turn(i)
        far(i)
        load(at.turn(i + 1), 0).start()
        load(zz, 1).wait()
        compute(zz * 2 + at.x, 1, False)

        @pl.when(i >= slots)
        def _():
            to_owner(i - slots).wait_send()
        to_beside(i).wait_recv()
        R.dkv.stage[i % slots, 1] = (acc[...] + R.dkv.xin[zz].astype(F32)).astype(BF)
        to_owner(i).start()

        @pl.when(i == 0)
        def _():
            after_first()
        return carry
    lax.fori_loop(0, nz - 1, step, 0)
    far(nz - 1)
    ff_start()
    load(at.z, 1).wait()
    compute(at.blk, 1, True)
    dq = jnp.where(in_half(0, rows), dqacc[0], dqacc[1]) * 0.125
    R.dproj[:, 384:512] = dq.astype(BF)
    R.dproj[:, 512:576] = (dqacc[2][:, 0:64] * 0.125).astype(BF)
    to_beside(nz - 1).wait_recv()
    acc[...] += R.dkv.xin[at.z].astype(F32)

    def add(i, carry):
        zz = at.turn(nz - 2 - i)
        from_sender(zz).wait_recv()
        acc[...] += R.dkv.zin[zz].astype(F32)
        return carry
    lax.fori_loop(0, nz - 1, add, 0)
    R.dproj[:, 0:384] = acc[...].astype(BF)
    if l > 0:
        pl.semaphore_signal(R.dkv.free, inc=1, device_id=at.beside, device_id_type=MESH)

        def free(i, carry):
            pl.semaphore_signal(R.dkv.free, inc=1, device_id=at.column(at.turn(i)), device_id_type=MESH)
            return carry
        lax.fori_loop(0, nz - 1, free, 0)

    def drain(i, carry):
        to_beside(i).wait_send()

        @pl.when(i < nz - 1)
        def _():
            to_owner(i).wait_send()
        return carry
    lax.fori_loop(max(0, nz - slots), nz, drain, 0)
    if nz > slots:
        to_owner(nz - 1 - slots).wait_send()


def bwd_kernel(nb, layers, host, R):
    at = Place(nb)
    rows = R.kvbuf.shape[1]
    half_rows = rows // 2
    quarter = R.hid.shape[1]

    mixed, yr, xr, gu_w, down_w = range(5)
    streams = ((R.mixed, R.mixed_now), (R.yr, R.yr_now), (R.xr, R.xr_now), (R.gu_w, R.gu_now), (R.down_w, R.down_now))

    def load(which, l):
        return pltpu.make_async_copy(streams[which][0][l], streams[which][1], R.load.at[which])

    for which in range(5):
        load(which, layers - 1).start()
    at.enter()

    gather_df = HeadGather(at, R.df, R.df_send, R.df_recv)
    gather_da = HeadGather(at, R.da, R.da_send, R.da_recv)
    part = R.part
    head_sum = HeadSum(at, part, R.hs_stage, R.hs_in, R.hs_send, R.hs_recv)

    if host:
        ff_sum, at_sum, ow_sum = [[BlockSum(at, item) for item in items] for items in (R.ff, R.at, R.ow)]

    def small(l, t):
        return R.small[8 * l + t : 8 * l + t + 1, :]

    def put_small(l, t, value):
        R.tok_small[8 * l + t : 8 * l + t + 1, :] = value

    def of(buf, half):
        v = buf[pl.ds(2 * half, 2)]
        return v.reshape(half_rows, v.shape[2])

    def half_at(half):
        return pl.ds(pl.multiple_of(half * half_rows, half_rows), half_rows)

    def wgrad(left, right, stage, lo):
        step = stage.shape[1]
        for first in range(0, left.shape[1], 384):
            for col in range(0, right.shape[1], 768):
                width = min(768, right.shape[1] - col)
                v = dot(left[:, first : first + 384], right[:, col : col + width], TN)
                for i in range(384 // step):
                    stage[first // step + i, :, lo + col : lo + col + width] = v[step * i : step * i + step].astype(BF)

    def emit_ff(l):
        def emit(v):
            R.gu_sum[l][...] = v[:, : 2 * quarter].astype(BF)
            R.down_sum[l][...] = v[:, 2 * quarter :]
        ff_sum[l].total(emit)

    def emit_at(l):
        def emit(v):
            R.qkv_sum[l][...] = v.astype(BF)

        def emit_out(v):
            R.out_sum[l][...] = v
        at_sum[l].total(emit)
        ow_sum[l].total(emit_out)

    R.g[...] = R.grad[...].astype(F32)
    for l in reversed(range(layers)):
        top = l == layers - 1
        relay_before = host and not top
        e2, d_gain, d_shift = norm_back(R.g[...], R.sum2[l][...], small(l, 1))
        put_small(l, 1, d_gain)
        put_small(l, 5, d_shift)
        low = e2.astype(BF)
        put_small(l, 4, jnp.sum(low.astype(F32), axis=0, keepdims=True))
        if not top:
            head_sum.finish()
        R.df[at.head] = low
        gather_df.start()
        R.e2[...] = e2
        for which in range(5):
            load(which, l).wait()
        if relay_before:
            ff_sum[l + 1].relay_one(at.turn(0))
        gather_df.wait_near()
        for number, half in enumerate((at.y, 1 - at.y)):
            if number == 1:
                gather_df.wait_far()
                if relay_before:
                    ff_sum[l + 1].relay_one(at.turn(1))
            here = half_at(half)
            df_half = of(R.df, half)
            for col in range(0, quarter, 256):
                dhid = dot(df_half, R.down_now[col : col + 256, :], NT)
                gate = R.mixed_now[here, col : col + 256]
                up = R.mixed_now[here, quarter + col : quarter + col + 256]
                cdf = normal_cdf(gate)
                act = gate * cdf
                R.hid[here, col : col + 256] = (act * up).astype(BF)
                R.dgu[here, col : col + 256] = (dhid * up * (cdf + gate * normal_pdf(gate))).astype(BF)
                R.dgu[here, quarter + col : quarter + col + 256] = (dhid * act).astype(BF)
            dy = dot(R.dgu[here, :], R.gu_now[...], NT)
            part[pl.ds(2 * half, 2)] = dy.reshape(2, half_rows // 2, dy.shape[1])
            if number == 0:
                head_sum.send_near()
            else:
                head_sum.send_cross()
        ff_stage = R.ff[l].stage
        wgrad(R.hid, R.df[...].reshape(rows, -1), ff_stage, 2 * quarter)
        head_sum.relay()
        if relay_before:
            def rest(i, carry):
                ff_sum[l + 1].relay_one(at.turn(i))
                return carry
            lax.fori_loop(2, at.nz - 1, rest, 0)
        dy = R.e2[...] + head_sum.total()
        e1, d_gain, d_shift = norm_back(dy, R.sum1[l][...], small(l, 0))
        put_small(l, 0, d_gain)
        put_small(l, 3, d_shift)
        low = e1.astype(BF)
        put_small(l, 2, jnp.sum(low.astype(F32), axis=0, keepdims=True))
        R.da[at.head] = low
        gather_da.start()
        R.e1[...] = e1
        wgrad(R.yr_now, R.dgu, ff_stage, 0)
        gather_da.wait_near()
        gather_da.wait_far()
        if l > 0:
            for which in (mixed, yr, gu_w, down_w):
                load(which, l - 1).start()
        da_all = R.da[...].reshape(rows, -1)
        dctx = dot(da_all, R.out_w[l][...], NT).astype(BF)
        d_out = dot(R.ctx[l][...], da_all, TN)
        if host:
            step = d_out.shape[0] // nb
            for b in range(nb):
                R.ow[l].stage[b] = jnp.concatenate(
                    [d_out[step * b : step * b + step], jnp.zeros((OW_ROWS - step, d_out.shape[1]), F32)]).astype(BF)
        else:
            R.ow[l].stage[...] = d_out.astype(BF)
        ctxf = R.ctxf[l]
        wide = dctx.astype(F32)
        first_two = wide[:, :128]
        third = jnp.concatenate([jnp.zeros((rows, 64), F32), wide[:, 128:192]], axis=1)
        prod = first_two * ctxf[:, :128]
        low_half = in_half(0, rows)
        deltas = [
            jnp.sum(jnp.where(low_half, prod, 0.0), axis=1, keepdims=True),
            jnp.sum(jnp.where(low_half, 0.0, prod), axis=1, keepdims=True),
            jnp.sum(wide[:, 128:192] * ctxf[:, 128:192], axis=1, keepdims=True),
        ]
        for h in range(3):
            half = V_AT[h][1]
            base = jnp.where(in_half(half, rows), first_two if h < 2 else third, 0.0)
            R.do[h] = with_lanes(base, 0 if half else 64, split3(-deltas[h])).astype(BF)

        def ff_start(l=l):
            if host:
                ff_sum[l].start()

        def after_first(l=l, relay_before=relay_before):
            if relay_before:
                at_sum[l + 1].relay()
                ow_sum[l + 1].relay()
        attn_back(at, R, l, None, top, ff_start, after_first)
        dproj = R.dproj
        R.bias_sum[l : l + 1, :] = jnp.sum(dproj[...].astype(F32), axis=0, keepdims=True)
        gather_df.finish()
        gather_da.finish()
        head_sum.finish()
        for number, half in enumerate((1 - at.y, at.y)):
            dx = dot(dproj[half_at(half), :], R.qkv_w[l][...], NT)
            part[pl.ds(2 * half, 2)] = dx.reshape(2, half_rows // 2, dx.shape[1])
            if number == 0:
                head_sum.send_cross()
            else:
                head_sum.send_near()
        head_sum.relay()
        wgrad(R.xr_now, dproj, R.at[l].stage, 0)
        if host:
            at_sum[l].start()
            ow_sum[l].start()
        if l > 0:
            load(xr, l - 1).start()
        if relay_before:
            emit_ff(l + 1)
            emit_at(l + 1)
        R.g[...] = R.e1[...] + head_sum.total()
    R.grad_in[...] = R.g[...]
    head_sum.finish()
    if host:
        ff_sum[0].relay()
        at_sum[0].relay()
        ow_sum[0].relay()
        emit_ff(0)
        emit_at(0)
        for l in range(layers):
            ff_sum[l].finish()
            at_sum[l].finish()
            ow_sum[l].finish()


def block_sum_item(nb, *dims):
    nz = nb // 2
    return dict(stage=keep(nb, *dims), xin=keep(nz, *dims), zin=keep(nz, *dims),
                xsend=copies(nz), xrecv=copies(nz), zsend=copies(nz), zrecv=copies(nz))


def bwd(grad, small, kaug, saved, host):
    layers = len(saved.qkv_w)
    nb, rows = kaug.shape[:2]
    nz = nb // 2
    tokens, width = grad.shape
    group3 = saved.qkv_w[0].shape[1]
    quarter = saved.down_w[0].shape[0]
    r = width // nb
    ff_width = 2 * quarter + width
    each = range(layers)
    slots = min(nz, 4)
    out = dict(grad_in=shape(tokens, width, dtype=F32), tok_small=shape(8 * layers, width, dtype=F32),
               bias_sum=shape(layers, group3, dtype=F32))
    scratch = {}
    if host:
        out.update(
            gu_sum=[shape(r, 2 * quarter) for _ in each], down_sum=[shape(r, width, dtype=F32) for _ in each],
            qkv_sum=[shape(r, group3) for _ in each], out_sum=[shape(OW_ROWS, width, dtype=F32) for _ in each])
        scratch.update(
            ff=[block_sum_item(nb, r, ff_width) for _ in each], at=[block_sum_item(nb, r, group3) for _ in each],
            ow=[block_sum_item(nb, OW_ROWS, width) for _ in each])
    else:
        out.update(
            ff=[dict(stage=shape(nb, r, ff_width)) for _ in each], at=[dict(stage=shape(nb, r, group3)) for _ in each],
            ow=[dict(stage=shape(group3 // 3, width)) for _ in each])
    like = lambda arrays: keep(*arrays[0].shape, dtype=arrays[0].dtype)
    scratch.update(
        mixed_now=like(saved.mixed), yr_now=like(saved.yr), xr_now=like(saved.xr), gu_now=like(saved.gu_w),
        down_now=like(saved.down_w), load=copies(5), kvbuf=keep(2, rows, 384), kvsem=copies(2),
        df=keep(4, tokens, width), df_send=copies(3), df_recv=copies(3),
        da=keep(4, tokens, width), da_send=copies(3), da_recv=copies(3),
        part=keep(4, tokens, width, dtype=F32),
        hs_stage=keep(3, tokens, width), hs_in=keep(3, tokens, width), hs_send=copies(3), hs_recv=copies(3),
        g=keep(tokens, width, dtype=F32), e1=keep(tokens, width, dtype=F32), e2=keep(tokens, width, dtype=F32),
        hid=keep(rows, quarter), dgu=keep(rows, 2 * quarter), do=keep(3, rows, 128),
        dqacc=keep(3, rows, 128, dtype=F32), dkv_acc=keep(rows, 384, dtype=F32), dproj=keep(rows, group3),
        dkv=dict(stage=keep(slots, 2, rows, 384), xin=keep(nz, rows, 384), zin=keep(nz, rows, 384), xsend=copies(nz),
                 xrecv=copies(nz), zsend=copies(nz), zrecv=copies(nz), free=pltpu.SemaphoreType.REGULAR))
    near = dict(grad=grad, small=small, kaug=kaug, sum1=saved.sum1, sum2=saved.sum2, ctx=saved.ctx, ctxf=saved.ctxf,
                qb=saved.qb, out_w=saved.out_w, qkv_w=saved.qkv_w)
    far = dict(mixed=saved.mixed, yr=saved.yr, xr=saved.xr, gu_w=saved.gu_w, down_w=saved.down_w, kv=saved.kv)
    return call(functools.partial(bwd_kernel, nb, layers, host), "backward", 1, near=near, far=far, out=out, scratch=scratch)


def three(value):
    high = lax.reduce_precision(value, 8, 7)
    rest = value - high
    mid = lax.reduce_precision(rest, 8, 7)
    return [part.astype(BF) for part in (high, mid, rest - mid)]


def shards(hidden_in, out_grad, segment_ids, alibi_slopes, qkv_weight, out_weight, gate_up_weight, down_weight, gains, biases):
    nh, nb = lax.axis_size("head"), lax.axis_size("blk")
    head, blk = lax.axis_index("head"), lax.axis_index("blk")
    token_rows, width = hidden_in.shape
    rows = token_rows * nh
    layers, wrows = qkv_weight.shape[:2]
    ff = gate_up_weight.shape[2] // 2
    ffd = down_weight.shape[1]
    group = width // nh
    quarter = ff // nh
    tokens = segment_ids.shape[0]
    qk = 3 * group
    host = (width // nb) % 16 == 0

    def to_groups(w):
        w = w.reshape(layers, wrows, 3, nh, 3, 64)
        q, k, v = w[:, :, 0], w[:, :, 1], w[:, :, 2]
        kv = jnp.stack([k[..., 0, :], k[..., 1, :], v[..., 0, :], v[..., 1, :], k[..., 2, :], v[..., 2, :]], axis=3)
        return jnp.concatenate([kv, q], axis=3).reshape(layers, wrows, nh, qk)

    def from_groups(g):
        g = g.reshape(layers, nh, wrows, 9, 64)
        pick = lambda *index: jnp.stack([g[:, :, :, i] for i in index], axis=3)
        all3 = jnp.stack([pick(6, 7, 8), pick(0, 1, 4), pick(2, 3, 5)], axis=1)
        return all3.transpose(0, 3, 1, 2, 4, 5).reshape(layers, wrows, 3 * width)

    small = jnp.concatenate([gains, biases], axis=1).transpose(0, 2, 1)
    small = jnp.concatenate([small[l] for l in range(layers)], axis=1)
    small = jnp.pad(small, ((0, 0), (0, 64 - small.shape[1])))
    small = jnp.broadcast_to(small[:, None], (wrows, nh, 64))
    gu_cols = gate_up_weight.reshape(layers, wrows, 2, nb, nh, ffd).transpose(0, 1, 4, 2, 3, 5).reshape(layers, wrows, nh, 2 * quarter)
    qkv_cols = to_groups(qkv_weight)
    pieces = [qkv_cols[0], small] + [qkv_cols[l] for l in range(1, layers)] + [gu_cols[l] for l in range(layers)]
    spread = lax.all_to_all(jnp.concatenate(pieces, axis=2), "head", split_axis=1, concat_axis=0, tiled=True)
    spread = spread.reshape(nh * wrows, -1)
    qkv0 = spread[:, : qk + 64]
    qkv_own = [qkv0] + [spread[:, qk * l + 64 : qk * l + qk + 64] for l in range(1, layers)]
    gu0 = qk * layers + 64
    gu_own = [spread[:, gu0 + 2 * quarter * l : gu0 + 2 * quarter * (l + 1)] for l in range(layers)]
    moves = [(b * nh + h, h * nb + b) for b in range(nb) for h in range(nh)]
    ow_own = lax.ppermute(out_weight, ("blk", "head"), [(target, source) for source, target in moves])
    if host:
        weights = types.SimpleNamespace(qkv_own=qkv_own, gu_own=gu_own, down_own=[down_weight[l] for l in range(layers)],
                                        ow_own=ow_own.reshape(layers * wrows, width))
    else:
        whole = lambda v: lax.all_gather(v, "blk", axis=0, tiled=True)
        qkv_all = [whole(v) for v in qkv_own]
        out_all = lax.all_gather(ow_own, "blk", axis=1, tiled=True)
        weights = types.SimpleNamespace(
            qkv_given=[v[:, :qk] for v in qkv_all], gu_given=[whole(v) for v in gu_own],
            down_given=[whole(down_weight[l]) for l in range(layers)], out_given=[out_all[l] for l in range(layers)],
            small_given=qkv_all[0][:, qk : qk + 8 * layers].astype(F32).T)

    slopes = lax.dynamic_slice_in_dim(alibi_slopes, head * 3, 3, 0)
    position = jnp.arange(tokens, dtype=jnp.int32).astype(F32)
    same = (segment_ids[:, None] == jnp.arange(5, dtype=jnp.int32)[None, :])
    apart = [jnp.where(same[:, s], 0.0, -1e30).astype(BF) for s in range(5)]
    one = jnp.ones((tokens,), BF)
    columns = [part for h in range(3) for part in three(slopes[h] * position)] + [one] * 3 + apart
    columns = jnp.pad(jnp.stack(columns, axis=-1), ((0, 0), (0, 64 - len(columns))))
    kaug = jnp.concatenate([columns, columns], axis=1).reshape(nb, rows, 128)
    inside = lax.dynamic_slice_in_dim(same, blk * rows, rows, 0).astype(BF)
    qaug = []
    for sign in (1.0, -1.0):
        for h in range(3):
            ones = [jnp.full((rows,), sign if i // 3 == h else 0.0, BF) for i in range(9)]
            a = jnp.concatenate([jnp.stack(ones, axis=-1), jnp.zeros((rows, 3), BF), inside, jnp.zeros((rows, 47), BF)], axis=1)
            qaug.append(jnp.concatenate([a, a], axis=1))
    qaug = jnp.stack(qaug).reshape(2, 3, rows, 128)

    saved = fwd(hidden_in, slopes, qaug, kaug, weights, layers, host)
    done = bwd(out_grad, saved.small, kaug, saved, host)
    if not host:
        done.gu_sum, done.down_sum, done.qkv_sum, done.out_sum = [], [], [], []
        for l in range(layers):
            ff_sum, at_sum, ow_sum = [
                lax.psum_scatter(items[l].stage.reshape(width, -1), "blk", scatter_dimension=0, tiled=True)
                for items in (done.ff, done.at, done.ow)]
            done.gu_sum.append(ff_sum[:, : 2 * quarter])
            done.down_sum.append(ff_sum[:, 2 * quarter :])
            done.qkv_sum.append(at_sum)
            done.out_sum.append(ow_sum.reshape(wrows, width))

    tok_small = done.tok_small.reshape(layers, 8, width)
    bias_sum = done.bias_sum
    rows_of = jnp.zeros((layers, 2, width), F32)
    dqb = bias_sum[:, 384:]
    dvb = jnp.concatenate([bias_sum[:, 128:256], bias_sum[:, 320:384]], axis=1)
    rows_of = lax.dynamic_update_slice_in_dim(rows_of, jnp.stack([dqb, dvb], axis=1), head * group, 2)
    small_g = jnp.concatenate([tok_small[:, :6], rows_of], axis=1)
    small_g = small_g.reshape(layers * 8, nb * nh, wrows).transpose(1, 0, 2).reshape(nb * nh, layers * 8 * wrows)
    small_sum = lax.psum_scatter(small_g, ("blk", "head"), scatter_dimension=0, tiled=True).reshape(layers, 8, wrows)
    gains_grad = small_sum[:, 0:2]
    biases_grad = jnp.concatenate([small_sum[:, 6:8], small_sum[:, 2:6]], axis=1)

    back = jnp.concatenate([jnp.stack(done.qkv_sum), jnp.stack(done.gu_sum)], axis=2).reshape(layers, nh, wrows, -1)
    back = lax.all_to_all(back, "head", split_axis=1, concat_axis=1, tiled=True).astype(F32)
    qkv_grad = from_groups(back[..., :qk])
    gu_grad = back[..., qk:].reshape(layers, nh, wrows, 2, nb, ffd).transpose(0, 2, 3, 4, 1, 5).reshape(layers, wrows, 2 * ff)
    out_grad_w = lax.ppermute(jnp.stack(done.out_sum)[:, :wrows], ("blk", "head"), moves).astype(F32)
    return saved.output, done.grad_in, qkv_grad, out_grad_w, gu_grad, jnp.stack(done.down_sum).astype(F32), gains_grad, biases_grad


def solution(mesh):
    both = ("blk", "head")
    tok, mid, last = P(both, None), P(None, both, None), P(None, None, both)
    return jax.shard_map(
        shards, mesh=mesh,
        in_specs=(tok, tok, P(), P(), mid, mid, mid, mid, last, last),
        out_specs=(tok, tok, mid, mid, mid, mid, last, last),
        check_vma=False,
    )
```

time: 865 us -> 585 us (0.68)
  Pallas kernels: 225 us -> 466 us
  waiting for transfers between devices: 180 us -> 0.01 us
  blocking collectives: 202 us -> 40.5 us
  other arithmetic: 51.1 us -> 7.43 us
  matrix products: 43 us -> 0 us
  local copies, waits for them, and re-layouts: 80 us -> 41.9 us
  starting transfers between devices: 52.8 us -> 17 us
  between operations: 19 us -> 1.71 us
    pallas_call x4 -> x2, Pallas kernels: 225 us -> 466 us  [call(): pl.pallas_call(kernel, out_shape=tuple(flat[3]) + tuple(flat[4]), in_spec...]
    reduce_scatter x4 -> x0, waiting for transfers between devices: 155 us -> none  [the longest x2 155 us: shards(): lax.psum_scatter(jnp.concatenate([d_gu, d_down], axis=1), 'blk', scatter_...]
    all_gather x10 -> x0, blocking collectives: 145 us -> none  [the longest x8 78 us: spread_rows(): return lax.all_gather(v, 'head', axis=0, tiled=True)]
    dot_general x24 -> x0, matrix products: 43 us -> none  [mm(): return lax.dot_general(a, b, dims, preferred_element_type=F32)]
    all_to_all x8 -> x1, starting transfers between devices: 42.1 us -> 4.29 us  [shards(): lax.all_to_all(jnp.concatenate(pieces, axis=2), 'head', split_axis=1, con...]
    another operation x76 -> x16, local copies, waits for them, and re-layouts: 19.9 us -> 1.38 us  [the longest x2 0.67 us: shards(): jnp.stack([dqb, dvb], axis=1)]
    all_to_all x8 -> x1, waiting for transfers between devices: 17.5 us -> 0.01 us  [shards(): lax.all_to_all(jnp.concatenate(pieces, axis=2), 'head', split_axis=1, con...]
    all_to_all x1 -> x0, blocking collectives: 14.2 us -> none  [shards(): lax.all_to_all(jnp.concatenate([qkv_cols, small, gu_cols], axis=3), 'head...]
  transfers between devices with their start and end apart: 19 -> 4, of which waited for: 8 -> 0; matrix products, arithmetic and copies ran while one was open for 16% -> 4% of each run, Pallas kernels for 19% -> 0%
where the time goes in v2:
time: 585 us; the launch traced here: 575 us
  Pallas kernels  466 us (80%)
  local copies, waits for them, and re-layouts  41.9 us (7%)
  blocking collectives  40.5 us (7%)
  starting transfers between devices  17 us (3%)
  other arithmetic  7.43 us (1%)
    pallas_call x2, Pallas kernels, call(): pl.pallas_call(kernel, out_shape=tuple(flat[3]) + tuple(flat[4]), in_spec...  466 us
    unnamed x1, blocking collectives  40.5 us
    concatenate x6, local copies, waits for them, and re-layouts, shards(): qaug.append(jnp.concatenate([a, a], axis=1))  12.2 us
  transfers between devices with their start and end apart: 4, of which 0 were waited for; matrix products, arithmetic and copies ran while one was open for 4% of the time, Pallas kernels for 0%

profile of v2, /device:TPU:21, one launch (start us, length us, event | category | flops | bytes accessed | tf_op | source)
XLA Modules:
  0.0 575.0 jit_solution(13453860390419244404)
XLA Ops:
  0.6 1.7 reshape.191
  3.0 2.2 concatenate.58
  8.3 1.4 concatenate.61
  9.7 4.3 all-to-all-start
  14.0 3.2 collective-permute-start
  18.6 1.4 fusion
  21.4 0.8 fusion.7
  22.6 1.0 concatenate.63
  24.4 4.4 concatenate.64
  29.7 4.4 concatenate.67
  35.5 1.3 copy.56
  37.0 0.8 slice_bitcast_fusion.4
  37.8 1.1 fusion.10
  40.8 205.2 %forward.1 = (bf16[128,768]{1,0:T(8,128)(2,1)}, f32[16,768]{1,0:T(8,128)}, bf16[512,192]{1,0:T(8,128)(2,1)}, bf16[512,192]{1,0:T(8,128)(2,1)}, f32[512,192]{1,0:...) custom-call(bf16[96,768]{1,0:T(8,128)(2,1)} %get-tuple-element.124.r, ...), custom_call_target="tpu_custom_call" | custom-call | flops 99999997952 | bytes 200000000 | tf_op jit(solution)/shard_map/forward/pallas_call | solution.py:245
  246.1 261.2 %backward.1 = (f32[2,576]{1,0:T(2,128)}, f32[96,768]{1,0:T(8,128)}, f32[96,768]{1,0:T(8,128)}, f32[128,768]{1,0:T(8,128)}, bf16[96,1536]{1,0:T(8,128)(2,1)}, /*i...) custom-call(bf16[512,192]{1,0:T(8,128)(2,1)} %get-tuple-element.48.r, ...), custom_call_target="tpu_custom_call" | custom-call | flops 99999997952 | bytes 200000000 | tf_op jit(solution)/shard_map/backward/pallas_call | solution.py:245
  509.4 1.4 maximum_maximum_fusion
  510.8 1.0 copy.69
  511.7 4.9 all-to-all-start.1
  516.6 4.6 collective-permute-start.1
  522.3 40.5 %all-reduce.2 = f32[32,384]{1,0:T(8,128)S(1)} all-reduce(f32[32,384]{1,0:T(8,128)S(1)} %reshape.214), channel_id=2, replica_groups=mesh['blk'=8,'head'=4] {'blk','head'}, use_global_device_ids=true, to_apply=%region_0.1.clone | all-reduce | flops 12288 | bytes 98304
  564.1 0.9 pad_maximum_fusion.1
  566.8 1.4 reshape.209
  569.0 1.0 copy.72
  570.0 2.6 reshape.211
  (128 shorter events, 20.7 us)
Async XLA Ops:
  2.9 2.6 copy-start.12
  3.0 2.6 copy-start.13
  5.1 1.1 copy-start
  8.3 5.7 copy-start.14
  8.3 8.9 %copy-start.16 = (f32[12]{0:T(128)S(1)}, f32[12]{0:T(128)}, u32[]{:S(2)}) copy-start(f32[12]{0:T(128)} %param.13) | copy-start | bytes 148
  8.3 13.0 %copy-start.10 = (s32[4096]{0:T(1024)S(1)}, s32[4096]{0:T(1024)}, u32[]{:S(2)}) copy-start(s32[4096]{0:T(1024)} %param.12) | copy-start | bytes 49156
  9.7 28.1 %all-to-all-start = ((bf16[24,4,4288]{2,0,1:T(8,128)(2,1)}), bf16[24,4,4288]{2,0,1:T(8,128)(2,1)S(1)}, u32[]{:S(2)}, u32[]{:S(2)}) async-start(bf16[24,4,4288]{2,0,1:T(8,128)(2,1)} %concatenate.61), calls=%async_computation | async-start | bytes 1671168 | tf_op jit(solution)/shard_map/all_to_all | solution.py:1121
  14.0 26.2 %collective-permute-start = (bf16[2,24,768]{2,1,0:T(8,128)(2,1)S(1)}, bf16[2,24,768]{2,1,0:T(8,128)(2,1)S(1)}, u32[]{:S(2)}, u32[]{:S(2)}) collective-permute-start(bf16[2,24,768]{2,1,0:T(8,128)(2,1)S(1)} %copy-done.14), channel_id=1, source_target_pairs={{0,0},{8,1},{16,2},{24,3},{1,4},{9,5},{17,6},{25,7},{2,8},{10,9},{... | collective-permute-start | bytes 221192 | tf_op jit(solution)/shard_map/ppermute | solution.py:1128
  17.4 6.2 %copy-start.11 = (f32[3]{0:T(128)}, f32[3]{0:T(128)S(1)}, u32[]{:S(2)}) copy-start(f32[3]{0:T(128)S(1)} %dynamic_slice.6.refs_10_) | copy-start | bytes 40
  35.5 1.5 copy-start.2
  37.0 3.2 copy-start.9
  40.2 0.6 copy-start.15
  510.8 5.8 %copy-start.6 = (f32[32,768]{1,0:T(8,128)S(1)}, f32[32,768]{1,0:T(8,128)}, u32[]{:S(2)}) copy-start(f32[32,768]{1,0:T(8,128)} %get-tuple-element.80) | copy-start | bytes 294916
  510.8 5.8 %copy-start.7 = (f32[32,768]{1,0:T(8,128)S(1)}, f32[32,768]{1,0:T(8,128)}, u32[]{:S(2)}) copy-start(f32[32,768]{1,0:T(8,128)} %get-tuple-element.81) | copy-start | bytes 294916
  510.8 11.0 %copy-start.8 = (f32[16,768]{1,0:T(8,128)S(1)}, f32[16,768]{1,0:T(8,128)}, u32[]{:S(2)}) copy-start(f32[16,768]{1,0:T(8,128)} %get-tuple-element.84) | copy-start | bytes 147460
  511.7 52.4 %copy-start.3 = (f32[96,768]{1,0:T(8,128)S(1)}, f32[96,768]{1,0:T(8,128)}, u32[]{:S(2)}) copy-start(f32[96,768]{1,0:T(8,128)} %get-tuple-element.82) | copy-start | bytes 884740
  511.7 52.4 %copy-start.4 = (f32[96,768]{1,0:T(8,128)S(1)}, f32[96,768]{1,0:T(8,128)}, u32[]{:S(2)}) copy-start(f32[96,768]{1,0:T(8,128)} %get-tuple-element.83) | copy-start | bytes 884740
  511.7 53.3 %all-to-all-start.1 = ((bf16[2,4,24,2112]{3,2,0,1:T(8,128)(2,1)}), bf16[2,4,24,2112]{3,2,0,1:T(8,128)(2,1)S(1)}, u32[]{:S(2)}, u32[]{:S(2)}) async-start(bf16[2,4,24,2112]{3,2,0,1:T(8,128)(2,1)} %copy.69), calls=%async_computation.1 | async-start | bytes 1671168 | tf_op jit(solution)/shard_map/all_to_all | solution.py:1184
  516.6 48.4 %collective-permute-start.1 = (f32[2,24,768]{2,1,0:T(8,128)S(1)}, f32[2,24,768]{2,1,0:T(8,128)S(1)}, u32[]{:S(2)}, u32[]{:S(2)}) collective-permute-start(f32[2,24,768]{2,1,0:T(8,128)S(1)} %pad_maximum_fusion.2), channel_id=1, source_target_pairs={{0,0},{1,8},{2,16},{3,24},{4,1},{5,9},{6,17},{7,25},{8,2},{9,10},{... | collective-permute-start | bytes 442376 | tf_op jit(solution)/shard_map/ppermute | solution.py:1187
  570.0 2.7 copy-start.5
  570.0 3.3 copy-start.1

commit v3 on v2

v3 whole, which is shorter than its diff:
```python
import functools
import types

import jax
import jax.numpy as jnp
from jax import lax
from jax.experimental import pallas as pl
from jax.experimental.pallas import tpu as pltpu
from jax.sharding import Mesh
from jax.sharding import PartitionSpec as P

MESH = pl.DeviceIdType.MESH
BF = jnp.bfloat16
F32 = jnp.float32
NT = (((1,), (1,)), ((), ()))
NN = (((1,), (0,)), ((), ()))
TN = (((0,), (0,)), ((), ()))
EPS = 1e-06
K_AT = ((0, 0), (0, 1), (2, 0))
V_AT = ((1, 0), (1, 1), (2, 1))
ROW_LANE, SEGMENT_LANE = 9, 12
OW_ROWS = 32
VMEM = pl.BlockSpec(memory_space=pltpu.VMEM)
ANY = pl.BlockSpec(memory_space=pl.ANY)


def dot(a, b, dims=NN):
    return lax.dot_general(a, b, dims, preferred_element_type=F32)


def lanes(rows):
    return lax.broadcasted_iota(jnp.int32, (rows, 128), 1)


def in_half(half, rows):
    return lanes(rows) >= 64 if half else lanes(rows) < 64


def ones_half(half, rows):
    first = 0 if half else 64
    lane = lanes(rows)
    return jnp.where((lane >= first) & (lane < first + 3), 1.0, 0.0).astype(BF)


def k_operand(kv, aug, h):
    col, half = K_AT[h]
    return jnp.where(in_half(half, kv.shape[0]), kv[:, 128 * col : 128 * col + 128], aug)


def v_operand(kv, h):
    col, half = V_AT[h]
    rows = kv.shape[0]
    return jnp.where(in_half(half, rows), kv[:, 128 * col : 128 * col + 128], ones_half(half, rows))


def split3(value):
    high = value.astype(BF).astype(F32)
    mid = (value - high).astype(BF).astype(F32)
    return high, mid, value - high - mid


def with_lanes(base, first, values):
    lane = lanes(base.shape[0])
    for i, v in enumerate(values):
        base = jnp.where(lane == first + i, v, base)
    return base


def layer_norm(total, gain, shift):
    centred = total - jnp.mean(total, axis=-1, keepdims=True)
    scale = lax.rsqrt(jnp.mean(centred * centred, axis=-1, keepdims=True) + EPS)
    return centred * scale * gain + shift


def norm_back(grad, total, gain):
    centred = total - jnp.mean(total, axis=-1, keepdims=True)
    scale = lax.rsqrt(jnp.mean(centred * centred, axis=-1, keepdims=True) + EPS)
    n = centred * scale
    dn = grad * gain
    e = scale * (dn - jnp.mean(dn, axis=-1, keepdims=True) - n * jnp.mean(dn * n, axis=-1, keepdims=True))
    return e, jnp.sum(grad * n, axis=0, keepdims=True), jnp.sum(grad, axis=0, keepdims=True)


def normal_cdf(u):
    return 0.5 * (1.0 + lax.erf(u * (0.5**0.5)))


def normal_pdf(u):
    return jnp.exp(-0.5 * u * u) * ((2.0 * jnp.pi) ** -0.5)


def remote(src, dst, send, recv, device):
    return pltpu.make_async_remote_copy(
        src_ref=src, dst_ref=dst, send_sem=send, recv_sem=recv, device_id=device, device_id_type=MESH)


def loop(first, last, do):
    def step(i, carry):
        do(i)
        return carry
    lax.fori_loop(first, last, step, 0)


class Place:
    def __init__(self, nz):
        self.nz = nz
        self.z, self.x, self.y, self.c = [lax.axis_index(name) for name in "zxyc"]
        self.g = 2 * self.x + self.y
        self.gx, self.gy = 2 * (1 - self.x) + self.y, 2 * self.x + 1 - self.y
        self.gd = 2 * (1 - self.x) + 1 - self.y
        self.oc = 1 - self.c
        self.beside = (self.z, self.x, self.y, self.oc)
        self.across_x = (self.z, 1 - self.x, self.y, self.c)
        self.across_y = (self.z, self.x, 1 - self.y, self.c)
        self.block = 2 * self.z + self.c
        self.has_left, self.has_right = self.z > 0, self.z < nz - 1

    def column(self, zz):
        return (zz, self.x, self.y, self.c)

    def neighbours(self):
        return 3 - (self.z == 0).astype(jnp.int32) - (self.z == self.nz - 1).astype(jnp.int32)

    def signal_neighbours(self, semaphore):
        pl.semaphore_signal(semaphore, inc=1, device_id=self.beside, device_id_type=MESH)

        @pl.when(self.has_left)
        def _():
            pl.semaphore_signal(semaphore, inc=1, device_id=self.column(self.z - 1), device_id_type=MESH)

        @pl.when(self.has_right)
        def _():
            pl.semaphore_signal(semaphore, inc=1, device_id=self.column(self.z + 1), device_id_type=MESH)

    def enter(self):
        barrier = pltpu.get_barrier_semaphore()
        for device in (self.across_x, self.across_y):
            pl.semaphore_signal(barrier, inc=1, device_id=device, device_id_type=MESH)
        self.signal_neighbours(barrier)
        pl.semaphore_wait(barrier, 2 + self.neighbours())

    def positions(self, zz, cc, tokens, rows):
        row = lax.broadcasted_iota(jnp.int32, (rows, 128), 0)
        return ((zz * 8 + (row // tokens) * 2 + cc) * tokens + row % tokens).astype(F32)


class SquareGather:
    def __init__(self, at, buf, send, recv):
        half = buf.shape[1] // 2
        first, second = pl.ds(0, half), pl.ds(half, half)
        own = buf.at[at.g]
        self.to_x = remote(own, own, send.at[0], recv.at[0], at.across_x)
        self.to_y = remote(own, own, send.at[1], recv.at[1], at.across_y)
        self.on_y = remote(buf.at[at.gx, first], buf.at[at.gx, first], send.at[2], recv.at[2], at.across_y)
        self.on_x = remote(buf.at[at.gy, second], buf.at[at.gy, second], send.at[3], recv.at[3], at.across_x)

    def start(self):
        self.to_x.start()
        self.to_y.start()

    def wait_near(self):
        self.to_x.wait_recv()
        self.on_y.start()
        self.to_y.wait_recv()
        self.on_x.start()

    def wait_far(self):
        self.on_x.wait_recv()
        self.on_y.wait_recv()

    def finish(self):
        for copy in (self.to_x, self.to_y, self.on_x, self.on_y):
            copy.wait_send()


class SquareSum:
    def __init__(self, at, part, pair, single, send, recv):
        self.at, self.part = at, part
        self.pair, self.single = pair, single
        self.half = part.shape[2] // 2
        to = (at.across_x, at.across_y, at.across_y, at.across_y, at.across_x)
        refs = [(pair.stage, pair.inbox)] + [(single.stage.at[i], single.inbox.at[i]) for i in range(4)]
        self.copies = [remote(refs[i][0], refs[i][1], send.at[i], recv.at[i], to[i]) for i in range(5)]

    def left(self, g):
        return self.part[g, :, : self.half]

    def right(self, g):
        return self.part[g, :, self.half :]

    def send_far(self):
        at = self.at
        self.pair.stage[...] = self.part[pl.ds(2 * (1 - at.x), 2), :, : self.half].astype(BF)
        self.copies[0].start()
        self.single.stage[1] = self.right(at.gd).astype(BF)
        self.copies[2].start()

    def send_near(self):
        self.single.stage[0] = self.right(self.at.gy).astype(BF)
        self.copies[1].start()

    def relay(self):
        at = self.at
        self.copies[0].wait_recv()
        self.single.stage[2] = (self.left(at.gy) + self.pair.inbox[1 - at.y].astype(F32)).astype(BF)
        self.copies[3].start()
        self.copies[2].wait_recv()
        self.single.stage[3] = (self.right(at.gx) + self.single.inbox[1].astype(F32)).astype(BF)
        self.copies[4].start()

    def total(self):
        at = self.at
        self.copies[1].wait_recv()
        left = self.left(at.g) + self.pair.inbox[at.y].astype(F32)
        right = self.right(at.g) + self.single.inbox[0].astype(F32)
        self.copies[3].wait_recv()
        self.copies[4].wait_recv()
        return jnp.concatenate(
            [left + self.single.inbox[2].astype(F32), right + self.single.inbox[3].astype(F32)], axis=1)

    def finish(self):
        for copy in self.copies:
            copy.wait_send()


class BlockGather:
    def __init__(self, at, item):
        self.at, self.buf, self.zsend, self.csend, self.recv = at, item.buf, item.zsend, item.csend, item.recv

    def copy(self, zz, send, device):
        at = self.at
        return remote(self.buf.at[zz, at.c], self.buf.at[zz, at.c], send, self.recv.at[zz, at.c], device)

    def to_right(self, zz):
        return self.copy(zz, self.zsend.at[0, zz], self.at.column(self.at.z + 1))

    def to_left(self, zz):
        return self.copy(zz, self.zsend.at[1, zz], self.at.column(self.at.z - 1))

    def to_beside(self, zz):
        return self.copy(zz, self.csend.at[zz], self.at.beside)

    def wait(self, zz, cc):
        at = self.at
        remote(self.buf.at[zz, cc], self.buf.at[zz, cc], self.csend.at[zz], self.recv.at[zz, cc], at.beside).wait_recv()

    def put(self, value):
        self.buf[self.at.z, self.at.c] = value

    def start(self):
        at = self.at

        @pl.when(at.has_right)
        def _():
            self.to_right(at.z).start()

        @pl.when(at.has_left)
        def _():
            self.to_left(at.z).start()
        self.to_beside(at.z).start()

    def serve(self, d):
        at = self.at

        @pl.when(at.z - d >= 0)
        def _():
            self.wait(at.z - d, at.c)

            @pl.when(at.has_right)
            def _():
                self.to_right(at.z - d).start()
            self.to_beside(at.z - d).start()

        @pl.when(at.z + d < at.nz)
        def _():
            self.wait(at.z + d, at.c)

            @pl.when(at.has_left)
            def _():
                self.to_left(at.z + d).start()
            self.to_beside(at.z + d).start()

    def serve_all(self):
        loop(1, self.at.nz, self.serve)

    def collect(self):
        loop(0, self.at.nz, lambda zz: self.wait(zz, self.at.oc))

    def finish(self):
        at = self.at

        def drain(zz):
            self.to_beside(zz).wait_send()

            @pl.when((zz <= at.z) & at.has_right)
            def _():
                self.to_right(zz).wait_send()

            @pl.when((zz >= at.z) & at.has_left)
            def _():
                self.to_left(zz).wait_send()
        loop(0, at.nz, drain)


def block_gather_item(nz, *dims):
    return dict(buf=keep(nz, 2, *dims), zsend=copies(2, nz), csend=copies(nz), recv=copies(nz, 2))


class BlockSum:
    def __init__(self, at, item):
        self.at, self.stage, self.cin, self.zin = at, item.stage, item.cin, item.zin
        self.csend, self.crecv, self.zsend, self.zrecv = item.csend, item.crecv, item.zsend, item.zrecv

    def to_beside(self, t):
        return remote(self.stage.at[t, self.at.oc], self.cin.at[t], self.csend.at[t], self.crecv.at[t], self.at.beside)

    def to_right(self, t):
        return remote(self.stage.at[t, self.at.c], self.zin.at[t + 1], self.zsend.at[t], self.zrecv.at[t + 1], self.at.column(self.at.z + 1))

    def to_left(self, t):
        return remote(self.stage.at[t, self.at.c], self.zin.at[t], self.zsend.at[t], self.zrecv.at[t], self.at.column(self.at.z - 1))

    def arrived(self, slot):
        at = self.at
        remote(self.zin.at[slot], self.zin.at[slot], self.zsend.at[0], self.zrecv.at[slot], at.beside).wait_recv()

    def start(self):
        loop(0, self.at.nz, lambda t: self.to_beside(t).start())

    def add(self, t, slot=None):
        value = self.stage[t, self.at.c].astype(F32) + self.cin[t].astype(F32)
        if slot is not None:
            value = value + self.zin[slot].astype(F32)
        self.stage[t, self.at.c] = value.astype(self.stage.dtype)

    def go_right(self, t):
        self.to_beside(t).wait_recv()

        @pl.when(self.at.has_left)
        def _():
            self.arrived(t + 1)
            self.add(t, t + 1)

        @pl.when(jnp.logical_not(self.at.has_left))
        def _():
            self.add(t)
        self.to_right(t).start()

    def go_left(self, t):
        self.to_beside(t).wait_recv()

        @pl.when(self.at.has_right)
        def _():
            self.arrived(t)
            self.add(t, t)

        @pl.when(jnp.logical_not(self.at.has_right))
        def _():
            self.add(t)
        self.to_left(t).start()

    def serve(self, p, source=True, relay=True):
        at = self.at
        right, left = p - at.z, p - (at.nz - 1 - at.z)
        go_r = (right >= 0) & (right < at.nz - 1 - at.z)
        go_l = (left >= 0) & (left < at.z)
        if not source:
            go_r, go_l = go_r & at.has_left, go_l & at.has_right
        if not relay:
            go_r, go_l = go_r & jnp.logical_not(at.has_left), go_l & jnp.logical_not(at.has_right)

        @pl.when(go_r)
        def _():
            self.go_right(at.nz - 1 - right)

        @pl.when(go_l)
        def _():
            self.go_left(left)

    def total(self):
        at = self.at
        self.to_beside(at.z).wait_recv()

        @pl.when(at.has_left)
        def _():
            self.arrived(at.z + 1)

        @pl.when(at.has_right)
        def _():
            self.arrived(at.z)
        value = self.stage[at.z, at.c].astype(F32) + self.cin[at.z].astype(F32)
        from_left = jnp.where(at.has_left, self.zin[at.z + 1].astype(F32), 0.0)
        from_right = jnp.where(at.has_right, self.zin[at.z].astype(F32), 0.0)
        return value + from_left + from_right

    def finish(self):
        at = self.at

        def drain(t):
            self.to_beside(t).wait_send()

            @pl.when(t > at.z)
            def _():
                self.to_right(t).wait_send()

            @pl.when(t < at.z)
            def _():
                self.to_left(t).wait_send()
        loop(0, at.nz, drain)


def box(tree):
    if isinstance(tree, dict):
        return types.SimpleNamespace(**{k: box(v) for k, v in tree.items()})
    return [box(v) for v in tree] if isinstance(tree, list) else tree


def call(body, name, collective_id, near=None, far=None, table=None, out=None, far_out=None, scratch=None):
    groups = [near or {}, far or {}, table or {}, out or {}, far_out or {}, scratch or {}]
    flat, trees = zip(*[jax.tree.flatten(g) for g in groups])
    counts = [len(f) for f in flat]

    def kernel(*refs):
        named, first = {}, 0
        for tree, count in zip(trees, counts):
            named.update(jax.tree.unflatten(tree, refs[first : first + count]))
            first += count
        body(box(named))

    smem = pl.BlockSpec(memory_space=pltpu.SMEM)
    results = pl.pallas_call(
        kernel,
        out_shape=tuple(flat[3]) + tuple(flat[4]),
        in_specs=[VMEM] * counts[0] + [ANY] * counts[1] + [smem] * counts[2],
        out_specs=(VMEM,) * counts[3] + (ANY,) * counts[4],
        scratch_shapes=list(flat[5]),
        compiler_params=pltpu.CompilerParams(
            collective_id=collective_id, has_side_effects=True, vmem_limit_bytes=63 * 2**20),
        cost_estimate=pl.CostEstimate(flops=10**11, bytes_accessed=2 * 10**8, transcendentals=10**7),
        name=name,
    )(*flat[0], *flat[1], *flat[2])
    done = jax.tree.unflatten(trees[3], results[: counts[3]])
    done.update(jax.tree.unflatten(trees[4], results[counts[3] :]))
    return box(done)


def shape(*dims, dtype=BF):
    return jax.ShapeDtypeStruct(dims, dtype)


def keep(*dims, dtype=BF):
    return pltpu.VMEM(dims, dtype)


def copies(*dims):
    return pltpu.SemaphoreType.DMA(dims)


def square_sum_items(tokens, width):
    half = width // 2
    return dict(
        pair=dict(stage=keep(2, tokens, half), inbox=keep(2, tokens, half)),
        single=dict(stage=keep(4, tokens, half), inbox=keep(4, tokens, half)), ss_send=copies(5), ss_recv=copies(5))


def flat_weight(ref, lo=0, hi=None):
    if len(ref.shape) == 2:
        return ref[:, lo:hi]
    v = ref[:, :, :, lo:hi]
    return v.reshape(v.shape[0] * v.shape[1] * v.shape[2], v.shape[3])


def side_weight(ref, cc, lo=0, hi=None):
    v = ref[:, cc, :, lo:hi]
    return v.reshape(v.shape[0] * v.shape[1], v.shape[2])


def block_sum_item(nz, *dims, dtype=BF):
    return dict(stage=keep(nz, 2, *dims, dtype=dtype), cin=keep(nz, *dims, dtype=dtype), zin=keep(nz + 1, *dims, dtype=dtype),
                csend=copies(nz), crecv=copies(nz), zsend=copies(nz), zrecv=copies(nz + 1))


def key_columns(at, slopes, seg, zz, cc, tokens):
    rows = 4 * tokens
    column = lax.broadcasted_iota(jnp.int32, (128, rows), 0) % 64
    row = lax.broadcasted_iota(jnp.int32, (128, rows), 1)
    position = ((zz * 8 + (row // tokens) * 2 + cc) * tokens + row % tokens).astype(F32)
    value = jnp.where(seg[2 * zz + cc] == column - SEGMENT_LANE, 0.0, -1e30)
    value = jnp.where(column < SEGMENT_LANE + 5, value, 0.0)
    value = jnp.where(column < SEGMENT_LANE, 1.0, value)
    for h in range(3):
        for i, term in enumerate(split3(position * slopes[3 * at.g + h])):
            value = jnp.where(column == 3 * h + i, term, value)
    return value.T.astype(BF)


def segment_columns(at, seg, rows):
    column = lax.broadcasted_iota(jnp.int32, (128, rows), 0) % 64
    return jnp.where(seg[at.block] == column - SEGMENT_LANE, 1.0, 0.0).T


def query_operand(at, q_ref, inside, slopes, side, h, tokens, lse=None):
    rows = 4 * tokens
    if h < 2:
        data = q_ref[:, 0:128]
    else:
        data = jnp.concatenate([q_ref[:, 128:192], jnp.zeros((rows, 64), q_ref.dtype)], axis=1)
    half = K_AT[h][1]
    sign = 1.0 if side == 0 else -1.0
    column = lanes(rows) % 64
    aug = jnp.where((column >= 3 * h) & (column < 3 * h + 3), sign, inside[...])
    term = at.positions(at.z, at.c, tokens, rows) * (slopes[3 * at.g + h] * -sign)
    if lse is not None:
        term = term - lse
    aug = with_lanes(aug, ROW_LANE if half else 64 + ROW_LANE, split3(term))
    return jnp.where(in_half(half, rows), data.astype(F32) * 0.125, aug).astype(BF)


def attention(at, gather, q_op, kaug, m_ref, acc_ref, behind):
    m_ref[...] = jnp.full(m_ref.shape, -1e30, F32)
    acc_ref[...] = jnp.zeros(acc_ref.shape, F32)

    def compute(zz, cc, same):
        kv, aug = gather.buf.at[zz, cc], kaug[zz, cc]
        side = (zz > at.z).astype(jnp.int32)
        for h in range(3):
            k = k_operand(kv, aug, h)
            if same:
                s = jnp.minimum(dot(q_op[0, h], k, NT), dot(q_op[1, h], k, NT))
            else:
                s = dot(q_op[side, h], k, NT)
            m_old = m_ref[h]
            m_new = jnp.maximum(m_old, jnp.max(s, axis=1, keepdims=True))
            p = jnp.exp(s - m_new[:, :1]).astype(BF)
            acc_ref[h] = acc_ref[h] * jnp.exp(m_old - m_new) + dot(p, v_operand(kv, h))
            m_ref[h] = m_new

    def here(i):
        cc = jnp.where(i == 0, at.c, at.oc)

        @pl.when(i == 1)
        def _():
            gather.wait(at.z, at.oc)
        compute(at.z, cc, True)
    loop(0, 2, here)

    def step(d):
        gather.serve(d)
        behind(d)

        def visit(i):
            zz = jnp.where(i % 2 == 0, at.z - d, at.z + d)

            @pl.when((zz >= 0) & (zz < at.nz))
            def _():
                @pl.when(i >= 2)
                def _():
                    gather.wait(zz, at.oc)
                compute(zz, jnp.where(i < 2, at.c, at.oc), False)
        loop(0, 4, visit)
    loop(1, at.nz, step)


def attention_end(at, q_ref, inside, slopes, tokens, m_ref, acc_ref, ctx_ref, ctxf_ref, qb_ref):
    for h in range(3):
        half = V_AT[h][1]
        first = 0 if half else 64
        acc = acc_ref[h]
        total = acc[:, first : first + 1]
        ctx = acc[:, 64 * half : 64 * half + 64] / total
        ctxf_ref[:, 64 * h : 64 * h + 64] = ctx
        ctx_ref[:, 64 * h : 64 * h + 64] = ctx.astype(BF)
        lse = m_ref[h] + jnp.log(total)
        for side in range(2):
            qb_ref[side, h] = query_operand(at, q_ref, inside, slopes, side, h, tokens, lse)


def fwd_kernel(nz, layers, host, R):
    at = Place(nz)
    tokens = R.x0.shape[0]
    rows, half_rows = 4 * tokens, 2 * tokens
    quarter = R.hid.shape[1]
    group = R.ctx_now[0].shape[1]
    at.enter()
    part = R.part
    square_sum = SquareSum(at, part, R.pair, R.single, R.ss_send, R.ss_recv)
    gather_x = [SquareGather(at, R.xr_now[l], R.x_send.at[l], R.x_recv.at[l]) for l in range(layers)]
    gather_y = [SquareGather(at, R.yr_now[l], R.y_send.at[l], R.y_recv.at[l]) for l in range(layers)]
    kv = BlockGather(at, R.kv_now)
    saves, waited = [], []

    def save(source, target):
        saves.append(pltpu.make_async_copy(source, target, R.saved.at[len(saves)]))
        saves[-1].start()
        return len(saves) - 1

    def wait_saved(number):
        saves[number].wait()
        waited.append(number)

    if host:
        qkv, gu, down = [[BlockGather(at, item) for item in items] for items in (R.qkv_now, R.gu_now, R.down_now)]
        ow = BlockGather(at, R.ow_now)
        qkv_w, gu_w, down_w, out_w = [g.buf for g in qkv], [g.buf for g in gu], [g.buf for g in down], R.out_now
        qkv[0].put(R.qkv_own[0][...])
        qkv[0].start()
    else:
        qkv_w, gu_w, down_w, out_w = R.qkv_given, R.gu_given, R.down_given, R.out_given

    R.xr_now[0][at.g] = R.x0[...]
    gather_x[0].start()
    if host:
        for l in range(layers):
            if l:
                qkv[l].put(R.qkv_own[l][...])
            gu[l].put(R.gu_own[l][...])
            down[l].put(R.down_own[l][...])
        ow.put(R.ow_own[...])

    def columns(b):
        R.kaug_now[b // 2, b % 2] = key_columns(at, R.slopes, R.seg, b // 2, b % 2, tokens)
    loop(0, 2 * nz, columns)
    save(R.kaug_now, R.kaug)
    R.inside[...] = segment_columns(at, R.seg, rows)

    def small(l, t):
        return R.small[8 * l + t : 8 * l + t + 1, :]

    def of(buf, half):
        v = buf[pl.ds(2 * half, 2)]
        return v.reshape(half_rows, v.shape[2])

    def half_at(half):
        return pl.ds(pl.multiple_of(half * half_rows, half_rows), half_rows)

    def put_part(half, value):
        part[pl.ds(2 * half, 2)] = value.reshape(2, tokens, value.shape[1])

    def of_group(row):
        value = jnp.zeros((1, group), F32)
        for g in range(4):
            value = jnp.where(at.g == g, row[:, group * g : group * g + group], value)
        return value

    if host:
        qkv[0].serve_all()
        ow.start()
        gu[0].start()
        down[0].start()
        qkv[0].collect()
    R.small[...] = side_weight(qkv_w[0], 1, 128, 256).astype(F32).T[64 : 64 + 8 * layers, :]
    R.state[...] = R.x0[...].astype(F32)
    gather_x[0].wait_near()
    gather_x[0].wait_far()

    for l in range(layers):
        last = l == layers - 1
        x_all = R.xr_now[l][...].reshape(rows, -1)
        save(R.xr_now[l], R.xr[l])
        qb, vb = of_group(small(l, 2)), of_group(small(l, 3))
        none = jnp.zeros((1, 128), F32)
        kv_bias = jnp.concatenate([none, vb[:, :128], none[:, :64], vb[:, 128:192]], axis=1)
        if l:
            pl.semaphore_wait(R.kv_free, at.neighbours())
        kv.put((dot(x_all, side_weight(qkv_w[l], 0)) + kv_bias).astype(BF))
        kv.start()
        R.q[...] = (dot(x_all, side_weight(qkv_w[l], 1, 0, group)) + qb).astype(BF)
        for side in range(2):
            for h in range(3):
                R.q_op[side, h] = query_operand(at, R.q, R.inside, R.slopes, side, h, tokens)

        def behind(d, l=l):
            if host:
                if l == 0:
                    ow.serve(d)
                gu[l].serve(d)
                down[l].serve(d)
        attention(at, kv, R.q_op, R.kaug_now, R.m, R.acc, behind)
        attention_end(at, R.q, R.inside, R.slopes, tokens, R.m, R.acc, R.ctx_now[l], R.ctxf_now[l], R.qb_now[l])
        kv_saved = save(kv.buf, R.kv[l])
        save(R.ctx_now[l], R.ctx[l])
        save(R.ctxf_now[l], R.ctxf[l])
        save(R.qb_now[l], R.qb[l])
        kv.finish()
        if l == 0 and host:
            ow.collect()
            step = group // (2 * nz)
            for i in range(layers):
                for b in range(2 * nz):
                    R.ow_wide[...] = ow.buf[b // 2, b % 2].astype(F32)
                    R.ow_flat[step * b : step * b + step, :] = R.ow_wide[step * i : step * i + step, :]
                R.out_now[i][...] = R.ow_flat[...].astype(BF)
                save(R.out_now[i], R.out_w[i])
        if not last and host:
            qkv[l + 1].start()
        if l:
            square_sum.finish()
        for number, half in enumerate((1 - at.x, at.x)):
            put_part(half, dot(R.ctx_now[l][half_at(half), :], out_w[l][...]))
            if number == 0:
                square_sum.send_far()
            else:
                square_sum.send_near()
        square_sum.relay()
        wait_saved(kv_saved)
        if not last:
            at.signal_neighbours(R.kv_free)
        R.sum1_now[l][...] = R.state[...] + (square_sum.total() + small(l, 4))
        save(R.sum1_now[l], R.sum1[l])
        y = layer_norm(R.sum1_now[l][...], small(l, 0), small(l, 5))
        R.yr_now[l][at.g] = y.astype(BF)
        gather_y[l].start()
        R.state[...] = y
        if host:
            gu[l].collect()
            down[l].collect()
        gather_y[l].wait_near()
        if l:
            wait_saved(mixed_saved)
        square_sum.finish()
        for number, half in enumerate((at.x, 1 - at.x)):
            if number == 1:
                if not last and host:
                    qkv[l + 1].serve_all()
                    gu[l + 1].start()
                    down[l + 1].start()
                gather_y[l].wait_far()
            here = half_at(half)
            y_half = of(R.yr_now[l], half)
            for col in range(0, quarter, 256):
                gate = dot(y_half, side_weight(gu_w[l], 0, col, col + 256))
                up = dot(y_half, side_weight(gu_w[l], 1, col, col + 256))
                R.mixed_now[here, col : col + 256] = gate
                R.mixed_now[here, quarter + col : quarter + col + 256] = up
                R.hid[:, col : col + 256] = (gate * normal_cdf(gate) * up).astype(BF)
            put_part(half, dot(R.hid[...], flat_weight(down_w[l])))
            if number == 0:
                square_sum.send_near()
            else:
                square_sum.send_far()
        mixed_saved = save(R.mixed_now, R.mixed[l])
        save(R.yr_now[l], R.yr[l])
        if host:
            save(qkv[l].buf, R.qkv_w[l])
            save(gu[l].buf, R.gu_w[l])
            save(down[l].buf, R.down_w[l])
        square_sum.relay()
        if not last and host:
            qkv[l + 1].collect()
        R.sum2_now[l][...] = R.state[...] + (square_sum.total() + small(l, 6))
        save(R.sum2_now[l], R.sum2[l])
        state = layer_norm(R.sum2_now[l][...], small(l, 1), small(l, 7))
        R.state[...] = state
        if last:
            R.output[...] = state.astype(BF)
        else:
            R.xr_now[l + 1][at.g] = state.astype(BF)
            gather_x[l + 1].start()
            gather_x[l + 1].wait_near()
            gather_x[l + 1].wait_far()
    for l in range(layers):
        gather_x[l].finish()
        gather_y[l].finish()
    square_sum.finish()
    if host:
        for items in (qkv, gu, down):
            for item in items:
                item.finish()
        ow.finish()
    for number, copy in enumerate(saves):
        if number not in waited:
            copy.wait()


def fwd(x0, slopes, seg, weights, layers, host):
    nb, _, rows = seg.shape
    nz = nb // 2
    tokens, width = x0.shape
    group = width // 4
    each = range(layers)
    quarter = (weights.gu_own[0].shape if host else weights.gu_given[0].shape)[-1]
    keep_rows = lambda: [keep(4, tokens, width) for _ in each]
    keep_wide = lambda: [keep(tokens, width, dtype=F32) for _ in each]
    scratch = dict(
        xr_now=keep_rows(), x_send=copies(layers, 4), x_recv=copies(layers, 4),
        yr_now=keep_rows(), y_send=copies(layers, 4), y_recv=copies(layers, 4),
        part=keep(4, tokens, width, dtype=F32), state=keep(tokens, width, dtype=F32), **square_sum_items(tokens, width),
        kv_now=block_gather_item(nz, rows, 384), kv_free=pltpu.SemaphoreType.REGULAR, saved=copies(16 * layers),
        kaug_now=keep(nz, 2, rows, 128), inside=keep(rows, 128, dtype=F32),
        q=keep(rows, group), q_op=keep(2, 3, rows, 128),
        m=keep(3, rows, 128, dtype=F32), acc=keep(3, rows, 128, dtype=F32),
        ctx_now=[keep(rows, group) for _ in each], ctxf_now=[keep(rows, group, dtype=F32) for _ in each],
        qb_now=[keep(2, 3, rows, 128) for _ in each], sum1_now=keep_wide(), sum2_now=keep_wide(),
        mixed_now=keep(rows, 2 * quarter, dtype=F32), hid=keep(2 * tokens, quarter))
    far_out = dict(
        xr=[shape(4, tokens, width) for _ in each], yr=[shape(4, tokens, width) for _ in each],
        kv=[shape(nz, 2, rows, 384) for _ in each], ctx=[shape(rows, group) for _ in each],
        ctxf=[shape(rows, group, dtype=F32) for _ in each], qb=[shape(2, 3, rows, 128) for _ in each],
        sum1=[shape(tokens, width, dtype=F32) for _ in each], sum2=[shape(tokens, width, dtype=F32) for _ in each],
        mixed=[shape(rows, 2 * quarter, dtype=F32) for _ in each], kaug=shape(nz, 2, rows, 128))
    near = dict(x0=x0, seg=seg, **vars(weights))
    if host:
        gathered = lambda arrays: [shape(nz, 2, *w.shape) for w in arrays]
        items = lambda arrays: [block_gather_item(nz, *w.shape) for w in arrays]
        far_out.update(qkv_w=gathered(weights.qkv_own), gu_w=gathered(weights.gu_own), down_w=gathered(weights.down_own),
                       out_w=[shape(group, width) for _ in each])
        scratch.update(
            qkv_now=items(weights.qkv_own), gu_now=items(weights.gu_own), down_now=items(weights.down_own),
            ow_now=block_gather_item(nz, *weights.ow_own.shape), out_now=[keep(group, width) for _ in each],
            ow_wide=keep(*weights.ow_own.shape, dtype=F32), ow_flat=keep(group, width, dtype=F32))
    out = dict(output=shape(tokens, width), small=shape(8 * layers, width, dtype=F32))
    done = call(functools.partial(fwd_kernel, nz, layers, host), "forward", 0, near=near, table=dict(slopes=slopes),
                out=out, far_out=far_out, scratch=scratch)
    if not host:
        done.qkv_w, done.gu_w, done.down_w, done.out_w = weights.qkv_given, weights.gu_given, weights.down_given, weights.out_given
    done.down_w = [w.reshape(quarter, width) for w in done.down_w]
    done.xr = [v.reshape(rows, width) for v in done.xr]
    done.yr = [v.reshape(rows, width) for v in done.yr]
    return done


def attn_back(at, R, l, top, begin, behind, at_end):
    nz, rows = at.nz, R.kvbuf.shape[1]
    q_ref, do_ref, dqacc = R.qb[l], R.do, R.dqacc
    dkv = BlockSum(at, R.dkv)

    def target(i):
        right = nz - 1 - at.z
        from_right = jnp.where(i < right, nz - 1 - i, i - right)
        from_left = jnp.where(i < at.z, i, nz - 1 - (i - at.z))
        return jnp.where(i == nz - 1, at.z, jnp.where(at.z < nz // 2, from_right, from_left))

    class Load:
        def __init__(self, t, slot):
            cc = at.oc if slot == 0 else at.c
            self.copies = [pltpu.make_async_copy(source.at[t, cc], target.at[slot], R.kvsem.at[i, slot])
                           for i, (source, target) in enumerate(((R.kv[l], R.kvbuf), (R.kaug, R.augbuf)))]

        def start(self):
            for copy in self.copies:
                copy.start()

        def wait(self):
            for copy in self.copies:
                copy.wait()

    load = Load

    dqacc[...] = jnp.zeros(dqacc.shape, F32)

    def compute(t, slot, same):
        cc = at.oc if slot == 0 else at.c
        side = (t > at.z).astype(jnp.int32)
        kv, aug = R.kvbuf.at[slot], R.augbuf[slot]
        dks, dvs = [], []
        for h in range(3):
            k, v = k_operand(kv, aug, h), v_operand(kv, h)
            if same:
                s = jnp.minimum(dot(k, q_ref[0, h], NT), dot(k, q_ref[1, h], NT))
            else:
                s = dot(k, q_ref[side, h], NT)
            p = jnp.exp(s)
            ds = (p * dot(v, do_ref[h], NT)).astype(BF)
            dvs.append(dot(p.astype(BF), do_ref[h]))
            dks.append(dot(ds, q_ref[side, h]))
            dqacc[h] += dot(ds, k, TN)
        low = in_half(0, rows)
        dkv.stage[t, cc, :, 0:128] = jnp.where(low, dks[0], dks[1]).astype(BF)
        dkv.stage[t, cc, :, 128:256] = jnp.where(low, dvs[0], dvs[1]).astype(BF)
        dkv.stage[t, cc, :, 256:384] = jnp.where(low, dks[2], dvs[2]).astype(BF)

    def far(t, same):
        load(t, 1).start()
        load(t, 0).wait()
        compute(t, 0, same)
        dkv.to_beside(t).start()

    load(target(0), 0).start()
    begin()
    if not top:
        pl.semaphore_wait(R.dkv.free, at.neighbours())

    def step(i):
        t = target(i)
        far(t, False)
        load(target(i + 1), 0).start()
        load(t, 1).wait()
        compute(t, 1, False)
        dkv.serve(i, relay=False)

        @pl.when(i > 0)
        def _():
            dkv.serve(i - 1, source=False)
        behind(i)
    loop(0, nz - 1, step)
    far(at.z, True)
    dkv.serve(nz - 2, source=False)
    load(at.z, 1).wait()
    compute(at.z, 1, True)
    at_end()
    dq = jnp.where(in_half(0, rows), dqacc[0], dqacc[1]) * 0.125
    R.dproj[:, 384:512] = dq.astype(BF)
    R.dproj[:, 512:576] = (dqacc[2][:, 0:64] * 0.125).astype(BF)
    R.dproj[:, 0:384] = dkv.total().astype(BF)
    if l > 0:
        at.signal_neighbours(R.dkv.free)
    dkv.finish()


def bwd_kernel(nz, layers, host, R):
    at = Place(nz)
    tokens = R.grad.shape[0]
    rows, half_rows = 4 * tokens, 2 * tokens
    quarter = R.hid.shape[1]
    width = R.grad.shape[1]
    mixed, yr, xr, gu_w, down_w, qkv_w = range(6)
    streams = ((R.mixed, R.mixed_now), (R.yr, R.yr_now), (R.xr, R.xr_now), (R.gu_w, R.gu_now), (R.down_w, R.down_now),
               (R.qkv_w, R.qkv_now))

    def load(which, l):
        return pltpu.make_async_copy(streams[which][0][l], streams[which][1], R.load.at[which])

    for which in range(6):
        load(which, layers - 1).start()
    at.enter()
    R.dproj[:, 576:768] = jnp.zeros((rows, 192), BF)
    gather_df = SquareGather(at, R.df, R.df_send, R.df_recv)
    gather_da = SquareGather(at, R.da, R.da_send, R.da_recv)
    part = R.part
    square_sum = SquareSum(at, part, R.pair, R.single, R.ss_send, R.ss_recv)
    if host:
        gu_sum, dn_sum, qk_sum, ow_sum = [[BlockSum(at, item) for item in items] for items in (R.gu, R.dn, R.qk, R.ow)]
        sm_sum = BlockSum(at, R.sm)

    def small(l, t):
        return R.small[8 * l + t : 8 * l + t + 1, :]

    def put_small(l, t, value):
        R.tok_small[8 * l + t : 8 * l + t + 1, :] = value

    def of(buf, half):
        v = buf[pl.ds(2 * half, 2)]
        return v.reshape(half_rows, v.shape[2])

    def half_at(half):
        return pl.ds(pl.multiple_of(half * half_rows, half_rows), half_rows)

    def put_part(half, value):
        part[pl.ds(2 * half, 2)] = value.reshape(2, tokens, value.shape[1])

    def wgrad(left, right, stage, cc, lo, hi):
        for first in range(0, left.shape[1], 384):
            v = dot(left[:, first : first + 384], right[:, lo:hi], TN)
            if len(stage.shape) == 2:
                stage[first : first + 384, :] = v.astype(BF)
                continue
            step = stage.shape[2]
            for i in range(384 // step):
                b = first // step + i
                zz, side = (b // 2, b % 2) if cc is None else (b, cc)
                stage[zz, side] = v[step * i : step * i + step].astype(BF)

    def feed_forward_sums(l):
        return (gu_sum[l], dn_sum[l]) if host and l < layers else ()

    def attention_sums(l):
        return (qk_sum[l], ow_sum[l]) if host and l < layers else ()

    def serve(items, p):
        for item in items:
            item.serve(p)

    def emit(l):
        if host and l < layers:
            R.gu_sum[l][...] = gu_sum[l].total().astype(BF)
            R.dn_sum[l][...] = dn_sum[l].total()
            R.qk_sum[l][...] = qk_sum[l].total().astype(BF)
            R.ow_sum[l][...] = ow_sum[l].total()

    R.g[...] = R.grad[...].astype(F32)
    for l in reversed(range(layers)):
        top = l == layers - 1
        e2, d_gain, d_shift = norm_back(R.g[...], R.sum2[l][...], small(l, 1))
        put_small(l, 1, d_gain)
        put_small(l, 5, d_shift)
        low = e2.astype(BF)
        put_small(l, 4, jnp.sum(low.astype(F32), axis=0, keepdims=True))
        if not top:
            square_sum.finish()
        R.df[at.g] = low
        gather_df.start()
        R.e2[...] = e2
        for which in range(6):
            load(which, l).wait()
        serve(feed_forward_sums(l + 1), 1)
        gather_df.wait_near()
        for number, half in enumerate((at.x, 1 - at.x)):
            if number == 1:
                gather_df.wait_far()
                serve(attention_sums(l + 1), 1)
            here = half_at(half)
            dhid_all = dot(of(R.df, half), R.down_now[...], NT)
            for col in range(0, quarter, 256):
                dhid = dhid_all[:, col : col + 256]
                gate = R.mixed_now[here, col : col + 256]
                up = R.mixed_now[here, quarter + col : quarter + col + 256]
                cdf = normal_cdf(gate)
                act = gate * cdf
                R.hid[here, col : col + 256] = (act * up).astype(BF)
                R.dgu[here, col : col + 256] = (dhid * up * (cdf + gate * normal_pdf(gate))).astype(BF)
                R.dgu[here, quarter + col : quarter + col + 256] = (dhid * act).astype(BF)
            put_part(half, dot(R.dgu[here, :quarter], side_weight(R.gu_now, 0), NT)
                     + dot(R.dgu[here, quarter:], side_weight(R.gu_now, 1), NT))
            if number == 0:
                square_sum.send_near()
            else:
                square_sum.send_far()
        wgrad(R.hid, R.df[...].reshape(rows, width), R.dn[l].stage, None, 0, width)
        square_sum.relay()
        serve(feed_forward_sums(l + 1), 2)
        for p in range(3, nz - 1):
            serve(feed_forward_sums(l + 1), p)
        dy = R.e2[...] + square_sum.total()
        e1, d_gain, d_shift = norm_back(dy, R.sum1[l][...], small(l, 0))
        put_small(l, 0, d_gain)
        put_small(l, 3, d_shift)
        low = e1.astype(BF)
        put_small(l, 2, jnp.sum(low.astype(F32), axis=0, keepdims=True))
        R.da[at.g] = low
        gather_da.start()
        R.e1[...] = e1
        for cc in range(2):
            wgrad(R.yr_now, R.dgu, R.gu[l].stage, cc, quarter * cc, quarter * cc + quarter)
        gather_da.wait_near()
        gather_da.wait_far()
        for item in feed_forward_sums(l):
            item.start()
        if l > 0:
            for which in (mixed, yr, gu_w, down_w):
                load(which, l - 1).start()
        da_all = R.da[...].reshape(rows, width)
        dctx = dot(da_all, R.out_w[l][...], NT).astype(BF)
        d_out = dot(R.ctx[l][...], da_all, TN)
        if host:
            step = d_out.shape[0] // (2 * nz)
            for b in range(2 * nz):
                R.ow[l].stage[b // 2, b % 2] = jnp.concatenate(
                    [d_out[step * b : step * b + step], jnp.zeros((OW_ROWS - step, width), F32)]).astype(BF)
        else:
            R.ow[l].stage[...] = d_out.astype(BF)
        ctxf = R.ctxf[l]
        wide = dctx.astype(F32)
        first_two = wide[:, :128]
        third = jnp.concatenate([jnp.zeros((rows, 64), F32), wide[:, 128:192]], axis=1)
        prod = first_two * ctxf[:, :128]
        low_half = in_half(0, rows)
        deltas = [
            jnp.sum(jnp.where(low_half, prod, 0.0), axis=1, keepdims=True),
            jnp.sum(jnp.where(low_half, 0.0, prod), axis=1, keepdims=True),
            jnp.sum(wide[:, 128:192] * ctxf[:, 128:192], axis=1, keepdims=True),
        ]
        for h in range(3):
            half = V_AT[h][1]
            base = jnp.where(in_half(half, rows), first_two if h < 2 else third, 0.0)
            R.do[h] = with_lanes(base, 0 if half else 64, split3(-deltas[h])).astype(BF)

        def begin(l=l):
            serve(attention_sums(l + 1), 2)
            for p in range(3, nz - 1):
                serve(attention_sums(l + 1), p)

        def behind(i):
            pass

        def at_end(l=l):
            serve(feed_forward_sums(l), 0)
        attn_back(at, R, l, top, begin, behind, at_end)
        dproj = R.dproj
        bias_sum = jnp.sum(dproj[...].astype(F32), axis=0, keepdims=True)
        for t, row in ((6, bias_sum[:, 384:576]), (7, jnp.concatenate([bias_sum[:, 128:256], bias_sum[:, 320:384]], axis=1))):
            put_small(l, t, jnp.concatenate([jnp.where(at.g == g, row, 0.0) for g in range(4)], axis=1))
        gather_df.finish()
        gather_da.finish()
        square_sum.finish()
        for number, half in enumerate((1 - at.x, at.x)):
            put_part(half, dot(dproj[half_at(half), :384], side_weight(R.qkv_now, 0), NT)
                     + dot(dproj[half_at(half), 384:], side_weight(R.qkv_now, 1), NT))
            if number == 0:
                square_sum.send_far()
            else:
                square_sum.send_near()
        square_sum.relay()
        for cc in range(2):
            wgrad(R.xr_now, dproj, R.qk[l].stage, cc, 384 * cc, 384 * cc + 384)
        for item in attention_sums(l):
            item.start()
        serve(attention_sums(l), 0)
        if l > 0:
            load(xr, l - 1).start()
            load(qkv_w, l - 1).start()
        emit(l + 1)
        R.g[...] = R.e1[...] + square_sum.total()
    R.grad_in[...] = R.g[...]
    square_sum.finish()
    if host:
        for b in range(2 * nz):
            step = width // (2 * nz)
            sm_sum.stage[b // 2, b % 2, :, 0:step] = R.tok_small[:, step * b : step * b + step]
        sm_sum.start()
        last = feed_forward_sums(0) + attention_sums(0) + (sm_sum,)
        sm_sum.serve(0)
        for p in range(1, nz - 1):
            serve(last, p)
        R.sm_sum[...] = sm_sum.total()
        emit(0)
        for l in range(layers):
            for item in feed_forward_sums(l) + attention_sums(l):
                item.finish()
        sm_sum.finish()


def bwd(grad, saved, host):
    layers = len(saved.qkv_w)
    nz, _, rows, _ = saved.kaug.shape
    tokens, width = grad.shape
    quarter, group = width, width // 4
    quarter = saved.down_w[0].shape[0]
    r, rd = width // nz, quarter // (2 * nz)
    each = range(layers)
    out = dict(grad_in=shape(tokens, width, dtype=F32))
    scratch = {}
    if host:
        out.update(
            gu_sum=[shape(r, quarter) for _ in each], dn_sum=[shape(rd, width, dtype=F32) for _ in each],
            qk_sum=[shape(r, 384) for _ in each], ow_sum=[shape(OW_ROWS, width, dtype=F32) for _ in each],
            sm_sum=shape(8 * layers, 128, dtype=F32))
        scratch.update(
            gu=[block_sum_item(nz, r, quarter) for _ in each], dn=[block_sum_item(nz, rd, width) for _ in each],
            qk=[block_sum_item(nz, r, 384) for _ in each], ow=[block_sum_item(nz, OW_ROWS, width) for _ in each],
            sm=block_sum_item(nz, 8 * layers, 128, dtype=F32), tok_small=keep(8 * layers, width, dtype=F32))
    else:
        out.update(
            gu=[dict(stage=shape(nz, 2, r, quarter)) for _ in each], dn=[dict(stage=shape(quarter, width)) for _ in each],
            qk=[dict(stage=shape(nz, 2, r, 384)) for _ in each], ow=[dict(stage=shape(group, width)) for _ in each],
            tok_small=shape(8 * layers, width, dtype=F32))
    like = lambda arrays: keep(*arrays[0].shape, dtype=arrays[0].dtype)
    scratch.update(
        mixed_now=like(saved.mixed), yr_now=like(saved.yr), xr_now=like(saved.xr), gu_now=like(saved.gu_w),
        down_now=like(saved.down_w), qkv_now=like(saved.qkv_w), load=copies(6), kvbuf=keep(2, rows, 384), augbuf=keep(2, rows, 128), kvsem=copies(2, 2),
        df=keep(4, tokens, width), df_send=copies(4), df_recv=copies(4),
        da=keep(4, tokens, width), da_send=copies(4), da_recv=copies(4),
        part=keep(4, tokens, width, dtype=F32), **square_sum_items(tokens, width),
        g=keep(tokens, width, dtype=F32), e1=keep(tokens, width, dtype=F32), e2=keep(tokens, width, dtype=F32),
        hid=keep(rows, quarter), dgu=keep(rows, 2 * quarter), do=keep(3, rows, 128),
        dqacc=keep(3, rows, 128, dtype=F32), dproj=keep(rows, 768),
        dkv=dict(block_sum_item(nz, rows, 384), free=pltpu.SemaphoreType.REGULAR))
    near = dict(grad=grad, small=saved.small, sum1=saved.sum1, sum2=saved.sum2, ctx=saved.ctx,
                ctxf=saved.ctxf, qb=saved.qb, out_w=saved.out_w)
    far = dict(mixed=saved.mixed, yr=saved.yr, xr=saved.xr, gu_w=saved.gu_w, down_w=saved.down_w, kv=saved.kv, kaug=saved.kaug,
               qkv_w=saved.qkv_w)
    return call(functools.partial(bwd_kernel, nz, layers, host), "backward", 1, near=near, far=far, out=out, scratch=scratch)


def shards(hidden_in, out_grad, segment_ids, alibi_slopes, qkv_weight, out_weight, gate_up_weight, down_weight, gains, biases):
    nz = lax.axis_size("z")
    nb = 2 * nz
    square, everyone, blocks = ("x", "y", "c"), ("z", "x", "y", "c"), ("z", "c")
    z, c = lax.axis_index("z"), lax.axis_index("c")
    tokens, width = hidden_in.shape
    layers, wrows = qkv_weight.shape[:2]
    ff = gate_up_weight.shape[2] // 2
    group, quarter = width // 4, ff // 4
    host = (width // nz) % 16 == 0 and down_weight.shape[1] % 16 == 0

    def to_groups(w):
        w = w.reshape(wrows, 3, 4, 3, 64)
        q, k, v = w[:, 0], w[:, 1], w[:, 2]
        kv = jnp.stack([k[:, :, 0], k[:, :, 1], v[:, :, 0], v[:, :, 1], k[:, :, 2], v[:, :, 2]], axis=2)
        return kv.reshape(wrows, 4, 384), q.reshape(wrows, 4, group)

    def from_groups(kv, q):
        kv, q = kv.reshape(4, wrows, 6, 64), q.reshape(4, wrows, 3, 64)
        k = jnp.stack([kv[:, :, 0], kv[:, :, 1], kv[:, :, 4]], axis=2)
        v = jnp.stack([kv[:, :, 2], kv[:, :, 3], kv[:, :, 5]], axis=2)
        return jnp.stack([q, k, v]).transpose(2, 0, 1, 3, 4).reshape(wrows, 3 * width)

    small = jnp.concatenate([gains, biases], axis=1).transpose(0, 2, 1)
    small = jnp.concatenate([small[l] for l in range(layers)], axis=1)
    small = jnp.pad(small, ((0, 0), (0, 192 - small.shape[1])))
    small = jnp.broadcast_to(small[:, None], (wrows, 4, 192))
    nothing = jnp.zeros((wrows, 4, 192), BF)
    gu = gate_up_weight.reshape(layers, wrows, 2, nz, 4, quarter // nz).transpose(0, 1, 4, 2, 3, 5).reshape(layers, wrows, 4, 2, quarter)
    sides = [[], []]
    for l in range(layers):
        kv, q = to_groups(qkv_weight[l])
        sides[0].append(kv)
        sides[1] += [q, nothing if l else small]
    for l in range(layers):
        for side in range(2):
            sides[side].append(gu[l, :, :, side])
    both = jnp.stack([jnp.concatenate(side, axis=2) for side in sides], axis=2).reshape(wrows, 8, -1)
    spread = lax.all_to_all(both, square, split_axis=1, concat_axis=0, tiled=True).reshape(8 * wrows, -1)
    qkv_own = [spread[:, 384 * l : 384 * l + 384] for l in range(layers)]
    gu0 = 384 * layers
    gu_own = [spread[:, gu0 + quarter * l : gu0 + quarter * l + quarter] for l in range(layers)]
    places = [(8 * zz + 2 * g + cc, g * nb + 2 * zz + cc) for zz in range(nz) for g in range(4) for cc in range(2)]
    ow_own = lax.ppermute(out_weight, everyone, [(chunk, device) for device, chunk in places])
    if host:
        weights = types.SimpleNamespace(qkv_own=qkv_own, gu_own=gu_own, down_own=[down_weight[l] for l in range(layers)],
                                        ow_own=ow_own.reshape(layers * wrows, width))
    else:
        whole = lambda v: lax.all_gather(v, blocks, axis=0).reshape(nz, 2, *v.shape)
        flat = lambda v: lax.all_gather(v, blocks, axis=0, tiled=True)
        weights = types.SimpleNamespace(
            qkv_given=[whole(v) for v in qkv_own], gu_given=[whole(v) for v in gu_own],
            down_given=[flat(down_weight[l]) for l in range(layers)], out_given=[flat(ow_own[l]) for l in range(layers)])

    seg = segment_ids.reshape(nz, 4, 2, tokens).transpose(0, 2, 1, 3).reshape(nb, 1, 4 * tokens)
    saved = fwd(hidden_in, alibi_slopes, seg, weights, layers, host)
    done = bwd(out_grad, saved, host)

    step = width // nb
    if host:
        sm = done.sm_sum[:, :step]
    else:
        blocks_sum = lambda v: lax.psum_scatter(v, blocks, scatter_dimension=0, tiled=True)
        done.gu_sum = [blocks_sum(item.stage.reshape(nb, -1, quarter))[0] for item in done.gu]
        done.qk_sum = [blocks_sum(item.stage.reshape(nb, -1, 384))[0] for item in done.qk]
        done.dn_sum = [blocks_sum(item.stage) for item in done.dn]
        done.ow_sum = [blocks_sum(item.stage) for item in done.ow]
        sm = lax.psum_scatter(done.tok_small.reshape(-1, nb, step), blocks, scatter_dimension=1, tiled=True)[:, 0]
    sm = sm.T.reshape(4, wrows, 8 * layers)
    high = lax.reduce_precision(sm, 8, 7)
    sm = jnp.concatenate([high, sm - high], axis=2).astype(BF)
    sm = lax.dynamic_update_slice_in_dim(jnp.zeros((8, wrows, 16 * layers), BF), sm, 4 * c, 0)
    rows_of = lambda v: v.reshape(8, wrows, -1)
    back = jnp.concatenate([rows_of(v) for v in done.qk_sum + done.gu_sum] + [sm], axis=2)
    back = lax.all_to_all(back, square, split_axis=0, concat_axis=0, tiled=True)
    sides = back.astype(F32).reshape(4, 2, wrows, -1)
    qkv_grad = jnp.stack([from_groups(sides[:, 0, :, 384 * l : 384 * l + 384], sides[:, 1, :, 384 * l : 384 * l + group])
                          for l in range(layers)])
    gu_grad = jnp.stack([sides[:, :, :, gu0 + quarter * l : gu0 + quarter * l + quarter] for l in range(layers)])
    gu_grad = gu_grad.reshape(layers, 4, 2, wrows, nz, quarter // nz).transpose(0, 3, 2, 4, 1, 5).reshape(layers, wrows, 2 * ff)
    sm = jnp.sum(sides[..., gu0 + quarter * layers :], axis=(0, 1))
    sm = (sm[:, : 8 * layers] + sm[:, 8 * layers :]).T.reshape(layers, 8, wrows)
    out_grad_w = lax.ppermute(jnp.stack(done.ow_sum)[:, :wrows].astype(F32), everyone, places)
    return (saved.output, done.grad_in, qkv_grad, out_grad_w, gu_grad, jnp.stack(done.dn_sum).astype(F32), sm[:, 0:2],
            jnp.concatenate([sm[:, 6:8], sm[:, 2:6]], axis=1))


def solution(mesh):
    nb, nh = mesh.devices.shape
    everyone = ("z", "x", "y", "c")
    tok, mid, last = P(everyone, None), P(None, everyone, None), P(None, None, everyone)
    return jax.shard_map(
        shards, mesh=Mesh(mesh.devices.reshape(nb // 2, 2, nh // 2, 2), everyone),
        in_specs=(tok, tok, P(), P(), mid, mid, mid, mid, last, last),
        out_specs=(tok, tok, mid, mid, mid, mid, last, last),
        check_vma=False,
    )
```

time: 585 us -> 471 us (0.81)
  the two profiles are of different devices: /device:TPU:21 before, /device:TPU:14 now
where the time goes in v3:
time: 471 us; the launch traced here: 467 us
  Pallas kernels  391 us (83%)
  local copies, waits for them, and re-layouts  30.3 us (6%)
  waiting for transfers between devices  23.6 us (5%)
  starting transfers between devices  15.8 us (3%)
  other arithmetic  4.78 us (1%)
    pallas_call x2, Pallas kernels, call(): pl.pallas_call(kernel, out_shape=tuple(flat[3]) + tuple(flat[4]), in_spec...  391 us
    unnamed x40, local copies, waits for them, and re-layouts  11 us
  transfers between devices with their start and end apart: 4, of which 3 were waited for; matrix products, arithmetic and copies ran while one was open for 1% of the time, Pallas kernels for 0%

profile of v3, /device:TPU:14, one launch (start us, length us, event | category | flops | bytes accessed | tf_op | source)
XLA Modules:
  0.0 466.6 jit_solution(6356894977569312358)
XLA Ops:
  0.7 1.0 fusion.11
  3.2 0.9 reshape.97
  6.6 1.0 copy.84
  7.5 4.2 all-to-all-start
  11.7 4.5 collective-permute-start
  17.6 8.6 %all-to-all-done = bf16[24,8,2304]{2,0,1:T(8,128)(2,1)S(1)} async-done(((bf16[24,8,2304]{2,0,1:T(8,128)(2,1)}), bf16[24,8,2304]{2,0,1:T(8,128)(2,1)S(1)}, u32[]{:S(2)}, u32[]{:S(2)}) %all-to-all-start) | async-done | bytes 884768 | tf_op jit(solution)/shard_map/all_to_all | solution.py:1202
  26.2 0.8 fusion.6
  28.4 186.3 %forward.1 = (bf16[128,768]{1,0:T(8,128)(2,1)}, f32[16,768]{1,0:T(8,128)}, bf16[512,192]{1,0:T(8,128)(2,1)}, bf16[512,192]{1,0:T(8,128)(2,1)}, f32[512,192]{1,0:...) custom-call(bf16[96,768]{1,0:T(8,128)(2,1)} %get-tuple-element.147.r, ...), custom_call_target="tpu_custom_call" | custom-call | flops 99999997952 | bytes 200000000 | tf_op jit(solution)/shard_map/forward/pallas_call | solution.py:431
  214.7 204.4 %backward.1 = (f32[96,768]{1,0:T(8,128)}, f32[96,768]{1,0:T(8,128)}, f32[128,768]{1,0:T(8,128)}, bf16[192,768]{1,0:T(8,128)(2,1)}, bf16[192,768]{1,0:T(8,128)(2,...) custom-call(bf16[512,192]{1,0:T(8,128)(2,1)} %get-tuple-element.48.r, ...), custom_call_target="tpu_custom_call" | custom-call | flops 99999997952 | bytes 200000000 | tf_op jit(solution)/shard_map/backward/pallas_call | solution.py:431
  419.1 1.6 constant_dynamic-update-slice_fusion.4
  421.6 1.6 constant_dynamic-update-slice_fusion.3
  423.2 1.8 constant_dynamic-update-slice_fusion.2
  425.0 1.7 constant_dynamic-update-slice_fusion.1
  427.3 4.9 %all-to-all-start.1 = ((bf16[8,24,2336]{2,1,0:T(8,128)(2,1)}), bf16[8,24,2336]{2,1,0:T(8,128)(2,1)S(1)}, u32[]{:S(2)}, u32[]{:S(2)}) async-start(bf16[8,24,2336]{2,1,0:T(8,128)(2,1)} %constant_dynamic-update-slice_fusion), calls=%async_computation.1 | async-start | bytes 1867776 | tf_op jit(solution)/shard_map/all_to_all | solution.py:1238
  432.3 2.2 collective-permute-start.1
  434.5 0.9 pad_maximum_fusion.1
  435.4 6.8 %collective-permute-done.1 = f32[2,24,768]{2,1,0:T(8,128)} collective-permute-done((f32[2,24,768]{2,1,0:T(8,128)S(1)}, f32[2,24,768]{2,1,0:T(8,128)}, u32[]{:S(2)}, u32[]{:S(2)}) %collective-permute-start.1) | collective-permute-done | bytes 147488 | tf_op jit(solution)/shard_map/ppermute | solution.py:1246
  442.2 8.2 %all-to-all-done.1 = bf16[8,24,2336]{2,1,0:T(8,128)(2,1)S(1)} async-done(((bf16[8,24,2336]{2,1,0:T(8,128)(2,1)}), bf16[8,24,2336]{2,1,0:T(8,128)(2,1)S(1)}, u32[]{:S(2)}, u32[]{:S(2)}) %all-to-all-start.1) | async-done | bytes 897056 | tf_op jit(solution)/shard_map/all_to_all | solution.py:1238
  454.0 1.2 maximum_bitcast_fusion.6
  458.5 1.0 copy.89
  459.5 2.4 reshape.117
  462.6 0.8 pad_maximum_fusion.2
  464.0 0.7 copy.113
  464.8 1.6 copy.114
  (109 shorter events, 16.1 us)
Async XLA Ops:
  0.6 2.3 copy-start.11
  0.6 2.3 copy-start.12
  0.7 2.6 copy-start
  6.5 5.2 %copy-start.13 = (bf16[2,24,768]{2,1,0:T(8,128)(2,1)S(1)}, bf16[2,24,768]{2,1,0:T(8,128)(2,1)}, u32[]{:S(2)}) copy-start(bf16[2,24,768]{2,1,0:T(8,128)(2,1)} %param.15) | copy-start | bytes 221188
  6.5 9.7 %copy-start.10 = (s32[4096]{0:T(1024)S(1)}, s32[4096]{0:T(1024)}, u32[]{:S(2)}) copy-start(s32[4096]{0:T(1024)} %param.12) | copy-start | bytes 49156
  6.5 10.3 %copy-start.2 = (bf16[2,96,768]{2,1,0:T(8,128)(2,1)S(1)}, bf16[2,96,768]{2,1,0:T(8,128)(2,1)}, u32[]{:S(2)}) copy-start(bf16[2,96,768]{2,1,0:T(8,128)(2,1)} %param.17) | copy-start | bytes 884740
  7.5 18.6 %all-to-all-start = ((bf16[24,8,2304]{2,0,1:T(8,128)(2,1)}), bf16[24,8,2304]{2,0,1:T(8,128)(2,1)S(1)}, u32[]{:S(2)}, u32[]{:S(2)}) async-start(bf16[24,8,2304]{2,0,1:T(8,128)(2,1)} %bitcast.16), calls=%async_computation | async-start | bytes 1769472 | tf_op jit(solution)/shard_map/all_to_all | solution.py:1202
  11.7 16.0 %collective-permute-start = (bf16[2,24,768]{2,1,0:T(8,128)(2,1)S(1)}, bf16[2,24,768]{2,1,0:T(8,128)(2,1)S(1)}, u32[]{:S(2)}, u32[]{:S(2)}) collective-permute-start(bf16[2,24,768]{2,1,0:T(8,128)(2,1)S(1)} %copy-done.13), channel_id=1, source_target_pairs={{0,0},{1,1},{8,2},{9,3},{16,4},{17,5},{24,6},{25,7},{2,8},{3,9},{1... | collective-permute-start | bytes 221192 | tf_op jit(solution)/shard_map/ppermute | solution.py:1207
  27.8 0.6 copy-start.14
  421.4 10.8 %copy-start.8 = (f32[32,768]{1,0:T(8,128)S(1)}, f32[32,768]{1,0:T(8,128)}, u32[]{:S(2)}) copy-start(f32[32,768]{1,0:T(8,128)} %get-tuple-element.82) | copy-start | bytes 294916
  421.4 10.8 %copy-start.9 = (f32[32,768]{1,0:T(8,128)S(1)}, f32[32,768]{1,0:T(8,128)}, u32[]{:S(2)}) copy-start(f32[32,768]{1,0:T(8,128)} %get-tuple-element.83) | copy-start | bytes 294916
  423.2 11.3 %copy-start.3 = (f32[96,768]{1,0:T(8,128)S(1)}, f32[96,768]{1,0:T(8,128)}, u32[]{:S(2)}) copy-start(f32[96,768]{1,0:T(8,128)} %get-tuple-element.84) | copy-start | bytes 884740
  423.2 11.3 %copy-start.4 = (f32[96,768]{1,0:T(8,128)S(1)}, f32[96,768]{1,0:T(8,128)}, u32[]{:S(2)}) copy-start(f32[96,768]{1,0:T(8,128)} %get-tuple-element.85) | copy-start | bytes 884740
  427.3 23.1 %all-to-all-start.1 = ((bf16[8,24,2336]{2,1,0:T(8,128)(2,1)}), bf16[8,24,2336]{2,1,0:T(8,128)(2,1)S(1)}, u32[]{:S(2)}, u32[]{:S(2)}) async-start(bf16[8,24,2336]{2,1,0:T(8,128)(2,1)} %constant_dynamic-update-slice_fusion), calls=%async_computation.1 | async-start | bytes 1867776 | tf_op jit(solution)/shard_map/all_to_all | solution.py:1238
  432.3 9.9 %collective-permute-start.1 = (f32[2,24,768]{2,1,0:T(8,128)S(1)}, f32[2,24,768]{2,1,0:T(8,128)}, u32[]{:S(2)}, u32[]{:S(2)}) collective-permute-start(f32[2,24,768]{2,1,0:T(8,128)S(1)} %pad_maximum_fusion.5), channel_id=1, source_target_pairs={{0,0},{1,1},{2,8},{3,9},{4,16},{5,17},{6,24},{7,25},{8,2},{9,3},{1... | collective-permute-start | bytes 442376 | tf_op jit(solution)/shard_map/ppermute | solution.py:1246
  455.2 0.8 copy-start.6
  455.2 0.8 copy-start.7
  459.5 3.8 copy-start.5
  459.5 4.5 copy-start.1

commit v4 on v3

--- a/solution.py
+++ b/solution.py
@@ -113,11 +113,26 @@
         self.across_x = (self.z, 1 - self.x, self.y, self.c)
         self.across_y = (self.z, self.x, 1 - self.y, self.c)
         self.block = 2 * self.z + self.c
+        self.member = 2 * self.g + self.c
+        self.number = 8 * self.z + self.member
+        nb = 2 * nz
+        self.chunk = self.g * nb + self.block
+        self.chunk_device = self.device(self.chunk)
+        place = self.number % nb
+        self.holder = (place // 2, self.number // nb // 2, self.number // nb % 2, place % 2)
+        self.moves = self.chunk != self.number
         self.has_left, self.has_right = self.z > 0, self.z < nz - 1
 
     def column(self, zz):
         return (zz, self.x, self.y, self.c)
 
+    def device(self, number):
+        k = number % 8
+        return (number // 8, k // 4, k // 2 % 2, k % 2)
+
+    def of_plane(self, k):
+        return (self.z, k // 4, k // 2 % 2, k % 2)
+
     def neighbours(self):
         return 3 - (self.z == 0).astype(jnp.int32) - (self.z == self.nz - 1).astype(jnp.int32)
 
@@ -132,12 +147,26 @@
         def _():
             pl.semaphore_signal(semaphore, inc=1, device_id=self.column(self.z + 1), device_id_type=MESH)
 
-    def enter(self):
+    def enter(self, plane):
         barrier = pltpu.get_barrier_semaphore()
-        for device in (self.across_x, self.across_y):
+
+        def greet(device):
             pl.semaphore_signal(barrier, inc=1, device_id=device, device_id_type=MESH)
+
+        if not plane:
+            greet(self.across_x)
+            greet(self.across_y)
+            self.signal_neighbours(barrier)
+            pl.semaphore_wait(barrier, 2 + self.neighbours())
+            return
+        loop(1, 8, lambda j: greet(self.of_plane((self.member + j) % 8)))
         self.signal_neighbours(barrier)
-        pl.semaphore_wait(barrier, 2 + self.neighbours())
+
+        @pl.when(self.moves)
+        def _():
+            greet(self.chunk_device)
+            greet(self.holder)
+        pl.semaphore_wait(barrier, 7 + self.neighbours() + 2 * self.moves.astype(jnp.int32))
 
     def positions(self, zz, cc, tokens, rows):
         row = lax.broadcasted_iota(jnp.int32, (rows, 128), 0)
@@ -407,6 +436,40 @@
             def _():
                 self.to_left(t).wait_send()
         loop(0, at.nz, drain)
+
+
+class PlaneExchange:
+    def __init__(self, at, out, inbox, send, recv, columns=None):
+        self.at, self.out, self.inbox, self.send, self.recv, self.columns = at, out, inbox, send, recv, columns
+
+    def source(self, k):
+        return self.out.at[k] if self.columns is None else self.out.at[k, :, self.columns]
+
+    def start(self):
+        at = self.at
+
+        def step(j):
+            k = (at.member + j) % 8
+            remote(self.source(k), self.inbox.at[at.member], self.send.at[k], self.recv.at[at.member], at.of_plane(k)).start()
+        loop(1, 8, step)
+        self.inbox[at.member] = self.source(at.member)[...]
+
+    def each(self, do):
+        at = self.at
+
+        def step(j):
+            k = (at.member + j) % 8
+            do(remote(self.source(k), self.inbox.at[k], self.send.at[k], self.recv.at[k], at.of_plane(k)))
+        loop(1, 8, step)
+
+    def wait(self):
+        self.each(lambda copy: copy.wait_recv())
+
+    def finish(self):
+        self.each(lambda copy: copy.wait_send())
+
+    def rows(self, count):
+        return jnp.concatenate([self.inbox[k].astype(F32)[0:count] for k in range(8)], axis=0)
 
 
 def box(tree):
@@ -581,7 +644,7 @@
     rows, half_rows = 4 * tokens, 2 * tokens
     quarter = R.hid.shape[1]
     group = R.ctx_now[0].shape[1]
-    at.enter()
+    at.enter(host)
     part = R.part
     square_sum = SquareSum(at, part, R.pair, R.single, R.ss_send, R.ss_recv)
     gather_x = [SquareGather(at, R.xr_now[l], R.x_send.at[l], R.x_recv.at[l]) for l in range(layers)]
@@ -602,20 +665,46 @@
         qkv, gu, down = [[BlockGather(at, item) for item in items] for items in (R.qkv_now, R.gu_now, R.down_now)]
         ow = BlockGather(at, R.ow_now)
         qkv_w, gu_w, down_w, out_w = [g.buf for g in qkv], [g.buf for g in gu], [g.buf for g in down], R.out_now
-        qkv[0].put(R.qkv_own[0][...])
-        qkv[0].start()
+        wrows = R.ow_now.buf.shape[2] // layers
+        lists = [qkv[l] for l in range(layers)] + [gu[l] for l in range(layers)]
+        columns, first = [], 0
+        for item in lists:
+            columns.append(pl.ds(first, item.buf.shape[3]))
+            first += item.buf.shape[3]
+        spread = [PlaneExchange(at, R.spread, R.spread_in[i], R.spread_send.at[i], R.spread_recv.at[i], columns[i])
+                  for i in range(len(lists))]
+
+        def arrive(i):
+            spread[i].wait()
+            lists[i].put(spread[i].rows(wrows).astype(BF))
+
+        to_holder = remote(R.ow_mine, R.ow_in, R.ow_send, R.ow_recv, at.holder)
+        spread[0].start()
     else:
         qkv_w, gu_w, down_w, out_w = R.qkv_given, R.gu_given, R.down_given, R.out_given
 
     R.xr_now[0][at.g] = R.x0[...]
     gather_x[0].start()
     if host:
+        spread[layers].start()
+
+        @pl.when(at.moves)
+        def _():
+            to_holder.start()
+
+        @pl.when(jnp.logical_not(at.moves))
+        def _():
+            R.ow_in[...] = R.ow_mine[...]
+        arrive(0)
+        qkv[0].start()
         for l in range(layers):
-            if l:
-                qkv[l].put(R.qkv_own[l][...])
-            gu[l].put(R.gu_own[l][...])
             down[l].put(R.down_own[l][...])
-        ow.put(R.ow_own[...])
+
+        @pl.when(at.moves)
+        def _():
+            to_holder.wait_recv()
+        ow.put(R.ow_in[...])
+        ow.start()
 
     def columns(b):
         R.kaug_now[b // 2, b % 2] = key_columns(at, R.slopes, R.seg, b // 2, b % 2, tokens)
@@ -644,7 +733,7 @@
 
     if host:
         qkv[0].serve_all()
-        ow.start()
+        arrive(layers)
         gu[0].start()
         down[0].start()
         qkv[0].collect()
@@ -664,17 +753,25 @@
             pl.semaphore_wait(R.kv_free, at.neighbours())
         kv.put((dot(x_all, side_weight(qkv_w[l], 0)) + kv_bias).astype(BF))
         kv.start()
+        if host and not last:
+            spread[l + 1].start()
+            spread[layers + l + 1].start()
         R.q[...] = (dot(x_all, side_weight(qkv_w[l], 1, 0, group)) + qb).astype(BF)
         for side in range(2):
             for h in range(3):
                 R.q_op[side, h] = query_operand(at, R.q, R.inside, R.slopes, side, h, tokens)
 
         def behind(d, l=l):
-            if host:
-                if l == 0:
-                    ow.serve(d)
+            if host and l == 0:
+                ow.serve(d)
                 gu[l].serve(d)
                 down[l].serve(d)
+
+        def ahead(d, l=l):
+            if host and l < layers - 1:
+                for p in range(d, nz if d == 3 else d + 1):
+                    gu[l + 1].serve(p)
+                    down[l + 1].serve(p)
         attention(at, kv, R.q_op, R.kaug_now, R.m, R.acc, behind)
         attention_end(at, R.q, R.inside, R.slopes, tokens, R.m, R.acc, R.ctx_now[l], R.ctxf_now[l], R.qb_now[l])
         kv_saved = save(kv.buf, R.kv[l])
@@ -692,7 +789,11 @@
                 R.out_now[i][...] = R.ow_flat[...].astype(BF)
                 save(R.out_now[i], R.out_w[i])
         if not last and host:
+            arrive(l + 1)
             qkv[l + 1].start()
+            arrive(layers + l + 1)
+            gu[l + 1].start()
+            down[l + 1].start()
         if l:
             square_sum.finish()
         for number, half in enumerate((1 - at.x, at.x)):
@@ -722,9 +823,8 @@
             if number == 1:
                 if not last and host:
                     qkv[l + 1].serve_all()
-                    gu[l + 1].start()
-                    down[l + 1].start()
                 gather_y[l].wait_far()
+                ahead(1)
             here = half_at(half)
             y_half = of(R.yr_now[l], half)
             for col in range(0, quarter, 256):
@@ -745,6 +845,7 @@
             save(gu[l].buf, R.gu_w[l])
             save(down[l].buf, R.down_w[l])
         square_sum.relay()
+        ahead(2)
         if not last and host:
             qkv[l + 1].collect()
         R.sum2_now[l][...] = R.state[...] + (square_sum.total() + small(l, 6))
@@ -757,6 +858,7 @@
             R.xr_now[l + 1][at.g] = state.astype(BF)
             gather_x[l + 1].start()
             gather_x[l + 1].wait_near()
+            ahead(3)
             gather_x[l + 1].wait_far()
     for l in range(layers):
         gather_x[l].finish()
@@ -767,6 +869,12 @@
             for item in items:
                 item.finish()
         ow.finish()
+        for item in spread:
+            item.finish()
+
+        @pl.when(at.moves)
+        def _():
+            to_holder.wait_send()
     for number, copy in enumerate(saves):
         if number not in waited:
             copy.wait()
@@ -778,7 +886,8 @@
     tokens, width = x0.shape
     group = width // 4
     each = range(layers)
-    quarter = (weights.gu_own[0].shape if host else weights.gu_given[0].shape)[-1]
+    quarter = weights.spread.shape[2] // layers - 384 if host else weights.gu_given[0].shape[3]
+    r = width // nz
     keep_rows = lambda: [keep(4, tokens, width) for _ in each]
     keep_wide = lambda: [keep(tokens, width, dtype=F32) for _ in each]
     scratch = dict(
@@ -800,14 +909,19 @@
         mixed=[shape(rows, 2 * quarter, dtype=F32) for _ in each], kaug=shape(nz, 2, rows, 128))
     near = dict(x0=x0, seg=seg, **vars(weights))
     if host:
-        gathered = lambda arrays: [shape(nz, 2, *w.shape) for w in arrays]
-        items = lambda arrays: [block_gather_item(nz, *w.shape) for w in arrays]
-        far_out.update(qkv_w=gathered(weights.qkv_own), gu_w=gathered(weights.gu_own), down_w=gathered(weights.down_own),
+        gathered = lambda *dims: [shape(nz, 2, *dims) for _ in each]
+        items = lambda *dims: [block_gather_item(nz, *dims) for _ in each]
+        rd = weights.down_own[0].shape[0]
+        padded = weights.spread.shape[1]
+        far_out.update(qkv_w=gathered(r, 384), gu_w=gathered(r, quarter), down_w=gathered(rd, width),
                        out_w=[shape(group, width) for _ in each])
         scratch.update(
-            qkv_now=items(weights.qkv_own), gu_now=items(weights.gu_own), down_now=items(weights.down_own),
-            ow_now=block_gather_item(nz, *weights.ow_own.shape), out_now=[keep(group, width) for _ in each],
-            ow_wide=keep(*weights.ow_own.shape, dtype=F32), ow_flat=keep(group, width, dtype=F32))
+            qkv_now=items(r, 384), gu_now=items(r, quarter), down_now=items(rd, width),
+            spread_in=[keep(8, padded, 384) for _ in each] + [keep(8, padded, quarter) for _ in each],
+            spread_send=copies(2 * layers, 8), spread_recv=copies(2 * layers, 8),
+            ow_in=keep(*weights.ow_mine.shape), ow_send=pltpu.SemaphoreType.DMA, ow_recv=pltpu.SemaphoreType.DMA,
+            ow_now=block_gather_item(nz, *weights.ow_mine.shape), out_now=[keep(group, width) for _ in each],
+            ow_wide=keep(*weights.ow_mine.shape, dtype=F32), ow_flat=keep(group, width, dtype=F32))
     out = dict(output=shape(tokens, width), small=shape(8 * layers, width, dtype=F32))
     done = call(functools.partial(fwd_kernel, nz, layers, host), "forward", 0, near=near, table=dict(slopes=slopes),
                 out=out, far_out=far_out, scratch=scratch)
@@ -922,7 +1036,7 @@
 
     for which in range(6):
         load(which, layers - 1).start()
-    at.enter()
+    at.enter(host)
     R.dproj[:, 576:768] = jnp.zeros((rows, 192), BF)
     gather_df = SquareGather(at, R.df, R.df_send, R.df_recv)
     gather_da = SquareGather(at, R.da, R.da_send, R.da_recv)
@@ -931,6 +1045,9 @@
     if host:
         gu_sum, dn_sum, qk_sum, ow_sum = [[BlockSum(at, item) for item in items] for items in (R.gu, R.dn, R.qk, R.ow)]
         sm_sum = BlockSum(at, R.sm)
+        back = [PlaneExchange(at, item.out, item.inbox, item.send, item.recv) for item in R.back]
+        wrows = R.out_grad.shape[1]
+        moved = [remote(R.ow_out.at[l], R.ow_in.at[l], R.ow_send.at[l], R.ow_recv.at[l], at.chunk_device) for l in range(layers)]
 
     def small(l, t):
         return R.small[8 * l + t : 8 * l + t + 1, :]
@@ -971,11 +1088,52 @@
             item.serve(p)
 
     def emit(l):
-        if host and l < layers:
-            R.gu_sum[l][...] = gu_sum[l].total().astype(BF)
-            R.dn_sum[l][...] = dn_sum[l].total()
-            R.qk_sum[l][...] = qk_sum[l].total().astype(BF)
-            R.ow_sum[l][...] = ow_sum[l].total()
+        if not host or l == layers:
+            return
+        pad = lambda v: jnp.concatenate([v, jnp.zeros((R.back[l].out.shape[1] - wrows, v.shape[1]), F32)], axis=0).astype(BF)
+        for item, lo in ((gu_sum[l], 0), (qk_sum[l], quarter)):
+            v = item.total()
+            for k in range(8):
+                R.back[l].out[k, :, lo : lo + v.shape[1]] = pad(v[wrows * k : wrows * k + wrows])
+        back[l].start()
+        R.dn_grad[l] = dn_sum[l].total()
+        R.ow_out[l] = ow_sum[l].total()
+
+        @pl.when(at.moves)
+        def _():
+            moved[l].start()
+
+        @pl.when(jnp.logical_not(at.moves))
+        def _():
+            R.ow_in[l] = R.ow_out[l]
+
+    def assemble(l):
+        back[l].wait()
+        piece = [R.back[l].inbox[k].astype(F32)[0:wrows] for k in range(8)]
+        join = lambda side, *spans: jnp.concatenate(
+            [piece[2 * g + side][:, lo:hi] for g in range(4) for lo, hi in spans], axis=1)
+        at_kv = quarter
+        R.qkv_grad[l, :, 0:width] = join(1, (at_kv, at_kv + 192))
+        R.qkv_grad[l, :, width : 2 * width] = join(0, (at_kv, at_kv + 128), (at_kv + 256, at_kv + 320))
+        R.qkv_grad[l, :, 2 * width : 3 * width] = join(0, (at_kv + 128, at_kv + 256), (at_kv + 320, at_kv + 384))
+        step = quarter // nz
+        for side in range(2):
+            for zz in range(nz):
+                lo = (side * nz + zz) * 4 * step
+                R.gu_grad[l, :, lo : lo + 4 * step] = join(side, (step * zz, step * zz + step))
+
+        @pl.when(at.moves)
+        def _():
+            moved[l].wait_recv()
+        R.out_grad[l] = R.ow_in[l, 0:wrows, :]
+
+    def small_copy(j):
+        k = 4 * at.c + j
+        return remote(R.sm_out, R.sm_in.at[at.g], R.sm_send.at[j], R.sm_recv.at[at.g], at.of_plane(k)), k != at.member
+
+    def small_from(g):
+        k = 2 * g + at.x
+        return remote(R.sm_out, R.sm_in.at[g], R.sm_send.at[0], R.sm_recv.at[g], at.of_plane(k)), k != at.member
 
     R.g[...] = R.grad[...].astype(F32)
     for l in reversed(range(layers)):
@@ -1111,11 +1269,48 @@
         sm_sum.serve(0)
         for p in range(1, nz - 1):
             serve(last, p)
-        R.sm_sum[...] = sm_sum.total()
+        R.sm_out[...] = sm_sum.total()
+        for j in range(4):
+            copy, away = small_copy(j)
+
+            @pl.when(away)
+            def _(copy=copy):
+                copy.start()
+
+            @pl.when(jnp.logical_not(away))
+            def _():
+                R.sm_in[at.g] = R.sm_out[...]
         emit(0)
+        for l in range(1, layers):
+            assemble(l)
+        total = jnp.zeros(R.sm_out.shape, F32)
+        for g in range(4):
+            copy, away = small_from(g)
+
+            @pl.when(away)
+            def _(copy=copy):
+                copy.wait_recv()
+            total = total + R.sm_in[g]
+        mine = jnp.zeros((8 * layers, wrows), F32)
+        for k in range(4):
+            mine = jnp.where(2 * at.y + at.c == k, total[:, wrows * k : wrows * k + wrows], mine)
         for l in range(layers):
-            for item in feed_forward_sums(l) + attention_sums(l):
+            R.gains_grad[l] = mine[8 * l : 8 * l + 2]
+            R.biases_grad[l] = jnp.concatenate([mine[8 * l + 6 : 8 * l + 8], mine[8 * l + 2 : 8 * l + 6]], axis=0)
+        assemble(0)
+        for l in range(layers):
+            for item in feed_forward_sums(l) + attention_sums(l) + (back[l],):
                 item.finish()
+
+            @pl.when(at.moves)
+            def _(l=l):
+                moved[l].wait_send()
+        for j in range(4):
+            copy, away = small_copy(j)
+
+            @pl.when(away)
+            def _(copy=copy):
+                copy.wait_send()
         sm_sum.finish()
 
 
@@ -1130,10 +1325,17 @@
     out = dict(grad_in=shape(tokens, width, dtype=F32))
     scratch = {}
     if host:
+        wrows, padded = width // (8 * nz), 32
         out.update(
-            gu_sum=[shape(r, quarter) for _ in each], dn_sum=[shape(rd, width, dtype=F32) for _ in each],
-            qk_sum=[shape(r, 384) for _ in each], ow_sum=[shape(OW_ROWS, width, dtype=F32) for _ in each],
-            sm_sum=shape(8 * layers, 128, dtype=F32))
+            qkv_grad=shape(layers, wrows, 3 * width, dtype=F32), out_grad=shape(layers, wrows, width, dtype=F32),
+            gu_grad=shape(layers, wrows, 8 * quarter, dtype=F32), dn_grad=shape(layers, rd, width, dtype=F32),
+            gains_grad=shape(layers, 2, wrows, dtype=F32), biases_grad=shape(layers, 6, wrows, dtype=F32))
+        scratch.update(
+            back=[dict(out=keep(8, padded, quarter + 384), inbox=keep(8, padded, quarter + 384), send=copies(8), recv=copies(8))
+                  for _ in each],
+            ow_out=keep(layers, OW_ROWS, width, dtype=F32), ow_in=keep(layers, OW_ROWS, width, dtype=F32),
+            ow_send=copies(layers), ow_recv=copies(layers),
+            sm_out=keep(8 * layers, 128, dtype=F32), sm_in=keep(4, 8 * layers, 128, dtype=F32), sm_send=copies(4), sm_recv=copies(4))
         scratch.update(
             gu=[block_sum_item(nz, r, quarter) for _ in each], dn=[block_sum_item(nz, rd, width) for _ in each],
             qk=[block_sum_item(nz, r, 384) for _ in each], ow=[block_sum_item(nz, OW_ROWS, width) for _ in each],
@@ -1184,6 +1386,19 @@
         v = jnp.stack([kv[:, :, 2], kv[:, :, 3], kv[:, :, 5]], axis=2)
         return jnp.stack([q, k, v]).transpose(2, 0, 1, 3, 4).reshape(wrows, 3 * width)
 
+    places = [(8 * zz + 2 * g + cc, g * nb + 2 * zz + cc) for zz in range(nz) for g in range(4) for cc in range(2)]
+    gu0 = 384 * layers
+
+    def gathered_outside(both, out_weight, down_weight):
+        spread = lax.all_to_all(both, square, split_axis=1, concat_axis=0, tiled=True).reshape(8 * wrows, -1)
+        ow_own = lax.ppermute(out_weight, everyone, [(chunk, device) for device, chunk in places])
+        whole = lambda v: lax.all_gather(v, blocks, axis=0).reshape(nz, 2, *v.shape)
+        flat = lambda v: lax.all_gather(v, blocks, axis=0, tiled=True)
+        return types.SimpleNamespace(
+            qkv_given=[whole(spread[:, 384 * l : 384 * l + 384]) for l in range(layers)],
+            gu_given=[whole(spread[:, gu0 + quarter * l : gu0 + quarter * l + quarter]) for l in range(layers)],
+            down_given=[flat(down_weight[l]) for l in range(layers)], out_given=[flat(ow_own[l]) for l in range(layers)])
+
     small = jnp.concatenate([gains, biases], axis=1).transpose(0, 2, 1)
     small = jnp.concatenate([small[l] for l in range(layers)], axis=1)
     small = jnp.pad(small, ((0, 0), (0, 192 - small.shape[1])))
@@ -1199,36 +1414,26 @@
         for side in range(2):
             sides[side].append(gu[l, :, :, side])
     both = jnp.stack([jnp.concatenate(side, axis=2) for side in sides], axis=2).reshape(wrows, 8, -1)
-    spread = lax.all_to_all(both, square, split_axis=1, concat_axis=0, tiled=True).reshape(8 * wrows, -1)
-    qkv_own = [spread[:, 384 * l : 384 * l + 384] for l in range(layers)]
-    gu0 = 384 * layers
-    gu_own = [spread[:, gu0 + quarter * l : gu0 + quarter * l + quarter] for l in range(layers)]
-    places = [(8 * zz + 2 * g + cc, g * nb + 2 * zz + cc) for zz in range(nz) for g in range(4) for cc in range(2)]
-    ow_own = lax.ppermute(out_weight, everyone, [(chunk, device) for device, chunk in places])
     if host:
-        weights = types.SimpleNamespace(qkv_own=qkv_own, gu_own=gu_own, down_own=[down_weight[l] for l in range(layers)],
-                                        ow_own=ow_own.reshape(layers * wrows, width))
+        spread = jnp.pad(both.transpose(1, 0, 2), ((0, 0), (0, 32 - wrows), (0, 0)))
+        weights = types.SimpleNamespace(
+            spread=spread, down_own=[down_weight[l] for l in range(layers)], ow_mine=out_weight.reshape(layers * wrows, width))
     else:
-        whole = lambda v: lax.all_gather(v, blocks, axis=0).reshape(nz, 2, *v.shape)
-        flat = lambda v: lax.all_gather(v, blocks, axis=0, tiled=True)
-        weights = types.SimpleNamespace(
-            qkv_given=[whole(v) for v in qkv_own], gu_given=[whole(v) for v in gu_own],
-            down_given=[flat(down_weight[l]) for l in range(layers)], out_given=[flat(ow_own[l]) for l in range(layers)])
+        weights = gathered_outside(both, out_weight, down_weight)
 
     seg = segment_ids.reshape(nz, 4, 2, tokens).transpose(0, 2, 1, 3).reshape(nb, 1, 4 * tokens)
     saved = fwd(hidden_in, alibi_slopes, seg, weights, layers, host)
     done = bwd(out_grad, saved, host)
-
+    if host:
+        return (saved.output, done.grad_in, done.qkv_grad, done.out_grad, done.gu_grad, done.dn_grad, done.gains_grad,
+                done.biases_grad)
     step = width // nb
-    if host:
-        sm = done.sm_sum[:, :step]
-    else:
-        blocks_sum = lambda v: lax.psum_scatter(v, blocks, scatter_dimension=0, tiled=True)
-        done.gu_sum = [blocks_sum(item.stage.reshape(nb, -1, quarter))[0] for item in done.gu]
-        done.qk_sum = [blocks_sum(item.stage.reshape(nb, -1, 384))[0] for item in done.qk]
-        done.dn_sum = [blocks_sum(item.stage) for item in done.dn]
-        done.ow_sum = [blocks_sum(item.stage) for item in done.ow]
-        sm = lax.psum_scatter(done.tok_small.reshape(-1, nb, step), blocks, scatter_dimension=1, tiled=True)[:, 0]
+    blocks_sum = lambda v: lax.psum_scatter(v, blocks, scatter_dimension=0, tiled=True)
+    done.gu_sum = [blocks_sum(item.stage.reshape(nb, -1, quarter))[0] for item in done.gu]
+    done.qk_sum = [blocks_sum(item.stage.reshape(nb, -1, 384))[0] for item in done.qk]
+    done.dn_sum = [blocks_sum(item.stage) for item in done.dn]
+    done.ow_sum = [blocks_sum(item.stage) for item in done.ow]
+    sm = lax.psum_scatter(done.tok_small.reshape(-1, nb, step), blocks, scatter_dimension=1, tiled=True)[:, 0]
     sm = sm.T.reshape(4, wrows, 8 * layers)
     high = lax.reduce_precision(sm, 8, 7)
     sm = jnp.concatenate([high, sm - high], axis=2).astype(BF)

time: 471 us -> 431 us (0.915)
  the two profiles are of different devices: /device:TPU:14 before, /device:TPU:21 now
where the time goes in v4:
time: 431 us; the launch traced here: 427 us
  Pallas kernels  408 us (95%)
  local copies, waits for them, and re-layouts  16.8 us (4%)
    pallas_call x2, Pallas kernels, call(): pl.pallas_call(kernel, out_shape=tuple(flat[3]) + tuple(flat[4]), in_spec...  408 us
    unnamed x26, local copies, waits for them, and re-layouts  8.88 us

profile of v4, /device:TPU:21, one launch (start us, length us, event | category | flops | bytes accessed | tf_op | source)
XLA Modules:
  0.0 427.0 jit_solution(12023120235336694387)
XLA Ops:
  0.6 0.7 copy.37
  1.3 0.7 maximum_bitcast_fusion.1
  2.1 1.3 copy.30
  3.5 1.0 fusion
  4.4 0.2 reshape_squeeze.13
  5.1 0.3 pad_maximum_fusion.2
  5.6 0.2 reshape_squeeze.12
  6.3 0.3 pad_maximum_fusion.1
  6.7 0.7 slice_bitcast_fusion.4
  7.5 0.9 reshape.64
  8.4 0.3 copy.35
  8.8 0.7 reshape.65
  9.8 1.1 pad.9.refs_4_
  10.9 181.0 %forward.1 = (bf16[128,768]{1,0:T(8,128)(2,1)}, f32[16,768]{1,0:T(8,128)}, bf16[512,192]{1,0:T(8,128)(2,1)}, bf16[512,192]{1,0:T(8,128)(2,1)}, f32[512,192]{1,0:...) custom-call(bf16[96,768]{1,0:T(8,128)(2,1)} %get-tuple-element.107.r, ...), custom_call_target="tpu_custom_call" | custom-call | flops 99999997952 | bytes 200000000 | tf_op jit(solution)/shard_map/forward/pallas_call | solution.py:494
  191.9 226.7 %backward.1 = (f32[2,6,24]{2,1,0:T(8,128)}, f32[2,96,768]{2,1,0:T(8,128)}, f32[2,2,24]{2,1,0:T(2,128)}, f32[128,768]{1,0:T(8,128)}, f32[2,24,6144]{2,1,0:T(8,128...) custom-call(bf16[512,192]{1,0:T(8,128)(2,1)} %get-tuple-element.45.refs_0_, ...), custom_call_target="tpu_custom_call" | custom-call | flops 99999997952 | bytes 200000000 | tf_op jit(solution)/shard_map/backward/pallas_call | solution.py:494
  418.6 1.4 copy.41
  420.0 0.7 copy.56
  420.6 1.8 copy.57
  422.4 0.8 copy.58
  423.2 0.7 copy.59
  423.8 1.0 copy.60
  424.9 0.5 copy-done.1
  425.3 0.8 copy.61
  426.1 0.6 copy.62
  (43 shorter events, 1.6 us)
Async XLA Ops:
  5.6 1.2 copy-start.4
  5.8 1.7 copy-start.2
  191.9 228.1 %copy-start.5 = (bf16[128,768]{1,0:T(8,128)(2,1)S(1)}, bf16[128,768]{1,0:T(8,128)(2,1)}, u32[]{:S(2)}) copy-start(bf16[128,768]{1,0:T(8,128)(2,1)} %get-tuple-element.120) | copy-start | bytes 589828
  418.6 3.8 copy-start.3
  418.6 4.6 %copy-start.6 = (f32[2,24,768]{2,1,0:T(8,128)S(1)}, f32[2,24,768]{2,1,0:T(8,128)}, u32[]{:S(2)}) copy-start(f32[2,24,768]{2,1,0:T(8,128)} %get-tuple-element.123) | copy-start | bytes 442372
  420.0 3.9 copy-start
  423.8 1.5 copy-start.1
  425.3 0.8 copy-start.7

commit v5 on v4

--- a/solution.py
+++ b/solution.py
@@ -157,8 +157,7 @@
             greet(self.across_x)
             greet(self.across_y)
             self.signal_neighbours(barrier)
-            pl.semaphore_wait(barrier, 2 + self.neighbours())
-            return
+            return lambda: pl.semaphore_wait(barrier, 2 + self.neighbours())
         loop(1, 8, lambda j: greet(self.of_plane((self.member + j) % 8)))
         self.signal_neighbours(barrier)
 
@@ -166,7 +165,7 @@
         def _():
             greet(self.chunk_device)
             greet(self.holder)
-        pl.semaphore_wait(barrier, 7 + self.neighbours() + 2 * self.moves.astype(jnp.int32))
+        return lambda: pl.semaphore_wait(barrier, 7 + self.neighbours() + 2 * self.moves.astype(jnp.int32))
 
     def positions(self, zz, cc, tokens, rows):
         row = lax.broadcasted_iota(jnp.int32, (rows, 128), 0)
@@ -177,39 +176,41 @@
     def __init__(self, at, buf, send, recv):
         half = buf.shape[1] // 2
         first, second = pl.ds(0, half), pl.ds(half, half)
-        own = buf.at[at.g]
-        self.to_x = remote(own, own, send.at[0], recv.at[0], at.across_x)
-        self.to_y = remote(own, own, send.at[1], recv.at[1], at.across_y)
-        self.on_y = remote(buf.at[at.gx, first], buf.at[at.gx, first], send.at[2], recv.at[2], at.across_y)
-        self.on_x = remote(buf.at[at.gy, second], buf.at[at.gy, second], send.at[3], recv.at[3], at.across_x)
+
+        def copy(i, g, rows, device):
+            return remote(buf.at[g, rows], buf.at[g, rows], send.at[i], recv.at[i], device)
+        self.x_first, self.x_second = copy(0, at.g, first, at.across_x), copy(1, at.g, second, at.across_x)
+        self.y_second, self.y_first = copy(2, at.g, second, at.across_y), copy(3, at.g, first, at.across_y)
+        self.on_y = copy(4, at.gx, first, at.across_y)
+        self.on_x = copy(5, at.gy, second, at.across_x)
 
     def start(self):
-        self.to_x.start()
-        self.to_y.start()
+        for copy in (self.x_first, self.y_second, self.x_second, self.y_first):
+            copy.start()
 
     def wait_near(self):
-        self.to_x.wait_recv()
+        self.x_first.wait_recv()
         self.on_y.start()
-        self.to_y.wait_recv()
+        self.y_second.wait_recv()
         self.on_x.start()
+        self.y_first.wait_recv()
 
     def wait_far(self):
+        self.x_second.wait_recv()
         self.on_x.wait_recv()
         self.on_y.wait_recv()
 
     def finish(self):
-        for copy in (self.to_x, self.to_y, self.on_x, self.on_y):
+        for copy in (self.x_first, self.x_second, self.y_first, self.y_second, self.on_x, self.on_y):
             copy.wait_send()
 
 
 class SquareSum:
-    def __init__(self, at, part, pair, single, send, recv):
-        self.at, self.part = at, part
-        self.pair, self.single = pair, single
+    def __init__(self, at, part, stage, inbox, send, recv):
+        self.at, self.part, self.stage, self.inbox = at, part, stage, inbox
         self.half = part.shape[2] // 2
-        to = (at.across_x, at.across_y, at.across_y, at.across_y, at.across_x)
-        refs = [(pair.stage, pair.inbox)] + [(single.stage.at[i], single.inbox.at[i]) for i in range(4)]
-        self.copies = [remote(refs[i][0], refs[i][1], send.at[i], recv.at[i], to[i]) for i in range(5)]
+        to = (at.across_x, at.across_x, at.across_y, at.across_y, at.across_y, at.across_x)
+        self.copies = [remote(stage.at[i], inbox.at[i], send.at[i], recv.at[i], to[i]) for i in range(6)]
 
     def left(self, g):
         return self.part[g, :, : self.half]
@@ -217,35 +218,30 @@
     def right(self, g):
         return self.part[g, :, self.half :]
 
+    def post(self, i, value):
+        self.stage[i] = value.astype(BF)
+        self.copies[i].start()
+
+    def came(self, i):
+        self.copies[i].wait_recv()
+        return self.inbox[i].astype(F32)
+
     def send_far(self):
-        at = self.at
-        self.pair.stage[...] = self.part[pl.ds(2 * (1 - at.x), 2), :, : self.half].astype(BF)
-        self.copies[0].start()
-        self.single.stage[1] = self.right(at.gd).astype(BF)
-        self.copies[2].start()
+        self.post(0, self.left(self.at.gd))
+        self.post(2, self.right(self.at.gd))
+        self.post(1, self.left(self.at.gx))
 
     def send_near(self):
-        self.single.stage[0] = self.right(self.at.gy).astype(BF)
-        self.copies[1].start()
+        self.post(3, self.right(self.at.gy))
 
     def relay(self):
-        at = self.at
-        self.copies[0].wait_recv()
-        self.single.stage[2] = (self.left(at.gy) + self.pair.inbox[1 - at.y].astype(F32)).astype(BF)
-        self.copies[3].start()
-        self.copies[2].wait_recv()
-        self.single.stage[3] = (self.right(at.gx) + self.single.inbox[1].astype(F32)).astype(BF)
-        self.copies[4].start()
+        self.post(4, self.left(self.at.gy) + self.came(0))
+        self.post(5, self.right(self.at.gx) + self.came(2))
 
     def total(self):
-        at = self.at
-        self.copies[1].wait_recv()
-        left = self.left(at.g) + self.pair.inbox[at.y].astype(F32)
-        right = self.right(at.g) + self.single.inbox[0].astype(F32)
-        self.copies[3].wait_recv()
-        self.copies[4].wait_recv()
-        return jnp.concatenate(
-            [left + self.single.inbox[2].astype(F32), right + self.single.inbox[3].astype(F32)], axis=1)
+        left = self.left(self.at.g) + self.came(1)
+        right = self.right(self.at.g) + self.came(3)
+        return jnp.concatenate([left + self.came(4), right + self.came(5)], axis=1)
 
     def finish(self):
         for copy in self.copies:
@@ -521,9 +517,7 @@
 
 def square_sum_items(tokens, width):
     half = width // 2
-    return dict(
-        pair=dict(stage=keep(2, tokens, half), inbox=keep(2, tokens, half)),
-        single=dict(stage=keep(4, tokens, half), inbox=keep(4, tokens, half)), ss_send=copies(5), ss_recv=copies(5))
+    return dict(ss_stage=keep(6, tokens, half), ss_inbox=keep(6, tokens, half), ss_send=copies(6), ss_recv=copies(6))
 
 
 def flat_weight(ref, lo=0, hi=None):
@@ -543,12 +537,16 @@
                 csend=copies(nz), crecv=copies(nz), zsend=copies(nz), zrecv=copies(nz + 1))
 
 
+def segment_row(seg, zz, cc):
+    return jnp.concatenate([seg[pl.ds(zz * 8 + 2 * k + cc, 1), :] for k in range(4)], axis=1)
+
+
 def key_columns(at, slopes, seg, zz, cc, tokens):
     rows = 4 * tokens
     column = lax.broadcasted_iota(jnp.int32, (128, rows), 0) % 64
     row = lax.broadcasted_iota(jnp.int32, (128, rows), 1)
     position = ((zz * 8 + (row // tokens) * 2 + cc) * tokens + row % tokens).astype(F32)
-    value = jnp.where(seg[2 * zz + cc] == column - SEGMENT_LANE, 0.0, -1e30)
+    value = jnp.where(segment_row(seg, zz, cc) == column - SEGMENT_LANE, 0.0, -1e30)
     value = jnp.where(column < SEGMENT_LANE + 5, value, 0.0)
     value = jnp.where(column < SEGMENT_LANE, 1.0, value)
     for h in range(3):
@@ -559,7 +557,7 @@
 
 def segment_columns(at, seg, rows):
     column = lax.broadcasted_iota(jnp.int32, (128, rows), 0) % 64
-    return jnp.where(seg[at.block] == column - SEGMENT_LANE, 1.0, 0.0).T
+    return jnp.where(segment_row(seg, at.z, at.c) == column - SEGMENT_LANE, 1.0, 0.0).T
 
 
 def query_operand(at, q_ref, inside, slopes, side, h, tokens, lse=None):
@@ -644,9 +642,9 @@
     rows, half_rows = 4 * tokens, 2 * tokens
     quarter = R.hid.shape[1]
     group = R.ctx_now[0].shape[1]
-    at.enter(host)
+    arrived = at.enter(host)
     part = R.part
-    square_sum = SquareSum(at, part, R.pair, R.single, R.ss_send, R.ss_recv)
+    square_sum = SquareSum(at, part, R.ss_stage, R.ss_inbox, R.ss_send, R.ss_recv)
     gather_x = [SquareGather(at, R.xr_now[l], R.x_send.at[l], R.x_recv.at[l]) for l in range(layers)]
     gather_y = [SquareGather(at, R.yr_now[l], R.y_send.at[l], R.y_recv.at[l]) for l in range(layers)]
     kv = BlockGather(at, R.kv_now)
@@ -678,9 +676,31 @@
             spread[i].wait()
             lists[i].put(spread[i].rows(wrows).astype(BF))
 
+        def regroup():
+            join = lambda *parts: jnp.concatenate(parts, axis=1)
+            part_width = quarter // nz
+            for l in range(layers):
+                w = R.qkv_mine[l].astype(F32)
+                for g in range(4):
+                    q, k, v = [w[:, part * 4 * group + group * g : part * 4 * group + group * g + group] for part in range(3)]
+                    beside = jnp.zeros(q.shape, F32) if l else R.small_mine[...].astype(F32)
+                    at_l = 384 * l
+                    R.spread[2 * g, 0:wrows, at_l : at_l + 384] = join(k[:, :128], v[:, :128], k[:, 128:], v[:, 128:]).astype(BF)
+                    R.spread[2 * g + 1, 0:wrows, at_l : at_l + 384] = join(q, beside).astype(BF)
+            for l in range(layers):
+                w = R.gu_mine[l].astype(F32)
+                lo = 384 * layers + quarter * l
+                for g in range(4):
+                    for side in range(2):
+                        firsts = [((side * nz + zz) * 4 + g) * part_width for zz in range(nz)]
+                        R.spread[2 * g + side, 0:wrows, lo : lo + quarter] = join(*[w[:, i : i + part_width] for i in firsts]).astype(BF)
+
+        regroup()
+        arrived()
         to_holder = remote(R.ow_mine, R.ow_in, R.ow_send, R.ow_recv, at.holder)
         spread[0].start()
     else:
+        arrived()
         qkv_w, gu_w, down_w, out_w = R.qkv_given, R.gu_given, R.down_given, R.out_given
 
     R.xr_now[0][at.g] = R.x0[...]
@@ -698,7 +718,7 @@
         arrive(0)
         qkv[0].start()
         for l in range(layers):
-            down[l].put(R.down_own[l][...])
+            down[l].put(R.down_mine[l])
 
         @pl.when(at.moves)
         def _():
@@ -881,18 +901,18 @@
 
 
 def fwd(x0, slopes, seg, weights, layers, host):
-    nb, _, rows = seg.shape
-    nz = nb // 2
+    nz = seg.shape[0] // 8
     tokens, width = x0.shape
+    rows = 4 * tokens
     group = width // 4
     each = range(layers)
-    quarter = weights.spread.shape[2] // layers - 384 if host else weights.gu_given[0].shape[3]
+    quarter = weights.gu_mine.shape[2] // 8 if host else weights.gu_given[0].shape[3]
     r = width // nz
     keep_rows = lambda: [keep(4, tokens, width) for _ in each]
     keep_wide = lambda: [keep(tokens, width, dtype=F32) for _ in each]
     scratch = dict(
-        xr_now=keep_rows(), x_send=copies(layers, 4), x_recv=copies(layers, 4),
-        yr_now=keep_rows(), y_send=copies(layers, 4), y_recv=copies(layers, 4),
+        xr_now=keep_rows(), x_send=copies(layers, 6), x_recv=copies(layers, 6),
+        yr_now=keep_rows(), y_send=copies(layers, 6), y_recv=copies(layers, 6),
         part=keep(4, tokens, width, dtype=F32), state=keep(tokens, width, dtype=F32), **square_sum_items(tokens, width),
         kv_now=block_gather_item(nz, rows, 384), kv_free=pltpu.SemaphoreType.REGULAR, saved=copies(16 * layers),
         kaug_now=keep(nz, 2, rows, 128), inside=keep(rows, 128, dtype=F32),
@@ -911,13 +931,13 @@
     if host:
         gathered = lambda *dims: [shape(nz, 2, *dims) for _ in each]
         items = lambda *dims: [block_gather_item(nz, *dims) for _ in each]
-        rd = weights.down_own[0].shape[0]
-        padded = weights.spread.shape[1]
+        rd = weights.down_mine.shape[1]
+        padded = 32
         far_out.update(qkv_w=gathered(r, 384), gu_w=gathered(r, quarter), down_w=gathered(rd, width),
                        out_w=[shape(group, width) for _ in each])
         scratch.update(
             qkv_now=items(r, 384), gu_now=items(r, quarter), down_now=items(rd, width),
-            spread_in=[keep(8, padded, 384) for _ in each] + [keep(8, padded, quarter) for _ in each],
+            spread=keep(8, padded, layers * (384 + quarter)), spread_in=[keep(8, padded, 384) for _ in each] + [keep(8, padded, quarter) for _ in each],
             spread_send=copies(2 * layers, 8), spread_recv=copies(2 * layers, 8),
             ow_in=keep(*weights.ow_mine.shape), ow_send=pltpu.SemaphoreType.DMA, ow_recv=pltpu.SemaphoreType.DMA,
             ow_now=block_gather_item(nz, *weights.ow_mine.shape), out_now=[keep(group, width) for _ in each],
@@ -1036,12 +1056,12 @@
 
     for which in range(6):
         load(which, layers - 1).start()
-    at.enter(host)
+    at.enter(host)()
     R.dproj[:, 576:768] = jnp.zeros((rows, 192), BF)
     gather_df = SquareGather(at, R.df, R.df_send, R.df_recv)
     gather_da = SquareGather(at, R.da, R.da_send, R.da_recv)
     part = R.part
-    square_sum = SquareSum(at, part, R.pair, R.single, R.ss_send, R.ss_recv)
+    square_sum = SquareSum(at, part, R.ss_stage, R.ss_inbox, R.ss_send, R.ss_recv)
     if host:
         gu_sum, dn_sum, qk_sum, ow_sum = [[BlockSum(at, item) for item in items] for items in (R.gu, R.dn, R.qk, R.ow)]
         sm_sum = BlockSum(at, R.sm)
@@ -1349,8 +1369,8 @@
     scratch.update(
         mixed_now=like(saved.mixed), yr_now=like(saved.yr), xr_now=like(saved.xr), gu_now=like(saved.gu_w),
         down_now=like(saved.down_w), qkv_now=like(saved.qkv_w), load=copies(6), kvbuf=keep(2, rows, 384), augbuf=keep(2, rows, 128), kvsem=copies(2, 2),
-        df=keep(4, tokens, width), df_send=copies(4), df_recv=copies(4),
-        da=keep(4, tokens, width), da_send=copies(4), da_recv=copies(4),
+        df=keep(4, tokens, width), df_send=copies(6), df_recv=copies(6),
+        da=keep(4, tokens, width), da_send=copies(6), da_recv=copies(6),
         part=keep(4, tokens, width, dtype=F32), **square_sum_items(tokens, width),
         g=keep(tokens, width, dtype=F32), e1=keep(tokens, width, dtype=F32), e2=keep(tokens, width, dtype=F32),
         hid=keep(rows, quarter), dgu=keep(rows, 2 * quarter), do=keep(3, rows, 128),
@@ -1389,7 +1409,20 @@
     places = [(8 * zz + 2 * g + cc, g * nb + 2 * zz + cc) for zz in range(nz) for g in range(4) for cc in range(2)]
     gu0 = 384 * layers
 
-    def gathered_outside(both, out_weight, down_weight):
+    def gathered_outside():
+        beside = jnp.broadcast_to(small[:, None], (wrows, 4, 192))
+        nothing = jnp.zeros((wrows, 4, 192), BF)
+        gu = gate_up_weight.reshape(layers, wrows, 2, nz, 4, quarter // nz).transpose(0, 1, 4, 2, 3, 5)
+        gu = gu.reshape(layers, wrows, 4, 2, quarter)
+        sides = [[], []]
+        for l in range(layers):
+            kv, q = to_groups(qkv_weight[l])
+            sides[0].append(kv)
+            sides[1] += [q, nothing if l else beside]
+        for l in range(layers):
+            for side in range(2):
+                sides[side].append(gu[l, :, :, side])
+        both = jnp.stack([jnp.concatenate(side, axis=2) for side in sides], axis=2).reshape(wrows, 8, -1)
         spread = lax.all_to_all(both, square, split_axis=1, concat_axis=0, tiled=True).reshape(8 * wrows, -1)
         ow_own = lax.ppermute(out_weight, everyone, [(chunk, device) for device, chunk in places])
         whole = lambda v: lax.all_gather(v, blocks, axis=0).reshape(nz, 2, *v.shape)
@@ -1402,26 +1435,13 @@
     small = jnp.concatenate([gains, biases], axis=1).transpose(0, 2, 1)
     small = jnp.concatenate([small[l] for l in range(layers)], axis=1)
     small = jnp.pad(small, ((0, 0), (0, 192 - small.shape[1])))
-    small = jnp.broadcast_to(small[:, None], (wrows, 4, 192))
-    nothing = jnp.zeros((wrows, 4, 192), BF)
-    gu = gate_up_weight.reshape(layers, wrows, 2, nz, 4, quarter // nz).transpose(0, 1, 4, 2, 3, 5).reshape(layers, wrows, 4, 2, quarter)
-    sides = [[], []]
-    for l in range(layers):
-        kv, q = to_groups(qkv_weight[l])
-        sides[0].append(kv)
-        sides[1] += [q, nothing if l else small]
-    for l in range(layers):
-        for side in range(2):
-            sides[side].append(gu[l, :, :, side])
-    both = jnp.stack([jnp.concatenate(side, axis=2) for side in sides], axis=2).reshape(wrows, 8, -1)
     if host:
-        spread = jnp.pad(both.transpose(1, 0, 2), ((0, 0), (0, 32 - wrows), (0, 0)))
         weights = types.SimpleNamespace(
-            spread=spread, down_own=[down_weight[l] for l in range(layers)], ow_mine=out_weight.reshape(layers * wrows, width))
+            qkv_mine=qkv_weight, gu_mine=gate_up_weight, down_mine=down_weight, small_mine=small,
+            ow_mine=out_weight.reshape(layers * wrows, width))
     else:
-        weights = gathered_outside(both, out_weight, down_weight)
-
-    seg = segment_ids.reshape(nz, 4, 2, tokens).transpose(0, 2, 1, 3).reshape(nb, 1, 4 * tokens)
+        weights = gathered_outside()
+    seg = segment_ids.reshape(8 * nz, tokens)
     saved = fwd(hidden_in, alibi_slopes, seg, weights, layers, host)
     done = bwd(out_grad, saved, host)
     if host:

time: 431 us -> 403 us (0.935)
  Pallas kernels: 408 us -> 384 us
  local copies, waits for them, and re-layouts: 16.8 us -> 11.2 us
    pallas_call x2, Pallas kernels: 408 us -> 384 us  [call(): pl.pallas_call(kernel, out_shape=tuple(flat[3]) + tuple(flat[4]), in_spec...]
    unnamed x26 -> x18, local copies, waits for them, and re-layouts: 8.88 us -> 11.2 us
where the time goes in v5:
time: 403 us; the launch traced here: 397 us
  Pallas kernels  384 us (95%)
  local copies, waits for them, and re-layouts  11.2 us (3%)
    pallas_call x2, Pallas kernels, call(): pl.pallas_call(kernel, out_shape=tuple(flat[3]) + tuple(flat[4]), in_spec...  384 us
    unnamed x18, local copies, waits for them, and re-layouts  11.2 us

profile of v5, /device:TPU:21, one launch (start us, length us, event | category | flops | bytes accessed | tf_op | source)
XLA Modules:
  0.0 396.8 jit_solution(8623441016237578239)
XLA Ops:
  0.6 0.8 copy.24
  1.4 0.8 copy.25
  2.2 0.1 maximum_bitcast_fusion
  2.3 0.7 fusion.2.refs_5_
  3.0 173.7 %forward.1 = (bf16[128,768]{1,0:T(8,128)(2,1)}, f32[16,768]{1,0:T(8,128)}, bf16[512,192]{1,0:T(8,128)(2,1)}, bf16[512,192]{1,0:T(8,128)(2,1)}, f32[512,192]{1,0:...) custom-call(bf16[2,96,768]{2,1,0:T(8,128)(2,1)} %refs_0_.1, ...), custom_call_target="tpu_custom_call" | custom-call | flops 99999997952 | bytes 200000000 | tf_op jit(solution)/shard_map/forward/pallas_call | solution.py:490
  176.7 0.0 copy-start.2
  176.7 210.2 %backward.1 = (f32[2,6,24]{2,1,0:T(8,128)}, f32[2,96,768]{2,1,0:T(8,128)}, f32[2,2,24]{2,1,0:T(2,128)}, f32[128,768]{1,0:T(8,128)}, f32[2,24,6144]{2,1,0:T(8,128...) custom-call(bf16[512,192]{1,0:T(8,128)(2,1)} %get-tuple-element.45.refs_0_, ...), custom_call_target="tpu_custom_call" | custom-call | flops 99999997952 | bytes 200000000 | tf_op jit(solution)/shard_map/backward/pallas_call | solution.py:490
  386.9 0.0 copy-start
  386.9 1.4 copy.26
  388.3 0.0 copy-done.2
  388.3 0.0 copy-start.1
  388.3 0.7 copy.34
  389.0 1.8 copy.35
  390.8 0.0 copy-start.3
  390.8 1.8 copy.36
  392.6 1.6 copy.37
  394.2 0.0 copy-done
  394.2 1.0 copy.38
  395.2 0.0 copy-done.1
  395.2 0.8 copy.39
  396.0 0.0 copy-done.3
  396.0 0.6 copy.40
  (1 shorter events, 0.0 us)
Async XLA Ops:
  176.7 211.6 %copy-start.2 = (bf16[128,768]{1,0:T(8,128)(2,1)S(1)}, bf16[128,768]{1,0:T(8,128)(2,1)}, u32[]{:S(2)}) copy-start(bf16[128,768]{1,0:T(8,128)(2,1)} %get-tuple-element.114) | copy-start | bytes 589828
  386.9 7.2 %copy-start = (f32[2,24,6144]{2,1,0:T(8,128)S(1)}, f32[2,24,6144]{2,1,0:T(8,128)}, u32[]{:S(2)}) copy-start(f32[2,24,6144]{2,1,0:T(8,128)} %get-tuple-element.118) | copy-start | bytes 3538948
  388.3 6.9 %copy-start.1 = (f32[2,96,768]{2,1,0:T(8,128)S(1)}, f32[2,96,768]{2,1,0:T(8,128)}, u32[]{:S(2)}) copy-start(f32[2,96,768]{2,1,0:T(8,128)} %get-tuple-element.119) | copy-start | bytes 1769476
  390.8 5.2 %copy-start.3 = (f32[2,2,24]{2,1,0:T(2,128)S(1)}, f32[2,2,24]{2,1,0:T(2,128)}, u32[]{:S(2)}) copy-start(f32[2,2,24]{2,1,0:T(2,128)} %get-tuple-element.120) | copy-start | bytes 1156

commit v6 on v5

--- a/solution.py
+++ b/solution.py
@@ -622,7 +622,7 @@
     loop(1, at.nz, step)
 
 
-def attention_end(at, q_ref, inside, slopes, tokens, m_ref, acc_ref, ctx_ref, ctxf_ref, qb_ref):
+def attention_end(m_ref, acc_ref, ctx_ref, ctxf_ref):
     for h in range(3):
         half = V_AT[h][1]
         first = 0 if half else 64
@@ -631,9 +631,7 @@
         ctx = acc[:, 64 * half : 64 * half + 64] / total
         ctxf_ref[:, 64 * h : 64 * h + 64] = ctx
         ctx_ref[:, 64 * h : 64 * h + 64] = ctx.astype(BF)
-        lse = m_ref[h] + jnp.log(total)
-        for side in range(2):
-            qb_ref[side, h] = query_operand(at, q_ref, inside, slopes, side, h, tokens, lse)
+        m_ref[h] = m_ref[h] + jnp.log(total)
 
 
 def fwd_kernel(nz, layers, host, R):
@@ -696,7 +694,10 @@
                         R.spread[2 * g + side, 0:wrows, lo : lo + quarter] = join(*[w[:, i : i + part_width] for i in firsts]).astype(BF)
 
         regroup()
+        for l in range(layers):
+            down[l].put(R.down_mine[l])
         arrived()
+        down[0].start()
         to_holder = remote(R.ow_mine, R.ow_in, R.ow_send, R.ow_recv, at.holder)
         spread[0].start()
     else:
@@ -717,8 +718,6 @@
             R.ow_in[...] = R.ow_mine[...]
         arrive(0)
         qkv[0].start()
-        for l in range(layers):
-            down[l].put(R.down_mine[l])
 
         @pl.when(at.moves)
         def _():
@@ -728,7 +727,15 @@
 
     def columns(b):
         R.kaug_now[b // 2, b % 2] = key_columns(at, R.slopes, R.seg, b // 2, b % 2, tokens)
-    loop(0, 2 * nz, columns)
+
+    def columns_and_serve(zz):
+        columns(2 * zz)
+        columns(2 * zz + 1)
+        if host:
+            @pl.when(zz > 0)
+            def _():
+                qkv[0].serve(zz)
+    loop(0, nz, columns_and_serve)
     save(R.kaug_now, R.kaug)
     R.inside[...] = segment_columns(at, R.seg, rows)
 
@@ -752,10 +759,6 @@
         return value
 
     if host:
-        qkv[0].serve_all()
-        arrive(layers)
-        gu[0].start()
-        down[0].start()
         qkv[0].collect()
     R.small[...] = side_weight(qkv_w[0], 1, 128, 256).astype(F32).T[64 : 64 + 8 * layers, :]
     R.state[...] = R.x0[...].astype(F32)
@@ -782,23 +785,37 @@
                 R.q_op[side, h] = query_operand(at, R.q, R.inside, R.slopes, side, h, tokens)
 
         def behind(d, l=l):
-            if host and l == 0:
-                ow.serve(d)
-                gu[l].serve(d)
-                down[l].serve(d)
-
-        def ahead(d, l=l):
+            if host:
+                if l == 0:
+                    ow.serve(d)
+
+                @pl.when(d == min(2, nz - 1))
+                def _():
+                    arrive(layers + l)
+                    gu[l].start()
+
+        def later(p, l=l):
+            if host:
+                for step in range(p, nz if p == 3 else p + 1):
+                    gu[l].serve(step)
+                    if l == 0:
+                        down[l].serve(step)
+
+        def ahead(p, l=l):
             if host and l < layers - 1:
-                for p in range(d, nz if d == 3 else d + 1):
-                    gu[l + 1].serve(p)
-                    down[l + 1].serve(p)
+                if p == 0:
+                    arrive(l + 1)
+                    qkv[l + 1].start()
+                    down[l + 1].start()
+                for step in range(p, nz if p == 3 else p + 1):
+                    if step:
+                        qkv[l + 1].serve(step)
+                        down[l + 1].serve(step)
         attention(at, kv, R.q_op, R.kaug_now, R.m, R.acc, behind)
-        attention_end(at, R.q, R.inside, R.slopes, tokens, R.m, R.acc, R.ctx_now[l], R.ctxf_now[l], R.qb_now[l])
+        attention_end(R.m, R.acc, R.ctx_now[l], R.ctxf_now[l])
         kv_saved = save(kv.buf, R.kv[l])
         save(R.ctx_now[l], R.ctx[l])
         save(R.ctxf_now[l], R.ctxf[l])
-        save(R.qb_now[l], R.qb[l])
-        kv.finish()
         if l == 0 and host:
             ow.collect()
             step = group // (2 * nz)
@@ -808,12 +825,6 @@
                     R.ow_flat[step * b : step * b + step, :] = R.ow_wide[step * i : step * i + step, :]
                 R.out_now[i][...] = R.ow_flat[...].astype(BF)
                 save(R.out_now[i], R.out_w[i])
-        if not last and host:
-            arrive(l + 1)
-            qkv[l + 1].start()
-            arrive(layers + l + 1)
-            gu[l + 1].start()
-            down[l + 1].start()
         if l:
             square_sum.finish()
         for number, half in enumerate((1 - at.x, at.x)):
@@ -822,7 +833,14 @@
                 square_sum.send_far()
             else:
                 square_sum.send_near()
+        later(1)
         square_sum.relay()
+        kv.finish()
+        for side in range(2):
+            for h in range(3):
+                R.qb_now[l][side, h] = query_operand(at, R.q, R.inside, R.slopes, side, h, tokens, R.m[h])
+        save(R.qb_now[l], R.qb[l])
+        later(2)
         wait_saved(kv_saved)
         if not last:
             at.signal_neighbours(R.kv_free)
@@ -832,6 +850,8 @@
         R.yr_now[l][at.g] = y.astype(BF)
         gather_y[l].start()
         R.state[...] = y
+        later(3)
+        ahead(0)
         if host:
             gu[l].collect()
             down[l].collect()
@@ -841,8 +861,6 @@
         square_sum.finish()
         for number, half in enumerate((at.x, 1 - at.x)):
             if number == 1:
-                if not last and host:
-                    qkv[l + 1].serve_all()
                 gather_y[l].wait_far()
                 ahead(1)
             here = half_at(half)
@@ -866,8 +884,6 @@
             save(down[l].buf, R.down_w[l])
         square_sum.relay()
         ahead(2)
-        if not last and host:
-            qkv[l + 1].collect()
         R.sum2_now[l][...] = R.state[...] + (square_sum.total() + small(l, 6))
         save(R.sum2_now[l], R.sum2[l])
         state = layer_norm(R.sum2_now[l][...], small(l, 1), small(l, 7))
@@ -877,9 +893,11 @@
         else:
             R.xr_now[l + 1][at.g] = state.astype(BF)
             gather_x[l + 1].start()
+            ahead(3)
             gather_x[l + 1].wait_near()
-            ahead(3)
             gather_x[l + 1].wait_far()
+            if host:
+                qkv[l + 1].collect()
     for l in range(layers):
         gather_x[l].finish()
         gather_y[l].finish()
@@ -1128,6 +1146,8 @@
             R.ow_in[l] = R.ow_out[l]
 
     def assemble(l):
+        if not host:
+            return
         back[l].wait()
         piece = [R.back[l].inbox[k].astype(F32)[0:wrows] for k in range(8)]
         join = lambda side, *spans: jnp.concatenate(
@@ -1218,14 +1238,6 @@
                 load(which, l - 1).start()
         da_all = R.da[...].reshape(rows, width)
         dctx = dot(da_all, R.out_w[l][...], NT).astype(BF)
-        d_out = dot(R.ctx[l][...], da_all, TN)
-        if host:
-            step = d_out.shape[0] // (2 * nz)
-            for b in range(2 * nz):
-                R.ow[l].stage[b // 2, b % 2] = jnp.concatenate(
-                    [d_out[step * b : step * b + step], jnp.zeros((OW_ROWS - step, width), F32)]).astype(BF)
-        else:
-            R.ow[l].stage[...] = d_out.astype(BF)
         ctxf = R.ctxf[l]
         wide = dctx.astype(F32)
         first_two = wide[:, :128]
@@ -1247,16 +1259,31 @@
             for p in range(3, nz - 1):
                 serve(attention_sums(l + 1), p)
 
-        def behind(i):
-            pass
+        def out_grad(l=l):
+            d_out = dot(R.ctx[l][...], R.da[...].reshape(rows, width), TN)
+            if host:
+                step = d_out.shape[0] // (2 * nz)
+                for b in range(2 * nz):
+                    R.ow[l].stage[b // 2, b % 2] = jnp.concatenate(
+                        [d_out[step * b : step * b + step], jnp.zeros((OW_ROWS - step, width), F32)]).astype(BF)
+            else:
+                R.ow[l].stage[...] = d_out.astype(BF)
+
+        def behind(i, l=l):
+            pl.when(i == 0)(out_grad)
+            if l < layers - 1:
+                @pl.when(i == min(1, nz - 2))
+                def _():
+                    emit(l + 1)
+
+                @pl.when(i == nz - 2)
+                def _():
+                    assemble(l + 1)
 
         def at_end(l=l):
             serve(feed_forward_sums(l), 0)
         attn_back(at, R, l, top, begin, behind, at_end)
         dproj = R.dproj
-        bias_sum = jnp.sum(dproj[...].astype(F32), axis=0, keepdims=True)
-        for t, row in ((6, bias_sum[:, 384:576]), (7, jnp.concatenate([bias_sum[:, 128:256], bias_sum[:, 320:384]], axis=1))):
-            put_small(l, t, jnp.concatenate([jnp.where(at.g == g, row, 0.0) for g in range(4)], axis=1))
         gather_df.finish()
         gather_da.finish()
         square_sum.finish()
@@ -1268,6 +1295,9 @@
             else:
                 square_sum.send_near()
         square_sum.relay()
+        bias_sum = jnp.sum(dproj[...].astype(F32), axis=0, keepdims=True)
+        for t, row in ((6, bias_sum[:, 384:576]), (7, jnp.concatenate([bias_sum[:, 128:256], bias_sum[:, 320:384]], axis=1))):
+            put_small(l, t, jnp.concatenate([jnp.where(at.g == g, row, 0.0) for g in range(4)], axis=1))
         for cc in range(2):
             wgrad(R.xr_now, dproj, R.qk[l].stage, cc, 384 * cc, 384 * cc + 384)
         for item in attention_sums(l):
@@ -1276,7 +1306,6 @@
         if l > 0:
             load(xr, l - 1).start()
             load(qkv_w, l - 1).start()
-        emit(l + 1)
         R.g[...] = R.e1[...] + square_sum.total()
     R.grad_in[...] = R.g[...]
     square_sum.finish()
@@ -1301,8 +1330,6 @@
             def _():
                 R.sm_in[at.g] = R.sm_out[...]
         emit(0)
-        for l in range(1, layers):
-            assemble(l)
         total = jnp.zeros(R.sm_out.shape, F32)
         for g in range(4):
             copy, away = small_from(g)

time: 403 us -> 395 us (0.980)
  Pallas kernels: 384 us -> 375 us
    pallas_call x2, Pallas kernels: 384 us -> 375 us  [call(): pl.pallas_call(kernel, out_shape=tuple(flat[3]) + tuple(flat[4]), in_spec...]
where the time goes in v6:
time: 395 us; the launch traced here: 388 us
  Pallas kernels  375 us (95%)
  local copies, waits for them, and re-layouts  11.2 us (3%)
    pallas_call x2, Pallas kernels, call(): pl.pallas_call(kernel, out_shape=tuple(flat[3]) + tuple(flat[4]), in_spec...  375 us
    unnamed x18, local copies, waits for them, and re-layouts  11.2 us

profile of v6, /device:TPU:21, one launch (start us, length us, event | category | flops | bytes accessed | tf_op | source)
XLA Modules:
  0.0 388.2 jit_solution(16569605259082107028)
XLA Ops:
  0.6 0.8 copy.24
  1.4 0.8 copy.25
  2.2 0.1 maximum_bitcast_fusion
  2.3 0.7 fusion.2.refs_5_
  3.0 161.6 %forward.1 = (bf16[128,768]{1,0:T(8,128)(2,1)}, f32[16,768]{1,0:T(8,128)}, bf16[512,192]{1,0:T(8,128)(2,1)}, bf16[512,192]{1,0:T(8,128)(2,1)}, f32[512,192]{1,0:...) custom-call(bf16[2,96,768]{2,1,0:T(8,128)(2,1)} %refs_0_.1, ...), custom_call_target="tpu_custom_call" | custom-call | flops 99999997952 | bytes 200000000 | tf_op jit(solution)/shard_map/forward/pallas_call | solution.py:490
  164.6 0.0 copy-start.2
  164.6 213.8 %backward.1 = (f32[2,6,24]{2,1,0:T(8,128)}, f32[2,96,768]{2,1,0:T(8,128)}, f32[2,2,24]{2,1,0:T(2,128)}, f32[128,768]{1,0:T(8,128)}, f32[2,24,6144]{2,1,0:T(8,128...) custom-call(bf16[512,192]{1,0:T(8,128)(2,1)} %get-tuple-element.45.refs_0_, ...), custom_call_target="tpu_custom_call" | custom-call | flops 99999997952 | bytes 200000000 | tf_op jit(solution)/shard_map/backward/pallas_call | solution.py:490
  378.4 0.0 copy-start
  378.4 1.4 copy.26
  379.8 0.0 copy-done.2
  379.8 0.0 copy-start.1
  379.8 0.7 copy.34
  380.5 1.8 copy.35
  382.2 0.0 copy-start.3
  382.2 1.8 copy.36
  384.1 1.6 copy.37
  385.6 0.0 copy-done
  385.6 1.0 copy.38
  386.6 0.0 copy-done.1
  386.6 0.8 copy.39
  387.5 0.0 copy-done.3
  387.5 0.6 copy.40
  (1 shorter events, 0.0 us)
Async XLA Ops:
  164.6 215.2 %copy-start.2 = (bf16[128,768]{1,0:T(8,128)(2,1)S(1)}, bf16[128,768]{1,0:T(8,128)(2,1)}, u32[]{:S(2)}) copy-start(bf16[128,768]{1,0:T(8,128)(2,1)} %get-tuple-element.114) | copy-start | bytes 589828
  378.4 7.2 %copy-start = (f32[2,24,6144]{2,1,0:T(8,128)S(1)}, f32[2,24,6144]{2,1,0:T(8,128)}, u32[]{:S(2)}) copy-start(f32[2,24,6144]{2,1,0:T(8,128)} %get-tuple-element.118) | copy-start | bytes 3538948
  379.8 6.9 %copy-start.1 = (f32[2,96,768]{2,1,0:T(8,128)S(1)}, f32[2,96,768]{2,1,0:T(8,128)}, u32[]{:S(2)}) copy-start(f32[2,96,768]{2,1,0:T(8,128)} %get-tuple-element.119) | copy-start | bytes 1769476
  382.2 5.2 %copy-start.3 = (f32[2,2,24]{2,1,0:T(2,128)S(1)}, f32[2,2,24]{2,1,0:T(2,128)}, u32[]{:S(2)}) copy-start(f32[2,2,24]{2,1,0:T(2,128)} %get-tuple-element.120) | copy-start | bytes 1156

commit v7 on v6

--- a/solution.py
+++ b/solution.py
@@ -251,59 +251,64 @@
 class BlockGather:
     def __init__(self, at, item):
         self.at, self.buf, self.zsend, self.csend, self.recv = at, item.buf, item.zsend, item.csend, item.recv
-
-    def copy(self, zz, send, device):
-        at = self.at
-        return remote(self.buf.at[zz, at.c], self.buf.at[zz, at.c], send, self.recv.at[zz, at.c], device)
-
-    def to_right(self, zz):
-        return self.copy(zz, self.zsend.at[0, zz], self.at.column(self.at.z + 1))
-
-    def to_left(self, zz):
-        return self.copy(zz, self.zsend.at[1, zz], self.at.column(self.at.z - 1))
-
-    def to_beside(self, zz):
-        return self.copy(zz, self.csend.at[zz], self.at.beside)
+        self.parts = self.recv.shape[2]
+        self.step = self.buf.shape[2] // self.parts
+
+    def copy(self, zz, cc, part, send, device):
+        block = self.buf.at[zz, cc, pl.ds(part * self.step, self.step)]
+        return remote(block, block, send, self.recv.at[zz, cc, part], device)
+
+    def to_right(self, zz, part):
+        return self.copy(zz, self.at.c, part, self.zsend.at[0, zz, part], self.at.column(self.at.z + 1))
+
+    def to_left(self, zz, part):
+        return self.copy(zz, self.at.c, part, self.zsend.at[1, zz, part], self.at.column(self.at.z - 1))
+
+    def to_beside(self, zz, part):
+        return self.copy(zz, self.at.c, part, self.csend.at[zz, part], self.at.beside)
+
+    def wait_part(self, zz, cc, part):
+        self.copy(zz, cc, part, self.csend.at[zz, part], self.at.beside).wait_recv()
 
     def wait(self, zz, cc):
-        at = self.at
-        remote(self.buf.at[zz, cc], self.buf.at[zz, cc], self.csend.at[zz], self.recv.at[zz, cc], at.beside).wait_recv()
+        for part in range(self.parts):
+            self.wait_part(zz, cc, part)
 
     def put(self, value):
         self.buf[self.at.z, self.at.c] = value
 
     def start(self):
         at = self.at
-
-        @pl.when(at.has_right)
-        def _():
-            self.to_right(at.z).start()
-
-        @pl.when(at.has_left)
-        def _():
-            self.to_left(at.z).start()
-        self.to_beside(at.z).start()
+        for part in range(self.parts):
+            @pl.when(at.has_right)
+            def _(part=part):
+                self.to_right(at.z, part).start()
+
+            @pl.when(at.has_left)
+            def _(part=part):
+                self.to_left(at.z, part).start()
+            self.to_beside(at.z, part).start()
 
     def serve(self, d):
         at = self.at
-
-        @pl.when(at.z - d >= 0)
-        def _():
-            self.wait(at.z - d, at.c)
-
-            @pl.when(at.has_right)
-            def _():
-                self.to_right(at.z - d).start()
-            self.to_beside(at.z - d).start()
-
-        @pl.when(at.z + d < at.nz)
-        def _():
-            self.wait(at.z + d, at.c)
-
-            @pl.when(at.has_left)
-            def _():
-                self.to_left(at.z + d).start()
-            self.to_beside(at.z + d).start()
+        for part in range(self.parts):
+            @pl.when(at.z - d >= 0)
+            def _(part=part):
+                self.wait_part(at.z - d, at.c, part)
+
+                @pl.when(at.has_right)
+                def _():
+                    self.to_right(at.z - d, part).start()
+                self.to_beside(at.z - d, part).start()
+
+            @pl.when(at.z + d < at.nz)
+            def _(part=part):
+                self.wait_part(at.z + d, at.c, part)
+
+                @pl.when(at.has_left)
+                def _():
+                    self.to_left(at.z + d, part).start()
+                self.to_beside(at.z + d, part).start()
 
     def serve_all(self):
         loop(1, self.at.nz, self.serve)
@@ -315,74 +320,73 @@
         at = self.at
 
         def drain(zz):
-            self.to_beside(zz).wait_send()
-
-            @pl.when((zz <= at.z) & at.has_right)
-            def _():
-                self.to_right(zz).wait_send()
-
-            @pl.when((zz >= at.z) & at.has_left)
-            def _():
-                self.to_left(zz).wait_send()
+            for part in range(self.parts):
+                self.to_beside(zz, part).wait_send()
+
+                @pl.when((zz <= at.z) & at.has_right)
+                def _(part=part):
+                    self.to_right(zz, part).wait_send()
+
+                @pl.when((zz >= at.z) & at.has_left)
+                def _(part=part):
+                    self.to_left(zz, part).wait_send()
         loop(0, at.nz, drain)
 
 
-def block_gather_item(nz, *dims):
-    return dict(buf=keep(nz, 2, *dims), zsend=copies(2, nz), csend=copies(nz), recv=copies(nz, 2))
+def block_gather_item(nz, *dims, parts=1):
+    return dict(buf=keep(nz, 2, *dims), zsend=copies(2, nz, parts), csend=copies(nz, parts), recv=copies(nz, 2, parts))
 
 
 class BlockSum:
     def __init__(self, at, item):
         self.at, self.stage, self.cin, self.zin = at, item.stage, item.cin, item.zin
         self.csend, self.crecv, self.zsend, self.zrecv = item.csend, item.crecv, item.zsend, item.zrecv
+        self.parts = self.zsend.shape[1]
+        self.step = self.stage.shape[2] // self.parts
+
+    def rows(self, part):
+        return pl.ds(part * self.step, self.step)
 
     def to_beside(self, t):
         return remote(self.stage.at[t, self.at.oc], self.cin.at[t], self.csend.at[t], self.crecv.at[t], self.at.beside)
 
-    def to_right(self, t):
-        return remote(self.stage.at[t, self.at.c], self.zin.at[t + 1], self.zsend.at[t], self.zrecv.at[t + 1], self.at.column(self.at.z + 1))
-
-    def to_left(self, t):
-        return remote(self.stage.at[t, self.at.c], self.zin.at[t], self.zsend.at[t], self.zrecv.at[t], self.at.column(self.at.z - 1))
-
-    def arrived(self, slot):
-        at = self.at
-        remote(self.zin.at[slot], self.zin.at[slot], self.zsend.at[0], self.zrecv.at[slot], at.beside).wait_recv()
+    def along(self, t, slot, part, device):
+        rows = self.rows(part)
+        return remote(self.stage.at[t, self.at.c, rows], self.zin.at[slot, rows], self.zsend.at[t, part],
+                      self.zrecv.at[slot, part], device)
+
+    def to_right(self, t, part):
+        return self.along(t, t + 1, part, self.at.column(self.at.z + 1))
+
+    def to_left(self, t, part):
+        return self.along(t, t, part, self.at.column(self.at.z - 1))
+
+    def arrived(self, slot, part):
+        block = self.zin.at[slot, self.rows(part)]
+        remote(block, block, self.zsend.at[0, part], self.zrecv.at[slot, part], self.at.beside).wait_recv()
 
     def start(self):
         loop(0, self.at.nz, lambda t: self.to_beside(t).start())
 
-    def add(self, t, slot=None):
-        value = self.stage[t, self.at.c].astype(F32) + self.cin[t].astype(F32)
+    def add(self, t, part, slot=None):
+        rows = self.rows(part)
+        value = self.stage[t, self.at.c, rows].astype(F32) + self.cin[t, rows].astype(F32)
         if slot is not None:
-            value = value + self.zin[slot].astype(F32)
-        self.stage[t, self.at.c] = value.astype(self.stage.dtype)
-
-    def go_right(self, t):
+            value = value + self.zin[slot, rows].astype(F32)
+        self.stage[t, self.at.c, rows] = value.astype(self.stage.dtype)
+
+    def go(self, t, slot, passed_on, send):
         self.to_beside(t).wait_recv()
-
-        @pl.when(self.at.has_left)
-        def _():
-            self.arrived(t + 1)
-            self.add(t, t + 1)
-
-        @pl.when(jnp.logical_not(self.at.has_left))
-        def _():
-            self.add(t)
-        self.to_right(t).start()
-
-    def go_left(self, t):
-        self.to_beside(t).wait_recv()
-
-        @pl.when(self.at.has_right)
-        def _():
-            self.arrived(t)
-            self.add(t, t)
-
-        @pl.when(jnp.logical_not(self.at.has_right))
-        def _():
-            self.add(t)
-        self.to_left(t).start()
+        for part in range(self.parts):
+            @pl.when(passed_on)
+            def _(part=part):
+                self.arrived(slot, part)
+                self.add(t, part, slot)
+
+            @pl.when(jnp.logical_not(passed_on))
+            def _(part=part):
+                self.add(t, part)
+            send(t, part).start()
 
     def serve(self, p, source=True, relay=True):
         at = self.at
@@ -396,23 +400,23 @@
 
         @pl.when(go_r)
         def _():
-            self.go_right(at.nz - 1 - right)
+            self.go(at.nz - 1 - right, at.nz - right, at.has_left, self.to_right)
 
         @pl.when(go_l)
         def _():
-            self.go_left(left)
+            self.go(left, left, at.has_right, self.to_left)
 
     def total(self):
         at = self.at
         self.to_beside(at.z).wait_recv()
-
-        @pl.when(at.has_left)
-        def _():
-            self.arrived(at.z + 1)
-
-        @pl.when(at.has_right)
-        def _():
-            self.arrived(at.z)
+        for part in range(self.parts):
+            @pl.when(at.has_left)
+            def _(part=part):
+                self.arrived(at.z + 1, part)
+
+            @pl.when(at.has_right)
+            def _(part=part):
+                self.arrived(at.z, part)
         value = self.stage[at.z, at.c].astype(F32) + self.cin[at.z].astype(F32)
         from_left = jnp.where(at.has_left, self.zin[at.z + 1].astype(F32), 0.0)
         from_right = jnp.where(at.has_right, self.zin[at.z].astype(F32), 0.0)
@@ -423,14 +427,14 @@
 
         def drain(t):
             self.to_beside(t).wait_send()
-
-            @pl.when(t > at.z)
-            def _():
-                self.to_right(t).wait_send()
-
-            @pl.when(t < at.z)
-            def _():
-                self.to_left(t).wait_send()
+            for part in range(self.parts):
+                @pl.when(t > at.z)
+                def _(part=part):
+                    self.to_right(t, part).wait_send()
+
+                @pl.when(t < at.z)
+                def _(part=part):
+                    self.to_left(t, part).wait_send()
         loop(0, at.nz, drain)
 
 
@@ -532,9 +536,9 @@
     return v.reshape(v.shape[0] * v.shape[1], v.shape[2])
 
 
-def block_sum_item(nz, *dims, dtype=BF):
+def block_sum_item(nz, *dims, dtype=BF, parts=1):
     return dict(stage=keep(nz, 2, *dims, dtype=dtype), cin=keep(nz, *dims, dtype=dtype), zin=keep(nz + 1, *dims, dtype=dtype),
-                csend=copies(nz), crecv=copies(nz), zsend=copies(nz), zrecv=copies(nz + 1))
+                csend=copies(nz), crecv=copies(nz), zsend=copies(nz, parts), zrecv=copies(nz + 1, parts))
 
 
 def segment_row(seg, zz, cc):
@@ -605,8 +609,13 @@
         compute(at.z, cc, True)
     loop(0, 2, here)
 
+    def both(d):
+        return (at.z - d >= 0) & (at.z + d < at.nz)
+
     def step(d):
-        gather.serve(d)
+        @pl.when(jnp.logical_not(both(d - 1)) | (d == 1))
+        def _():
+            gather.serve(d)
         behind(d)
 
         def visit(i):
@@ -618,6 +627,10 @@
                 def _():
                     gather.wait(zz, at.oc)
                 compute(zz, jnp.where(i < 2, at.c, at.oc), False)
+
+            @pl.when((i == 1) & both(d) & (d + 1 < at.nz))
+            def _():
+                gather.serve(d + 1)
         loop(0, 4, visit)
     loop(1, at.nz, step)
 
@@ -932,7 +945,7 @@
         xr_now=keep_rows(), x_send=copies(layers, 6), x_recv=copies(layers, 6),
         yr_now=keep_rows(), y_send=copies(layers, 6), y_recv=copies(layers, 6),
         part=keep(4, tokens, width, dtype=F32), state=keep(tokens, width, dtype=F32), **square_sum_items(tokens, width),
-        kv_now=block_gather_item(nz, rows, 384), kv_free=pltpu.SemaphoreType.REGULAR, saved=copies(16 * layers),
+        kv_now=block_gather_item(nz, rows, 384, parts=2), kv_free=pltpu.SemaphoreType.REGULAR, saved=copies(16 * layers),
         kaug_now=keep(nz, 2, rows, 128), inside=keep(rows, 128, dtype=F32),
         q=keep(rows, group), q_op=keep(2, 3, rows, 128),
         m=keep(3, rows, 128, dtype=F32), acc=keep(3, rows, 128, dtype=F32),
@@ -948,7 +961,7 @@
     near = dict(x0=x0, seg=seg, **vars(weights))
     if host:
         gathered = lambda *dims: [shape(nz, 2, *dims) for _ in each]
-        items = lambda *dims: [block_gather_item(nz, *dims) for _ in each]
+        items = lambda *dims: [block_gather_item(nz, *dims, parts=2) for _ in each]
         rd = weights.down_mine.shape[1]
         padded = 32
         far_out.update(qkv_w=gathered(r, 384), gu_w=gathered(r, quarter), down_w=gathered(rd, width),
@@ -1038,15 +1051,10 @@
         load(target(i + 1), 0).start()
         load(t, 1).wait()
         compute(t, 1, False)
-        dkv.serve(i, relay=False)
-
-        @pl.when(i > 0)
-        def _():
-            dkv.serve(i - 1, source=False)
+        dkv.serve(i)
         behind(i)
     loop(0, nz - 1, step)
     far(at.z, True)
-    dkv.serve(nz - 2, source=False)
     load(at.z, 1).wait()
     compute(at.z, 1, True)
     at_end()
@@ -1384,8 +1392,8 @@
             ow_send=copies(layers), ow_recv=copies(layers),
             sm_out=keep(8 * layers, 128, dtype=F32), sm_in=keep(4, 8 * layers, 128, dtype=F32), sm_send=copies(4), sm_recv=copies(4))
         scratch.update(
-            gu=[block_sum_item(nz, r, quarter) for _ in each], dn=[block_sum_item(nz, rd, width) for _ in each],
-            qk=[block_sum_item(nz, r, 384) for _ in each], ow=[block_sum_item(nz, OW_ROWS, width) for _ in each],
+            gu=[block_sum_item(nz, r, quarter, parts=2) for _ in each], dn=[block_sum_item(nz, rd, width, parts=2) for _ in each],
+            qk=[block_sum_item(nz, r, 384, parts=2) for _ in each], ow=[block_sum_item(nz, OW_ROWS, width) for _ in each],
             sm=block_sum_item(nz, 8 * layers, 128, dtype=F32), tok_small=keep(8 * layers, width, dtype=F32))
     else:
         out.update(
@@ -1402,7 +1410,7 @@
         g=keep(tokens, width, dtype=F32), e1=keep(tokens, width, dtype=F32), e2=keep(tokens, width, dtype=F32),
         hid=keep(rows, quarter), dgu=keep(rows, 2 * quarter), do=keep(3, rows, 128),
         dqacc=keep(3, rows, 128, dtype=F32), dproj=keep(rows, 768),
-        dkv=dict(block_sum_item(nz, rows, 384), free=pltpu.SemaphoreType.REGULAR))
+        dkv=dict(block_sum_item(nz, rows, 384, parts=2), free=pltpu.SemaphoreType.REGULAR))
     near = dict(grad=grad, small=saved.small, sum1=saved.sum1, sum2=saved.sum2, ctx=saved.ctx,
                 ctxf=saved.ctxf, qb=saved.qb, out_w=saved.out_w)
     far = dict(mixed=saved.mixed, yr=saved.yr, xr=saved.xr, gu_w=saved.gu_w, down_w=saved.down_w, kv=saved.kv, kaug=saved.kaug,

time: 395 us -> 387 us (0.980)
  Pallas kernels: 375 us -> 367 us
    pallas_call x2, Pallas kernels: 375 us -> 367 us  [call(): pl.pallas_call(kernel, out_shape=tuple(flat[3]) + tuple(flat[4]), in_spec...]
where the time goes in v7:
time: 387 us; the launch traced here: 380 us
  Pallas kernels  367 us (95%)
  local copies, waits for them, and re-layouts  11.2 us (3%)
    pallas_call x2, Pallas kernels, call(): pl.pallas_call(kernel, out_shape=tuple(flat[3]) + tuple(flat[4]), in_spec...  367 us
    unnamed x18, local copies, waits for them, and re-layouts  11.2 us

profile of v7, /device:TPU:21, one launch (start us, length us, event | category | flops | bytes accessed | tf_op | source)
XLA Modules:
  0.0 380.2 jit_solution(2629734254833365493)
XLA Ops:
  0.6 0.8 copy.24
  1.4 0.8 copy.25
  2.2 0.1 maximum_bitcast_fusion
  2.3 0.7 fusion.2.refs_5_
  3.0 158.7 %forward.1 = (bf16[128,768]{1,0:T(8,128)(2,1)}, f32[16,768]{1,0:T(8,128)}, bf16[512,192]{1,0:T(8,128)(2,1)}, bf16[512,192]{1,0:T(8,128)(2,1)}, f32[512,192]{1,0:...) custom-call(bf16[2,96,768]{2,1,0:T(8,128)(2,1)} %refs_0_.1, ...), custom_call_target="tpu_custom_call" | custom-call | flops 99999997952 | bytes 200000000 | tf_op jit(solution)/shard_map/forward/pallas_call | solution.py:494
  161.7 0.0 copy-start.2
  161.7 208.4 %backward.1 = (f32[2,6,24]{2,1,0:T(8,128)}, f32[2,96,768]{2,1,0:T(8,128)}, f32[2,2,24]{2,1,0:T(2,128)}, f32[128,768]{1,0:T(8,128)}, f32[2,24,6144]{2,1,0:T(8,128...) custom-call(bf16[512,192]{1,0:T(8,128)(2,1)} %get-tuple-element.45.refs_0_, ...), custom_call_target="tpu_custom_call" | custom-call | flops 99999997952 | bytes 200000000 | tf_op jit(solution)/shard_map/backward/pallas_call | solution.py:494
  370.1 0.0 copy-start
  370.1 1.4 copy.26
  371.5 0.0 copy-done.2
  371.5 0.0 copy-start.1
  371.5 0.7 copy.34
  372.2 1.8 copy.35
  374.0 0.0 copy-start.3
  374.0 1.8 copy.36
  375.8 1.6 copy.37
  377.4 0.0 copy-done
  377.4 1.0 copy.38
  378.4 0.0 copy-done.1
  378.4 0.8 copy.39
  379.2 0.0 copy-done.3
  379.2 0.6 copy.40
  (1 shorter events, 0.0 us)
Async XLA Ops:
  161.7 209.8 %copy-start.2 = (bf16[128,768]{1,0:T(8,128)(2,1)S(1)}, bf16[128,768]{1,0:T(8,128)(2,1)}, u32[]{:S(2)}) copy-start(bf16[128,768]{1,0:T(8,128)(2,1)} %get-tuple-element.114) | copy-start | bytes 589828
  370.1 7.2 %copy-start = (f32[2,24,6144]{2,1,0:T(8,128)S(1)}, f32[2,24,6144]{2,1,0:T(8,128)}, u32[]{:S(2)}) copy-start(f32[2,24,6144]{2,1,0:T(8,128)} %get-tuple-element.118) | copy-start | bytes 3538948
  371.5 6.9 %copy-start.1 = (f32[2,96,768]{2,1,0:T(8,128)S(1)}, f32[2,96,768]{2,1,0:T(8,128)}, u32[]{:S(2)}) copy-start(f32[2,96,768]{2,1,0:T(8,128)} %get-tuple-element.119) | copy-start | bytes 1769476
  374.0 5.2 %copy-start.3 = (f32[2,2,24]{2,1,0:T(2,128)S(1)}, f32[2,2,24]{2,1,0:T(2,128)}, u32[]{:S(2)}) copy-start(f32[2,2,24]{2,1,0:T(2,128)} %get-tuple-element.120) | copy-start | bytes 1156

commit v8 on v7

--- a/solution.py
+++ b/solution.py
@@ -986,7 +986,7 @@
 
 def attn_back(at, R, l, top, begin, behind, at_end):
     nz, rows = at.nz, R.kvbuf.shape[1]
-    q_ref, do_ref, dqacc = R.qb[l], R.do, R.dqacc
+    q_ref, do_ref, dqacc = R.qb_now, R.do, R.dqacc
     dkv = BlockSum(at, R.dkv)
 
     def target(i):
@@ -1073,14 +1073,14 @@
     rows, half_rows = 4 * tokens, 2 * tokens
     quarter = R.hid.shape[1]
     width = R.grad.shape[1]
-    mixed, yr, xr, gu_w, down_w, qkv_w = range(6)
+    mixed, yr, xr, gu_w, down_w, qkv_w, qb, ctx, ctxf, out_w = range(10)
     streams = ((R.mixed, R.mixed_now), (R.yr, R.yr_now), (R.xr, R.xr_now), (R.gu_w, R.gu_now), (R.down_w, R.down_now),
-               (R.qkv_w, R.qkv_now))
+               (R.qkv_w, R.qkv_now), (R.qb, R.qb_now), (R.ctx, R.ctx_now), (R.ctxf, R.ctxf_now), (R.out_w, R.out_now))
 
     def load(which, l):
         return pltpu.make_async_copy(streams[which][0][l], streams[which][1], R.load.at[which])
 
-    for which in range(6):
+    for which in range(10):
         load(which, layers - 1).start()
     at.enter(host)()
     R.dproj[:, 576:768] = jnp.zeros((rows, 192), BF)
@@ -1091,7 +1091,7 @@
     if host:
         gu_sum, dn_sum, qk_sum, ow_sum = [[BlockSum(at, item) for item in items] for items in (R.gu, R.dn, R.qk, R.ow)]
         sm_sum = BlockSum(at, R.sm)
-        back = [PlaneExchange(at, item.out, item.inbox, item.send, item.recv) for item in R.back]
+        back = [[PlaneExchange(at, item.out, item.inbox, item.send, item.recv) for item in items] for items in R.back]
         wrows = R.out_grad.shape[1]
         moved = [remote(R.ow_out.at[l], R.ow_in.at[l], R.ow_send.at[l], R.ow_recv.at[l], at.chunk_device) for l in range(layers)]
 
@@ -1136,12 +1136,12 @@
     def emit(l):
         if not host or l == layers:
             return
-        pad = lambda v: jnp.concatenate([v, jnp.zeros((R.back[l].out.shape[1] - wrows, v.shape[1]), F32)], axis=0).astype(BF)
-        for item, lo in ((gu_sum[l], 0), (qk_sum[l], quarter)):
+        for item, exchange in zip((gu_sum[l], qk_sum[l]), back[l]):
             v = item.total()
+            rest = jnp.zeros((exchange.out.shape[1] - wrows, v.shape[1]), F32)
             for k in range(8):
-                R.back[l].out[k, :, lo : lo + v.shape[1]] = pad(v[wrows * k : wrows * k + wrows])
-        back[l].start()
+                exchange.out[k] = jnp.concatenate([v[wrows * k : wrows * k + wrows], rest], axis=0).astype(BF)
+            exchange.start()
         R.dn_grad[l] = dn_sum[l].total()
         R.ow_out[l] = ow_sum[l].total()
 
@@ -1156,19 +1156,23 @@
     def assemble(l):
         if not host:
             return
-        back[l].wait()
-        piece = [R.back[l].inbox[k].astype(F32)[0:wrows] for k in range(8)]
-        join = lambda side, *spans: jnp.concatenate(
-            [piece[2 * g + side][:, lo:hi] for g in range(4) for lo, hi in spans], axis=1)
-        at_kv = quarter
-        R.qkv_grad[l, :, 0:width] = join(1, (at_kv, at_kv + 192))
-        R.qkv_grad[l, :, width : 2 * width] = join(0, (at_kv, at_kv + 128), (at_kv + 256, at_kv + 320))
-        R.qkv_grad[l, :, 2 * width : 3 * width] = join(0, (at_kv + 128, at_kv + 256), (at_kv + 320, at_kv + 384))
+        def pieces(exchange):
+            exchange.wait()
+            piece = [exchange.inbox[k].astype(F32)[0:wrows] for k in range(8)]
+            return lambda side, *spans: jnp.concatenate(
+                [piece[2 * g + side][:, lo:hi] for g in range(4) for lo, hi in spans], axis=1)
+
+        join = pieces(back[l][0])
         step = quarter // nz
         for side in range(2):
             for zz in range(nz):
                 lo = (side * nz + zz) * 4 * step
                 R.gu_grad[l, :, lo : lo + 4 * step] = join(side, (step * zz, step * zz + step))
+        join = pieces(back[l][1])
+        at_kv = 0
+        R.qkv_grad[l, :, 0:width] = join(1, (at_kv, at_kv + 192))
+        R.qkv_grad[l, :, width : 2 * width] = join(0, (at_kv, at_kv + 128), (at_kv + 256, at_kv + 320))
+        R.qkv_grad[l, :, 2 * width : 3 * width] = join(0, (at_kv + 128, at_kv + 256), (at_kv + 320, at_kv + 384))
 
         @pl.when(at.moves)
         def _():
@@ -1196,7 +1200,7 @@
         R.df[at.g] = low
         gather_df.start()
         R.e2[...] = e2
-        for which in range(6):
+        for which in range(10):
             load(which, l).wait()
         serve(feed_forward_sums(l + 1), 1)
         gather_df.wait_near()
@@ -1245,17 +1249,17 @@
             for which in (mixed, yr, gu_w, down_w):
                 load(which, l - 1).start()
         da_all = R.da[...].reshape(rows, width)
-        dctx = dot(da_all, R.out_w[l][...], NT).astype(BF)
-        ctxf = R.ctxf[l]
+        dctx = dot(da_all, R.out_now[...], NT).astype(BF)
+        heads_out = R.ctxf_now
         wide = dctx.astype(F32)
         first_two = wide[:, :128]
         third = jnp.concatenate([jnp.zeros((rows, 64), F32), wide[:, 128:192]], axis=1)
-        prod = first_two * ctxf[:, :128]
+        prod = first_two * heads_out[:, :128]
         low_half = in_half(0, rows)
         deltas = [
             jnp.sum(jnp.where(low_half, prod, 0.0), axis=1, keepdims=True),
             jnp.sum(jnp.where(low_half, 0.0, prod), axis=1, keepdims=True),
-            jnp.sum(wide[:, 128:192] * ctxf[:, 128:192], axis=1, keepdims=True),
+            jnp.sum(wide[:, 128:192] * heads_out[:, 128:192], axis=1, keepdims=True),
         ]
         for h in range(3):
             half = V_AT[h][1]
@@ -1268,7 +1272,7 @@
                 serve(attention_sums(l + 1), p)
 
         def out_grad(l=l):
-            d_out = dot(R.ctx[l][...], R.da[...].reshape(rows, width), TN)
+            d_out = dot(R.ctx_now[...], R.da[...].reshape(rows, width), TN)
             if host:
                 step = d_out.shape[0] // (2 * nz)
                 for b in range(2 * nz):
@@ -1312,8 +1316,8 @@
             item.start()
         serve(attention_sums(l), 0)
         if l > 0:
-            load(xr, l - 1).start()
-            load(qkv_w, l - 1).start()
+            for which in (xr, qkv_w, qb, ctx, ctxf, out_w):
+                load(which, l - 1).start()
         R.g[...] = R.e1[...] + square_sum.total()
     R.grad_in[...] = R.g[...]
     square_sum.finish()
@@ -1354,7 +1358,7 @@
             R.biases_grad[l] = jnp.concatenate([mine[8 * l + 6 : 8 * l + 8], mine[8 * l + 2 : 8 * l + 6]], axis=0)
         assemble(0)
         for l in range(layers):
-            for item in feed_forward_sums(l) + attention_sums(l) + (back[l],):
+            for item in feed_forward_sums(l) + attention_sums(l) + tuple(back[l]):
                 item.finish()
 
             @pl.when(at.moves)
@@ -1386,8 +1390,8 @@
             gu_grad=shape(layers, wrows, 8 * quarter, dtype=F32), dn_grad=shape(layers, rd, width, dtype=F32),
             gains_grad=shape(layers, 2, wrows, dtype=F32), biases_grad=shape(layers, 6, wrows, dtype=F32))
         scratch.update(
-            back=[dict(out=keep(8, padded, quarter + 384), inbox=keep(8, padded, quarter + 384), send=copies(8), recv=copies(8))
-                  for _ in each],
+            back=[[dict(out=keep(8, padded, cols), inbox=keep(8, padded, cols), send=copies(8), recv=copies(8))
+                   for cols in (quarter, 384)] for _ in each],
             ow_out=keep(layers, OW_ROWS, width, dtype=F32), ow_in=keep(layers, OW_ROWS, width, dtype=F32),
             ow_send=copies(layers), ow_recv=copies(layers),
             sm_out=keep(8 * layers, 128, dtype=F32), sm_in=keep(4, 8 * layers, 128, dtype=F32), sm_send=copies(4), sm_recv=copies(4))
@@ -1403,7 +1407,8 @@
     like = lambda arrays: keep(*arrays[0].shape, dtype=arrays[0].dtype)
     scratch.update(
         mixed_now=like(saved.mixed), yr_now=like(saved.yr), xr_now=like(saved.xr), gu_now=like(saved.gu_w),
-        down_now=like(saved.down_w), qkv_now=like(saved.qkv_w), load=copies(6), kvbuf=keep(2, rows, 384), augbuf=keep(2, rows, 128), kvsem=copies(2, 2),
+        down_now=like(saved.down_w), qkv_now=like(saved.qkv_w), qb_now=like(saved.qb),
+        ctx_now=like(saved.ctx), ctxf_now=like(saved.ctxf), out_now=like(saved.out_w), load=copies(10), kvbuf=keep(2, rows, 384), augbuf=keep(2, rows, 128), kvsem=copies(2, 2),
         df=keep(4, tokens, width), df_send=copies(6), df_recv=copies(6),
         da=keep(4, tokens, width), da_send=copies(6), da_recv=copies(6),
         part=keep(4, tokens, width, dtype=F32), **square_sum_items(tokens, width),
@@ -1411,10 +1416,9 @@
         hid=keep(rows, quarter), dgu=keep(rows, 2 * quarter), do=keep(3, rows, 128),
         dqacc=keep(3, rows, 128, dtype=F32), dproj=keep(rows, 768),
         dkv=dict(block_sum_item(nz, rows, 384, parts=2), free=pltpu.SemaphoreType.REGULAR))
-    near = dict(grad=grad, small=saved.small, sum1=saved.sum1, sum2=saved.sum2, ctx=saved.ctx,
-                ctxf=saved.ctxf, qb=saved.qb, out_w=saved.out_w)
+    near = dict(grad=grad, small=saved.small, sum1=saved.sum1, sum2=saved.sum2)
     far = dict(mixed=saved.mixed, yr=saved.yr, xr=saved.xr, gu_w=saved.gu_w, down_w=saved.down_w, kv=saved.kv, kaug=saved.kaug,
-               qkv_w=saved.qkv_w)
+               qkv_w=saved.qkv_w, qb=saved.qb, ctx=saved.ctx, ctxf=saved.ctxf, out_w=saved.out_w)
     return call(functools.partial(bwd_kernel, nz, layers, host), "backward", 1, near=near, far=far, out=out, scratch=scratch)
 
 

time: 387 us -> 386 us (level)
  no operation moved by 1% of the time
where the time goes in v8:
time: 386 us; the launch traced here: 380 us
  Pallas kernels  367 us (95%)
  local copies, waits for them, and re-layouts  11.2 us (3%)
    pallas_call x2, Pallas kernels, call(): pl.pallas_call(kernel, out_shape=tuple(flat[3]) + tuple(flat[4]), in_spec...  367 us
    unnamed x18, local copies, waits for them, and re-layouts  11.2 us

profile of v8, /device:TPU:21, one launch (start us, length us, event | category | flops | bytes accessed | tf_op | source)
XLA Modules:
  0.0 380.0 jit_solution(11028602334743685314)
XLA Ops:
  0.6 0.8 copy.24
  1.4 0.8 copy.25
  2.2 0.1 maximum_bitcast_fusion
  2.3 0.7 fusion.2.refs_5_
  3.0 158.7 %forward.1 = (bf16[128,768]{1,0:T(8,128)(2,1)}, f32[16,768]{1,0:T(8,128)}, bf16[512,192]{1,0:T(8,128)(2,1)}, bf16[512,192]{1,0:T(8,128)(2,1)}, f32[512,192]{1,0:...) custom-call(bf16[2,96,768]{2,1,0:T(8,128)(2,1)} %refs_0_.2, ...), custom_call_target="tpu_custom_call" | custom-call | flops 99999997952 | bytes 200000000 | tf_op jit(solution)/shard_map/forward/pallas_call | solution.py:494
  161.7 0.0 copy-start.2
  161.7 208.2 %backward.1 = (f32[2,6,24]{2,1,0:T(8,128)}, f32[2,96,768]{2,1,0:T(8,128)}, f32[2,2,24]{2,1,0:T(2,128)}, f32[128,768]{1,0:T(8,128)}, f32[2,24,6144]{2,1,0:T(8,128...) custom-call(bf16[128,768]{1,0:T(8,128)(2,1)} %refs_0_.3, f32[16,768]{1,0:T(8,128)} %get-tuple-element.45.refs_1_, ...), custom_call_target="tpu_custom_call" | custom-call | flops 99999997952 | bytes 200000000 | tf_op jit(solution)/shard_map/backward/pallas_call | solution.py:494
  369.9 0.0 copy-start
  369.9 1.4 copy.26
  371.3 0.0 copy-done.2
  371.3 0.0 copy-start.1
  371.3 0.7 copy.34
  372.0 1.8 copy.35
  373.8 0.0 copy-start.3
  373.8 1.8 copy.36
  375.6 1.6 copy.37
  377.1 0.0 copy-done
  377.1 1.0 copy.38
  378.2 0.0 copy-done.1
  378.2 0.8 copy.39
  379.0 0.0 copy-done.3
  379.0 0.6 copy.40
  (1 shorter events, 0.0 us)
Async XLA Ops:
  161.7 209.6 %copy-start.2 = (bf16[128,768]{1,0:T(8,128)(2,1)S(1)}, bf16[128,768]{1,0:T(8,128)(2,1)}, u32[]{:S(2)}) copy-start(bf16[128,768]{1,0:T(8,128)(2,1)} %get-tuple-element.114) | copy-start | bytes 589828
  369.9 7.2 %copy-start = (f32[2,24,6144]{2,1,0:T(8,128)S(1)}, f32[2,24,6144]{2,1,0:T(8,128)}, u32[]{:S(2)}) copy-start(f32[2,24,6144]{2,1,0:T(8,128)} %get-tuple-element.118) | copy-start | bytes 3538948
  371.3 6.9 %copy-start.1 = (f32[2,96,768]{2,1,0:T(8,128)S(1)}, f32[2,96,768]{2,1,0:T(8,128)}, u32[]{:S(2)}) copy-start(f32[2,96,768]{2,1,0:T(8,128)} %get-tuple-element.119) | copy-start | bytes 1769476
  373.8 5.2 %copy-start.3 = (f32[2,2,24]{2,1,0:T(2,128)S(1)}, f32[2,2,24]{2,1,0:T(2,128)}, u32[]{:S(2)}) copy-start(f32[2,2,24]{2,1,0:T(2,128)} %get-tuple-element.120) | copy-start | bytes 1156

commit v9 on v8

--- a/solution.py
+++ b/solution.py
@@ -865,10 +865,10 @@
         R.state[...] = y
         later(3)
         ahead(0)
+        gather_y[l].wait_near()
         if host:
             gu[l].collect()
             down[l].collect()
-        gather_y[l].wait_near()
         if l:
             wait_saved(mixed_saved)
         square_sum.finish()
@@ -906,8 +906,8 @@
         else:
             R.xr_now[l + 1][at.g] = state.astype(BF)
             gather_x[l + 1].start()
+            gather_x[l + 1].wait_near()
             ahead(3)
-            gather_x[l + 1].wait_near()
             gather_x[l + 1].wait_far()
             if host:
                 qkv[l + 1].collect()

time: 386 us -> 388 us (level)
  no operation moved by 1% of the time
where the time goes in v9:
time: 388 us; the launch traced here: 380 us
  Pallas kernels  367 us (95%)
  local copies, waits for them, and re-layouts  11.2 us (3%)
    pallas_call x2, Pallas kernels, call(): pl.pallas_call(kernel, out_shape=tuple(flat[3]) + tuple(flat[4]), in_spec...  367 us
    unnamed x18, local copies, waits for them, and re-layouts  11.2 us

profile of v9, /device:TPU:21, one launch (start us, length us, event | category | flops | bytes accessed | tf_op | source)
XLA Modules:
  0.0 379.9 jit_solution(13586875268092227114)
XLA Ops:
  0.6 0.8 copy.24
  1.4 0.8 copy.25
  2.2 0.1 maximum_bitcast_fusion
  2.3 0.7 fusion.2.refs_5_
  3.0 160.3 %forward.1 = (bf16[128,768]{1,0:T(8,128)(2,1)}, f32[16,768]{1,0:T(8,128)}, bf16[512,192]{1,0:T(8,128)(2,1)}, bf16[512,192]{1,0:T(8,128)(2,1)}, f32[512,192]{1,0:...) custom-call(bf16[2,96,768]{2,1,0:T(8,128)(2,1)} %refs_0_.2, ...), custom_call_target="tpu_custom_call" | custom-call | flops 99999997952 | bytes 200000000 | tf_op jit(solution)/shard_map/forward/pallas_call | solution.py:494
  163.2 0.0 copy-start.2
  163.2 206.5 %backward.1 = (f32[2,6,24]{2,1,0:T(8,128)}, f32[2,96,768]{2,1,0:T(8,128)}, f32[2,2,24]{2,1,0:T(2,128)}, f32[128,768]{1,0:T(8,128)}, f32[2,24,6144]{2,1,0:T(8,128...) custom-call(bf16[128,768]{1,0:T(8,128)(2,1)} %refs_0_.3, f32[16,768]{1,0:T(8,128)} %get-tuple-element.45.refs_1_, ...), custom_call_target="tpu_custom_call" | custom-call | flops 99999997952 | bytes 200000000 | tf_op jit(solution)/shard_map/backward/pallas_call | solution.py:494
  369.8 0.0 copy-start
  369.8 1.4 copy.26
  371.2 0.0 copy-done.2
  371.2 0.0 copy-start.1
  371.2 0.7 copy.34
  371.9 1.8 copy.35
  373.6 0.0 copy-start.3
  373.6 1.8 copy.36
  375.4 1.6 copy.37
  377.0 0.0 copy-done
  377.0 1.0 copy.38
  378.0 0.0 copy-done.1
  378.0 0.8 copy.39
  378.9 0.0 copy-done.3
  378.9 0.6 copy.40
  (1 shorter events, 0.0 us)
Async XLA Ops:
  163.2 208.0 %copy-start.2 = (bf16[128,768]{1,0:T(8,128)(2,1)S(1)}, bf16[128,768]{1,0:T(8,128)(2,1)}, u32[]{:S(2)}) copy-start(bf16[128,768]{1,0:T(8,128)(2,1)} %get-tuple-element.114) | copy-start | bytes 589828
  369.8 7.2 %copy-start = (f32[2,24,6144]{2,1,0:T(8,128)S(1)}, f32[2,24,6144]{2,1,0:T(8,128)}, u32[]{:S(2)}) copy-start(f32[2,24,6144]{2,1,0:T(8,128)} %get-tuple-element.118) | copy-start | bytes 3538948
  371.2 6.9 %copy-start.1 = (f32[2,96,768]{2,1,0:T(8,128)S(1)}, f32[2,96,768]{2,1,0:T(8,128)}, u32[]{:S(2)}) copy-start(f32[2,96,768]{2,1,0:T(8,128)} %get-tuple-element.119) | copy-start | bytes 1769476
  373.6 5.2 %copy-start.3 = (f32[2,2,24]{2,1,0:T(2,128)S(1)}, f32[2,2,24]{2,1,0:T(2,128)}, u32[]{:S(2)}) copy-start(f32[2,2,24]{2,1,0:T(2,128)} %get-tuple-element.120) | copy-start | bytes 1156
